TPU v7x, 256 devices: a whole 4x4x8 slice. The times are simulated.
256 devices in a mesh: sx: 8 (over x, y_lo), sy: 32 (over z, y_hi, core).
Axes of the slice: x: 4, y: 4 (y_hi: 2, y_lo: 2; y = y_hi * 2 + y_lo), z: 8, core: 2. Of those that a mesh axis runs over, the one named last changes fastest.
Arguments:
- volume: bfloat16 [16, 32, 256, 256], P('sx', None, 'sy'), may hold values from -6 to 6
- kernel_one: bfloat16 [32, 32, 3, 3, 3], replicated, may hold values from -0.21875 to 0.21875
- bias_one: bfloat16 [32], replicated, may hold values from -3 to 3
- kernel_two: bfloat16 [64, 32, 3, 3, 3], replicated, may hold values from -0.21875 to 0.21875
- out_grad: bfloat16 [8, 64, 128, 128], P(None, 'sx', 'sy'), may hold values from -12 to 12
Outputs:
- strided_out: bfloat16 [8, 64, 128, 128], P(None, 'sx', 'sy')
- grad_two: float32 [64, 32, 3, 3, 3], P('sx')
- grad_one: float32 [32, 32, 3, 3, 3], replicated
- grad_volume: bfloat16 [16, 32, 256, 256], P('sx', None, 'sy')
All inputs are finite; a program needn't handle non-finite values.
Results may differ from a plain program's by a relative error of at most 0.005.
Values may be sent and summed in bfloat16 or wider, within the bound.
No kernel may reach another device: no remote copies, remote signals or barrier semaphores. Data moves between devices by JAX's collectives and lax.ppermute only.
A program may use at most 128 MiB of HBM per device.

v0:
```python
import jax
import jax.numpy as jnp
from jax import lax
from jax.sharding import PartitionSpec as P

FORWARD_SPEC = ("NDCHW", "OIDHW", "NDCHW")
TURNED_SPEC = ("NDCHW", "IODHW", "NDCHW")
KERNEL_SPEC = ("CDNHW", "IDOHW", "CNDHW")


def with_halo(value, sides, width):
    for axis, dim in sides:
        count, length = (lax.axis_size(axis), value.shape[dim])
        up = [(i, (i + 1) % count) for i in range(count - 1)]
        down = [(j, i) for i, j in up]
        last = lax.slice_in_dim(value, length - width, length, axis=dim)
        first = lax.slice_in_dim(value, 0, width, axis=dim)
        before = lax.ppermute(last, axis, up)
        after = lax.ppermute(first, axis, down)
        value = jnp.concatenate([before, value, after], axis=dim)
    return value


def from_behind(block, axis, distance):
    devices = range(lax.axis_size(axis))
    route = [(i - distance, i) for i in devices if i - distance in devices]
    return lax.ppermute(block, axis, route)


def forward_conv(inputs, weights, strides, pads):
    return lax.conv_general_dilated(
        inputs[None],
        weights,
        strides,
        pads,
        dimension_numbers=FORWARD_SPEC,
        preferred_element_type=jnp.float32,
    )[0]


def input_conv(grads, weights, dilation, pads):
    turned = weights[:, :, ::-1, ::-1, ::-1]
    return lax.conv_general_dilated(
        grads[None],
        turned,
        (1, 1, 1),
        pads,
        lhs_dilation=dilation,
        dimension_numbers=TURNED_SPEC,
        preferred_element_type=jnp.float32,
    )[0]


def kernel_conv(inputs, grads, dilation, pads):
    return lax.conv_general_dilated(
        inputs[None],
        grads[None],
        (1, 1, 1),
        pads,
        rhs_dilation=dilation,
        dimension_numbers=KERNEL_SPEC,
        preferred_element_type=jnp.float32,
    )


def per_device(volume, kernel_one, bias_one, kernel_two, out_grad):
    depth, chans, rows, width = volume.shape
    kinds = kernel_two.shape[0]
    across = lax.axis_size("sx")
    down = lax.axis_size("sy")
    share = kinds // across
    half_depth = depth * across // 2
    out_scale = (half_depth * (rows * down // 2) * (width // 2)) ** (-0.5)
    in_scale = (depth * across * rows * down * width) ** (-0.5)
    padded_volume = with_halo(volume, (("sx", 0), ("sy", 2)), 1)
    pre = forward_conv(padded_volume, kernel_one, (1, 1, 1), ((0, 0), (0, 0), (1, 1)))
    pre = pre + bias_one.astype(jnp.float32)[None, :, None, None]
    act = jax.nn.silu(pre).astype(jnp.bfloat16)
    below = from_behind(act[:, :, rows - 1 :, :], "sy", 1)
    extended = jnp.concatenate([below, act], axis=2)
    plane = from_behind(extended[depth - 1 :], "sx", 1)
    full = jnp.concatenate([plane, extended], axis=0)
    local_out = forward_conv(full, kernel_two, (2, 2, 2), ((0, 0), (0, 0), (1, 0))).astype(
        jnp.bfloat16
    )
    strided_out = lax.all_to_all(local_out, "sx", split_axis=1, concat_axis=0, tiled=True)
    local_grad = lax.all_to_all(out_grad, "sx", split_axis=0, concat_axis=1, tiled=True)
    kernel_part = kernel_conv(full, local_grad, (2, 2, 2), ((0, 0), (0, 0), (1, 0)))
    spread = input_conv(local_grad, kernel_two, (2, 2, 2), ((2, 2), (2, 2), (1, 2)))
    upper = from_behind(spread[0:1], "sx", -1)
    grad_ext = jnp.concatenate([spread[1:depth], spread[depth:] + upper], axis=0)
    lower = from_behind(grad_ext[:, :, 0:1], "sy", -1)
    grad_act = jnp.concatenate([grad_ext[:, :, 1:rows], grad_ext[:, :, rows:] + lower], axis=2)
    sigma = jax.nn.sigmoid(pre)
    grad_pre = (grad_act * sigma * (1.0 + pre * (1.0 - sigma))).astype(jnp.bfloat16)
    padded_grad_pre = with_halo(grad_pre, (("sx", 0), ("sy", 2)), 1)
    grad_volume = input_conv(
        padded_grad_pre, kernel_one, (1, 1, 1), ((0, 0), (0, 0), (1, 1))
    ).astype(jnp.bfloat16)
    kernel_one_part = kernel_conv(padded_volume, grad_pre, (1, 1, 1), ((0, 0), (0, 0), (1, 1)))
    summed = lax.psum((kernel_one_part, kernel_part), ("sx", "sy"))
    grad_one = summed[0] * in_scale
    grad_two = (
        lax.dynamic_slice_in_dim(summed[1], lax.axis_index("sx") * share, share, 0) * out_scale
    )
    return (strided_out, grad_two, grad_one, grad_volume)


def solution(mesh):
    return jax.shard_map(
        per_device,
        mesh=mesh,
        in_specs=(P("sx", None, "sy", None), P(), P(), P(), P(None, "sx", "sy", None)),
        out_specs=(
            P(None, "sx", "sy", None),
            P("sx", None, None, None, None),
            P(),
            P("sx", None, "sy", None),
        ),
        check_vma=False,
    )
```

profile of v0, /device:TPU:16, one launch (start us, length us, event | category | flops | bytes accessed | tf_op | source)
XLA Modules:
  0.0 471.2 jit_solution(3050227807896589002)
XLA Ops:
  7.2 1.5 copy.168
  8.7 5.0 %all-to-all-start.1 = ((bf16[8,8,4,128]{3,1,2,0:T(8,128)(2,1)}), bf16[8,8,4,128]{3,1,2,0:T(8,128)(2,1)S(1)}, u32[]{:S(2)}, u32[]{:S(2)}) async-start(bf16[8,8,4,128]{3,1,2,0:T(8,128)(2,1)} %copy.168), calls=%async_computation.1 | async-start | bytes 131072 | tf_op jit(solution)/shard_map/all_to_all | solution.py:87
  13.8 1.0 fusion.67
  15.4 4.6 collective-permute-start
  20.0 1.3 collective-permute-start.1
  22.3 2.3 convolution_select_fusion
  24.6 1.3 fusion.64
  25.9 2.9 copy.176
  28.8 2.4 reshape.55
  31.2 1.6 copy.180
  32.8 1.6 reshape.59
  34.5 1.0 slice_bitcast_fusion.5
  35.5 0.9 constant_dynamic-update-slice_fusion.2
  36.5 0.9 constant_dynamic-update-slice_fusion
  38.1 1.9 collective-permute-start.2
  40.0 5.1 %collective-permute-start.3 = (bf16[4,32,1,256]{3,1,2,0:T(8,128)(2,1)}, bf16[4,32,1,256]{3,1,2,0:T(8,128)(2,1)S(1)}, u32[]{:S(2)}, u32[]{:S(2)}) collective-permute-start(bf16[4,32,1,256]{3,1,2,0:T(8,128)(2,1)} %get-tuple-element.43), channel_id=1, source_target_pairs={{1,0},{2,1},{3,2},{4,3},{5,4},{6,5},{7,6},{8,7},{9,8},{10,9},{11,1... | collective-permute-start | bytes 196616 | tf_op jit(solution)/shard_map/ppermute | solution.py:19
  45.9 0.9 copy.171
  46.8 1.3 collective-permute-start.6
  48.8 1.1 reshape.57
  49.9 2.0 fusion.40
  51.9 1.4 pad
  53.3 3.9 reshape.37
  57.2 3.9 copy.160
  61.1 1.0 slice.95
  62.1 5.0 %fusion.5 = f32[2,8,8,33,32]{4,2,3,1,0:T(8,128)S(1)} fusion(bf16[32,32,3,3,3]{1,0,4,3,2:T(8,128)(2,1)S(1)} %copy-done, bf16[4,32,10,1,7,2]{1,4,5,2,0,3:T(8,128)(2,1)S(1)} %slice.95, bf16[4,32,10,1,8,33]{1,4,5,2,0,3:T(8,128)(2,1)} %copy.160), kind=kOutput, calls=%fused_computation.7 | convolution fusion | flops 235720704 | bytes 1307648 | tf_op jit(solution)/shard_map/conv_general_dilated | solution.py:31
  67.1 2.2 copy.161
  69.3 3.9 add_divide_fusion
  73.2 3.0 copy.183
  76.2 2.8 reshape.68
  78.9 4.6 copy.184
  83.5 2.8 reshape.70
  86.3 3.0 copy.162
  89.3 2.2 reshape.41
  91.5 8.0 %copy.185 = bf16[1,4,32,10,256]{2,0,4,3,1:T(2,128)(2,1)} copy(bf16[1,4,32,10,256]{4,2,3,1,0:T(8,128)(2,1)S(1)} %copy-done.3) | data formatting | bytes 1310720 | tf_op jit(solution)/shard_map/broadcast_in_dim | solution.py:32
  99.6 2.7 collective-permute-start.7
  102.4 1.8 collective-permute-done.7
  104.6 6.2 %collective-permute-start.4 = (bf16[2,32,1,256]{3,1,2,0:T(8,128)(2,1)S(1)}, bf16[2,32,1,256]{3,1,2,0:T(8,128)(2,1)S(1)}, u32[]{:S(2)}, u32[]{:S(2)}) collective-permute-start(bf16[2,32,1,256]{3,1,2,0:T(8,128)(2,1)S(1)} %slice.97), channel_id=1, source_target_pairs={{0,1},{1,2},{2,3},{3,4},{4,5},{5,6},{6,7},{7,8},{8,9},{9,10},{10,1... | collective-permute-start | bytes 98312 | tf_op jit(solution)/shard_map/ppermute | solution.py:27
  111.7 3.7 copy.186
  115.4 5.5 %collective-permute-start.8 = (bf16[1,32,8,256]{3,1,2,0:T(8,128)(2,1)}, bf16[1,32,8,256]{3,1,2,0:T(8,128)(2,1)}, u32[]{:S(2)}, u32[]{:S(2)}) collective-permute-start(bf16[1,32,8,256]{3,1,2,0:T(8,128)(2,1)} %get-tuple-element.46), channel_id=1, source_target_pairs={{0,32},{32,64},{64,96},{96,128},{128,160},{160,192},{192,224},{1,3... | collective-permute-start | bytes 393224 | tf_op jit(solution)/shard_map/ppermute | solution.py:18
  121.0 1.3 collective-permute-start.9
  123.0 5.2 %collective-permute-start.5 = (bf16[1,32,9,256]{3,1,2,0:T(8,128)(2,1)}, bf16[1,32,9,256]{3,1,2,0:T(8,128)(2,1)}, u32[]{:S(2)}, u32[]{:S(2)}) collective-permute-start(bf16[1,32,9,256]{3,1,2,0:T(8,128)(2,1)} %pad_maximum_fusion.1), channel_id=1, source_target_pairs={{0,32},{32,64},{64,96},{96,128},{128,160},{160,192},{192,224},{1,3... | collective-permute-start | bytes 442376 | tf_op jit(solution)/shard_map/ppermute | solution.py:27
  128.2 32.0 %fusion.69 = f32[32,32,3,3,3]{0,1,4,3,2:T(8,128)} fusion(bf16[1,4,32,10,256]{2,0,4,3,1:T(2,128)(2,1)} %copy.185, bf16[1,2,32,8,256]{2,0,4,3,1:T(2,128)(2,1)} %copy.186), kind=kOutput, calls=%fused_computation.99 | convolution fusion | flops 225902592 | bytes 1028096 | tf_op jit(solution)/shard_map/conv_general_dilated | solution.py:55
  160.2 1.4 pad_maximum_fusion.4
  161.6 1.9 collective-permute-start.10
  163.5 5.1 %collective-permute-start.11 = (bf16[4,32,1,256]{3,1,2,0:T(8,128)(2,1)S(1)}, bf16[4,32,1,256]{3,1,2,0:T(8,128)(2,1)S(1)}, u32[]{:S(2)}, u32[]{:S(2)}) collective-permute-start(bf16[4,32,1,256]{3,1,2,0:T(8,128)(2,1)S(1)} %get-tuple-element.41), channel_id=1, source_target_pairs={{1,0},{2,1},{3,2},{4,3},{5,4},{6,5},{7,6},{8,7},{9,8},{10,9},{11,1... | collective-permute-start | bytes 196616 | tf_op jit(solution)/shard_map/ppermute | solution.py:19
  168.7 1.0 fusion.42
  170.0 1.5 reshape.44
  171.5 3.0 copy.164
  174.5 0.9 slice.98
  175.5 2.6 fusion.26
  178.9 4.3 all-to-all-start
  183.3 6.4 %copy.170 = bf16[1,3,32,9,256]{2,0,4,3,1:T(2,128)(2,1)} copy(bf16[1,3,32,9,256]{4,2,3,1,0:T(8,128)(2,1)S(1)} %get-tuple-element.44) | data formatting | bytes 884736 | tf_op jit(solution)/shard_map/broadcast_in_dim | solution.py:32
  189.7 9.2 %fusion.68 = f32[64,32,3,3,3]{1,0,4,3,2:T(8,128)} fusion(bf16[1,3,32,9,256]{2,0,4,3,1:T(2,128)(2,1)} %copy.170, bf16[1,1,64,4,128]{2,0,4,3,1:T(2,128)(2,1)S(1)} %copy-done.11), kind=kOutput, calls=%fused_computation.98 | convolution fusion | flops 56475648 | bytes 729088 | tf_op jit(solution)/shard_map/conv_general_dilated | solution.py:55
  198.9 1.1 maximum_bitcast_fusion
  200.0 1.4 pad.6
  201.4 3.7 reshape.62
  205.1 3.9 copy.188
  209.0 1.0 slice.115
  210.0 4.8 %fusion.9 = bf16[2,8,8,33,32]{4,2,3,1,0:T(8,128)(2,1)S(1)} fusion(bf16[32,32,3,3,3]{1,0,4,3,2:T(8,128)(2,1)S(1)} %copy-done, bf16[4,32,10,1,7,2]{1,4,5,2,0,3:T(8,128)(2,1)S(1)} %slice.115, bf16[4,32,10,1,8,33]{1,4,5,2,0,3:T(8,128)(2,1)} %copy.188), kind=kOutput, calls=%fused_computation.10 | convolution fusion | flops 235720704 | bytes 1037312 | tf_op jit(solution)/shard_map/conv_general_dilated | solution.py:43
  214.8 1.1 copy.189
  218.3 241.8 %all-reduce.3.cloned.1.call-done = (f32[64,32,3,3,3]{1,0,4,3,2:T(8,128)}, f32[32,32,3,3,3]{0,1,4,3,2:T(8,128)}) async-done(((f32[64,32,3,3,3]{1,0,4,3,2:T(8,128)}, f32[32,32,3,3,3]{0,1,4,3,2:T(8,128)}), (f32[64,32,3,3,3]{1,0,4,3,2:T(8,128)}, f32[32,32,3,3,3]{0,1,4,3,2:T(8,128)})) %all-reduce.3.cloned.1.call-update) | async-done | bytes 331792 | tf_op jit(solution)/shard_map/psum | solution.py:101
  460.0 1.0 broadcast_multiply_fusion
  461.1 0.9 copy.192
  462.0 1.6 dynamic-slice_multiply_fusion
  (85 shorter events, 10.0 us)
Async XLA Ops:
  7.2 54.9 %copy-start = (bf16[32,32,3,3,3]{1,0,4,3,2:T(8,128)(2,1)S(1)}, bf16[32,32,3,3,3]{1,0,4,3,2:T(8,128)(2,1)}, u32[]{:S(2)}) copy-start(bf16[32,32,3,3,3]{1,0,4,3,2:T(8,128)(2,1)} %param.6) | copy-start | bytes 165892
  7.2 15.1 %copy-start.15 = (pred[8,34]{0,1:T(8,128)(4,1)S(1)}, pred[8,34]{0,1:T(8,128)(4,1)}, u32[]{:S(2)}) copy-start(pred[8,34]{0,1:T(8,128)(4,1)} %constant.40) | copy-start | bytes 820
  7.2 15.1 %copy-start.12 = (bf16[64,32,3,3,3]{0,1,4,3,2:T(8,128)(2,1)S(1)}, bf16[64,32,3,3,3]{0,1,4,3,2:T(8,128)(2,1)}, u32[]{:S(2)}) copy-start(bf16[64,32,3,3,3]{0,1,4,3,2:T(8,128)(2,1)} %param.8) | copy-start | bytes 331780
  8.7 13.2 %all-to-all-start.1 = ((bf16[8,8,4,128]{3,1,2,0:T(8,128)(2,1)}), bf16[8,8,4,128]{3,1,2,0:T(8,128)(2,1)S(1)}, u32[]{:S(2)}, u32[]{:S(2)}) async-start(bf16[8,8,4,128]{3,1,2,0:T(8,128)(2,1)} %copy.168), calls=%async_computation.1 | async-start | bytes 131072 | tf_op jit(solution)/shard_map/all_to_all | solution.py:87
  15.4 20.0 %collective-permute-start = (bf16[1,32,8,256]{3,1,2,0:T(8,128)(2,1)}, bf16[1,32,8,256]{3,1,2,0:T(8,128)(2,1)}, u32[]{:S(2)}, u32[]{:S(2)}) collective-permute-start(bf16[1,32,8,256]{3,1,2,0:T(8,128)(2,1)} %copy.199), channel_id=1, source_target_pairs={{0,32},{32,64},{64,96},{96,128},{128,160},{160,192},{192,224},{1,3... | collective-permute-start | bytes 393224 | tf_op jit(solution)/shard_map/ppermute | solution.py:18
  20.0 16.4 %collective-permute-start.1 = (bf16[1,32,8,256]{3,1,2,0:T(8,128)(2,1)S(1)}, bf16[1,32,8,256]{3,1,2,0:T(8,128)(2,1)}, u32[]{:S(2)}, u32[]{:S(2)}) collective-permute-start(bf16[1,32,8,256]{3,1,2,0:T(8,128)(2,1)S(1)} %copy.200), channel_id=1, source_target_pairs={{32,0},{64,32},{96,64},{128,96},{160,128},{192,160},{224,192},{33,... | collective-permute-start | bytes 393224 | tf_op jit(solution)/shard_map/ppermute | solution.py:19
  31.2 5.2 %copy-start.10 = (bf16[2,32,8,256]{3,2,1,0:T(8,128)(2,1)S(1)}, bf16[2,32,8,256]{3,2,1,0:T(8,128)(2,1)}, u32[]{:S(2)}) copy-start(bf16[2,32,8,256]{3,2,1,0:T(8,128)(2,1)} %param.5) | copy-start | bytes 786436
  37.4 10.7 %copy-start.9 = (bf16[4,32,8,256]{3,1,2,0:T(8,128)(2,1)}, bf16[4,32,8,256]{3,1,2,0:T(8,128)(2,1)S(1)}, u32[]{:S(2)}) copy-start(bf16[4,32,8,256]{3,1,2,0:T(8,128)(2,1)S(1)} %constant_dynamic-update-slice_fusion) | copy-start | bytes 1572868
  38.1 11.8 %collective-permute-start.2 = (bf16[4,32,1,256]{3,1,2,0:T(8,128)(2,1)}, bf16[4,32,1,256]{3,1,2,0:T(8,128)(2,1)S(1)}, u32[]{:S(2)}, u32[]{:S(2)}) collective-permute-start(bf16[4,32,1,256]{3,1,2,0:T(8,128)(2,1)} %get-tuple-element.42), channel_id=1, source_target_pairs={{0,1},{1,2},{2,3},{3,4},{4,5},{5,6},{6,7},{7,8},{8,9},{9,10},{10,1... | collective-permute-start | bytes 196616 | tf_op jit(solution)/shard_map/ppermute | solution.py:18
  40.0 9.9 %collective-permute-start.3 = (bf16[4,32,1,256]{3,1,2,0:T(8,128)(2,1)}, bf16[4,32,1,256]{3,1,2,0:T(8,128)(2,1)S(1)}, u32[]{:S(2)}, u32[]{:S(2)}) collective-permute-start(bf16[4,32,1,256]{3,1,2,0:T(8,128)(2,1)} %get-tuple-element.43), channel_id=1, source_target_pairs={{1,0},{2,1},{3,2},{4,3},{5,4},{6,5},{7,6},{8,7},{9,8},{10,9},{11,1... | collective-permute-start | bytes 196616 | tf_op jit(solution)/shard_map/ppermute | solution.py:19
  46.8 52.7 %collective-permute-start.6 = (f32[1,32,9,256]{3,1,2,0:T(8,128)}, f32[1,32,9,256]{3,1,2,0:T(8,128)S(1)}, u32[]{:S(2)}, u32[]{:S(2)}) collective-permute-start(f32[1,32,9,256]{3,1,2,0:T(8,128)} %slice_bitcast_fusion.3), channel_id=1, source_target_pairs={{32,0},{64,32},{96,64},{128,96},{160,128},{192,160},{224,192},{33,... | collective-permute-start | bytes 884744 | tf_op jit(solution)/shard_map/ppermute | solution.py:27
  67.1 2.2 copy-start.16
  89.3 2.2 copy-start.3
  91.5 8.1 %copy-start.8 = (f32[1,9,1,272,32]{3,4,1,2,0:T(8,128)S(1)}, f32[1,9,1,272,32]{3,4,1,2,0:T(8,128)}, u32[]{:S(2)}) copy-start(f32[1,9,1,272,32]{3,4,1,2,0:T(8,128)} %reshape.57) | copy-start | bytes 940036
  99.6 11.3 %copy-start.6 = (f32[2,8,1,264,32]{3,4,1,0,2:T(8,128)S(1)}, f32[2,8,1,264,32]{3,4,1,0,2:T(8,128)}, u32[]{:S(2)}) copy-start(f32[2,8,1,264,32]{3,4,1,0,2:T(8,128)} %reshape.68) | copy-start | bytes 1622020
  99.6 11.3 %copy-start.7 = (f32[2,8,1,264,32]{3,4,1,0,2:T(8,128)S(1)}, f32[2,8,1,264,32]{3,4,1,0,2:T(8,128)}, u32[]{:S(2)}) copy-start(f32[2,8,1,264,32]{3,4,1,0,2:T(8,128)} %reshape.70) | copy-start | bytes 1622020
  99.6 4.6 collective-permute-start.7
  104.6 6.4 %copy-start.1 = (bf16[2,32,8,256]{3,1,2,0:T(8,128)(2,1)}, bf16[2,32,8,256]{3,1,2,0:T(8,128)(2,1)S(1)}, u32[]{:S(2)}) copy-start(bf16[2,32,8,256]{3,1,2,0:T(8,128)(2,1)S(1)} %get-tuple-element.36) | copy-start | bytes 786436
  104.6 17.7 %copy-start.4 = (bf16[2,32,8,256]{3,1,2,0:T(8,128)(2,1)}, bf16[2,32,8,256]{3,1,2,0:T(8,128)(2,1)S(1)}, u32[]{:S(2)}) copy-start(bf16[2,32,8,256]{3,1,2,0:T(8,128)(2,1)S(1)} %get-tuple-element.37) | copy-start | bytes 786436
  104.6 17.6 %collective-permute-start.4 = (bf16[2,32,1,256]{3,1,2,0:T(8,128)(2,1)S(1)}, bf16[2,32,1,256]{3,1,2,0:T(8,128)(2,1)S(1)}, u32[]{:S(2)}, u32[]{:S(2)}) collective-permute-start(bf16[2,32,1,256]{3,1,2,0:T(8,128)(2,1)S(1)} %slice.97), channel_id=1, source_target_pairs={{0,1},{1,2},{2,3},{3,4},{4,5},{5,6},{6,7},{7,8},{8,9},{9,10},{10,1... | collective-permute-start | bytes 98312 | tf_op jit(solution)/shard_map/ppermute | solution.py:27
  115.4 44.7 %collective-permute-start.8 = (bf16[1,32,8,256]{3,1,2,0:T(8,128)(2,1)}, bf16[1,32,8,256]{3,1,2,0:T(8,128)(2,1)}, u32[]{:S(2)}, u32[]{:S(2)}) collective-permute-start(bf16[1,32,8,256]{3,1,2,0:T(8,128)(2,1)} %get-tuple-element.46), channel_id=1, source_target_pairs={{0,32},{32,64},{64,96},{96,128},{128,160},{160,192},{192,224},{1,3... | collective-permute-start | bytes 393224 | tf_op jit(solution)/shard_map/ppermute | solution.py:18
  121.0 39.2 %collective-permute-start.9 = (bf16[1,32,8,256]{3,1,2,0:T(8,128)(2,1)}, bf16[1,32,8,256]{3,1,2,0:T(8,128)(2,1)}, u32[]{:S(2)}, u32[]{:S(2)}) collective-permute-start(bf16[1,32,8,256]{3,1,2,0:T(8,128)(2,1)} %get-tuple-element.47), channel_id=1, source_target_pairs={{32,0},{64,32},{96,64},{128,96},{160,128},{192,160},{224,192},{33,... | collective-permute-start | bytes 393224 | tf_op jit(solution)/shard_map/ppermute | solution.py:19
  122.3 37.9 %copy-start.14 = (bf16[2,32,1,256]{3,1,2,0:T(8,128)(2,1)}, bf16[2,32,1,256]{3,1,2,0:T(8,128)(2,1)S(1)}, u32[]{:S(2)}) copy-start(bf16[2,32,1,256]{3,1,2,0:T(8,128)(2,1)S(1)} %collective-permute-done.4) | copy-start | bytes 98308
  123.0 45.7 %collective-permute-start.5 = (bf16[1,32,9,256]{3,1,2,0:T(8,128)(2,1)}, bf16[1,32,9,256]{3,1,2,0:T(8,128)(2,1)}, u32[]{:S(2)}, u32[]{:S(2)}) collective-permute-start(bf16[1,32,9,256]{3,1,2,0:T(8,128)(2,1)} %pad_maximum_fusion.1), channel_id=1, source_target_pairs={{0,32},{32,64},{64,96},{96,128},{128,160},{160,192},{192,224},{1,3... | collective-permute-start | bytes 442376 | tf_op jit(solution)/shard_map/ppermute | solution.py:27
  128.2 32.0 %copy-start.2 = (bf16[2,32,8,256]{3,1,2,0:T(8,128)(2,1)S(1)}, bf16[2,32,8,256]{3,1,2,0:T(8,128)(2,1)}, u32[]{:S(2)}) copy-start(bf16[2,32,8,256]{3,1,2,0:T(8,128)(2,1)} %copy-done.1) | copy-start | bytes 786436
  128.2 40.5 %copy-start.5 = (bf16[2,32,8,256]{3,1,2,0:T(8,128)(2,1)S(1)}, bf16[2,32,8,256]{3,1,2,0:T(8,128)(2,1)}, u32[]{:S(2)}) copy-start(bf16[2,32,8,256]{3,1,2,0:T(8,128)(2,1)} %copy-done.4) | copy-start | bytes 786436
  161.6 37.3 %collective-permute-start.10 = (bf16[4,32,1,256]{3,1,2,0:T(8,128)(2,1)}, bf16[4,32,1,256]{3,1,2,0:T(8,128)(2,1)S(1)}, u32[]{:S(2)}, u32[]{:S(2)}) collective-permute-start(bf16[4,32,1,256]{3,1,2,0:T(8,128)(2,1)} %get-tuple-element.40), channel_id=1, source_target_pairs={{0,1},{1,2},{2,3},{3,4},{4,5},{5,6},{6,7},{7,8},{8,9},{9,10},{10,1... | collective-permute-start | bytes 196616 | tf_op jit(solution)/shard_map/ppermute | solution.py:18
  163.5 35.4 %collective-permute-start.11 = (bf16[4,32,1,256]{3,1,2,0:T(8,128)(2,1)S(1)}, bf16[4,32,1,256]{3,1,2,0:T(8,128)(2,1)S(1)}, u32[]{:S(2)}, u32[]{:S(2)}) collective-permute-start(bf16[4,32,1,256]{3,1,2,0:T(8,128)(2,1)S(1)} %get-tuple-element.41), channel_id=1, source_target_pairs={{1,0},{2,1},{3,2},{4,3},{5,4},{6,5},{7,6},{8,7},{9,8},{10,9},{11,1... | collective-permute-start | bytes 196616 | tf_op jit(solution)/shard_map/ppermute | solution.py:19
  171.5 4.0 copy-start.13
  171.5 4.0 copy-start.18
  178.2 11.5 %copy-start.11 = (bf16[1,1,64,4,128]{2,0,4,3,1:T(2,128)(2,1)S(1)}, bf16[1,1,64,4,128]{2,0,4,3,1:T(2,128)(2,1)}, u32[]{:S(2)}) copy-start(bf16[1,1,64,4,128]{2,0,4,3,1:T(2,128)(2,1)} %copy.171) | copy-start | bytes 196612
  178.9 39.3 %all-to-all-start = ((bf16[1,64,4,128]{3,2,0,1:T(4,128)(2,1)}), bf16[1,64,4,128]{3,2,0,1:T(4,128)(2,1)S(1)}, u32[]{:S(2)}, u32[]{:S(2)}) async-start(bf16[1,64,4,128]{3,2,0,1:T(4,128)(2,1)} %copy.166), calls=%async_computation | async-start | bytes 131072 | tf_op jit(solution)/shard_map/all_to_all | solution.py:86
  183.2 276.8 %all-reduce.3.cloned.1.call-start = ((), (), s32[]{:S(2)}) async-start(), calls=%async_computation.2 | async-start | bytes 2654208 | tf_op jit(solution)/shard_map/psum | solution.py:101
  210.0 5.9 %copy-start.17 = (pred[8,33]{1,0:T(8,128)(4,1)S(1)}, pred[8,33]{1,0:T(8,128)(4,1)}, u32[]{:S(2)}) copy-start(pred[8,33]{1,0:T(8,128)(4,1)} %constant.39) | copy-start | bytes 796
Sparse Core Ops, SparseCore 0:
  199.0 260.9 all-reduce.2
where the time goes:
time: 479 us; the launch traced here: 471 us
  waiting for transfers between devices  244 us (51%)
  local copies, waits for them, and re-layouts  91.1 us (19%)
  matrix products  55.9 us (12%)
  starting transfers between devices  51.5 us (11%)
  between operations  14.9 us (3%)
  other arithmetic  14.1 us (3%)
    psum x1, waiting for transfers between devices, per_device(): summed = lax.psum((kernel_one_part, kernel_part), ('sx', 'sy'))  242 us
    conv_general_dilated x2, matrix products, kernel_conv(): lax.conv_general_dilated(inputs[None], grads[None], (1, 1, 1), pads, rhs_...  41.2 us
    conv_general_dilated x9, local copies, waits for them, and re-layouts, forward_conv(): lax.conv_general_dilated(inputs[None], weights, strides, pads, dimension_...  21.5 us
    conv_general_dilated x13, local copies, waits for them, and re-layouts, input_conv(): lax.conv_general_dilated(grads[None], turned, (1, 1, 1), pads, lhs_dilati...  21.3 us
    broadcast_in_dim x4, local copies, waits for them, and re-layouts, forward_conv(): inputs[None]  16.2 us
    ppermute x4, starting transfers between devices, from_behind(): return lax.ppermute(block, axis, route)  15.4 us
    ppermute x4, starting transfers between devices, with_halo(): before = lax.ppermute(last, axis, up)  13.9 us
    ppermute x4, starting transfers between devices, with_halo(): after = lax.ppermute(first, axis, down)  12.9 us
  transfers between devices with their start and end apart: 15, of which 2 were waited for; matrix products, arithmetic and copies ran while one was open for 33% of the time, Pallas kernels for 0%

commit v1 on v0

v1 whole, which is shorter than its diff:
```python
import functools

import jax
import jax.numpy as jnp
import numpy as np
from jax import lax
from jax.experimental import pallas as pl
from jax.experimental.pallas import tpu as pltpu
from jax.sharding import PartitionSpec as P

F32 = jnp.float32
BF16 = jnp.bfloat16
NX = 8
NY = 32
C = 32
K = 64
W = 256
CLASSES = ((0, 0), (0, 1), (1, 0), (1, 1))
TAPS = tuple((a, c) for a in range(3) for c in range(3))
VMEM = 48 * 1024 * 1024


def row_order(outer, middle, inner):
    n = outer * middle * inner
    m = np.zeros((n, n), np.float32)
    for o in range(outer):
        for a in range(middle):
            for b in range(inner):
                m[(o * inner + b) * middle + a, (o * middle + a) * inner + b] = 1
    return m


def spread_columns():
    m = np.zeros((640, NX * 128), np.float32)
    for j in range(NX):
        for u in range(18):
            for pd, pw in CLASSES:
                w = 32 * j - 2 + 2 * u + pw
                if 0 <= w < W:
                    m[pd * W + w, j * 128 + (pd * 2 + pw) * 20 + u] = 1
            g = 16 * j - 1 + u
            if 0 <= g < 128:
                m[512 + g, j * 128 + 80 + u] = 1
    return m


def class_columns():
    m = np.zeros((512, 512), np.float32)
    for s in range(4):
        for cls in range(4):
            for u in range(18):
                m[s * 128 + cls * 20 + u, cls * 128 + s * 32 + u] = 1
    return m


def cotangent_columns():
    m = np.zeros((1024, 256), np.float32)
    for e in range(8):
        for u in range(18):
            m[e * 128 + 80 + u, e * 32 + u] = 1
    return m


def strided_columns():
    m = np.zeros((256, 128), np.float32)
    for e in range(8):
        for u in range(16):
            m[e * 32 + 1 + u, e * 16 + u] = 1
    return m


def gather_columns():
    m = np.zeros((1024, 512), np.float32)
    for half in range(2):
        for cls in range(4):
            for e in range(4):
                for u in range(16):
                    m[half * 512 + cls * 128 + e * 32 + 1 + u, e * 128 + half * 64 + cls * 16 + u] = 1
    return m


def plane_columns():
    m = np.zeros((512, 512), np.float32)
    for j in range(4):
        for half in range(2):
            for pd, pw in CLASSES:
                for u in range(16):
                    row = j * 128 + half * 64 + (pd * 2 + pw) * 16 + u
                    m[row, (pd * 2 + half) * 128 + 32 * j + 2 * u + pw] = 1
    return m


def strided_planes():
    m = np.zeros((1024, 1024), np.float32)
    for j in range(8):
        for e in range(8):
            for u in range(16):
                m[j * 128 + e * 16 + u, e * 128 + j * 16 + u] = 1
    return m


def kernel_rows():
    m = np.zeros((320, 288), np.float32)
    for s in range(8):
        for t in range(9):
            for o in range(4):
                m[s * 40 + t * 4 + o, t * 32 + 4 * s + o] = 1
    return m


def const(m):
    return jnp.asarray(m, BF16)


def dot(a, b):
    return jnp.dot(a, b, preferred_element_type=F32)


def move(a, b):
    return dot(a, b).astype(BF16)


def dot_nt(a, b):
    return lax.dot_general(a, b, (((1,), (1,)), ((), ())), preferred_element_type=F32)


def ahead(x, n):
    return jnp.concatenate([x[:, n:], jnp.zeros((x.shape[0], n), x.dtype)], axis=1)


def behind(x, n):
    return jnp.concatenate([jnp.zeros((x.shape[0], n), x.dtype), x[:, :-n]], axis=1)


def step(parity, offset):
    at = parity + offset
    return (1, 1) if at == -1 else (0, 1) if at == 2 else (at, 0)


def variant(pd, pw, da, dc):
    qd, sd = step(pd, da)
    qw, sw = step(pw, dc)
    return ((qd * 2 + qw) * 2 + sd) * 2 + sw


def store_variants(ref, x, cls):
    pd, pw = cls
    base = (pd * 2 + pw) * 4
    move_d = behind if pd else ahead
    move_w = behind if pw else ahead
    along = move_w(x, 1)
    ref[base] = x
    ref[base + 1] = along
    ref[base + 2] = move_d(x, 32)
    ref[base + 3] = move_d(along, 32)


def pack_kernel(vol_ref, og_ref, rows_ref, og_rows_ref, cols_ref, out_ref):
    rows = rows_ref[...]
    v0 = move(rows, vol_ref[0:256])
    v1 = move(rows, vol_ref[256:512])
    og = move(og_rows_ref[...], og_ref[...])
    cat = jnp.concatenate([v0, v1, og], axis=1)
    for j in range(NX):
        out_ref[j] = move(cat, cols_ref[:, j * 128 : (j + 1) * 128])


def unpack_kernel(r_ref, cls_ref, og_cols_ref, x_ref, og_ref, up_ref, down_ref):
    for q in range(2):
        cat = jnp.concatenate([r_ref[4 * q + s] for s in range(4)], axis=1)
        got = move(cat, cls_ref[...])
        for cls in range(4):
            at = slice(cls * 256 + q * 128, cls * 256 + (q + 1) * 128)
            part = got[:, cls * 128 : (cls + 1) * 128]
            x_ref[:, at] = part
            up_ref[:, at] = part[192:256]
            down_ref[:, at] = part[0:64]
    parts = []
    for s in range(NX):
        parts.append(jnp.concatenate([r_ref[s, e * 32 : (e + 1) * 32, :] for e in range(8)], axis=1))
    og = dot(jnp.concatenate(parts, axis=0), og_cols_ref[...])
    og = jnp.concatenate(
        [og[s * 32 + g * 8 : s * 32 + g * 8 + 8] for g in range(4) for s in range(NX)], axis=0
    ).astype(BF16)
    og_ref[...] = og
    up_ref[:, 1024:1280] = og[192:256]
    down_ref[:, 1024:1280] = og[0:64]


def place(strip, offset, width):
    parts = [strip]
    if offset:
        parts.insert(0, jnp.zeros((strip.shape[0], offset), strip.dtype))
    rest = width - offset - strip.shape[1]
    if rest:
        parts.append(jnp.zeros((strip.shape[0], rest), strip.dtype))
    return jnp.concatenate(parts, axis=1)


def weights_kernel(k1_ref, k2_ref, t1_ref, t1t_ref, t2_ref, t2t_ref):
    for t, (a, c) in enumerate(TAPS):
        k1 = [k1_ref[a * 9 + b * 3 + c].astype(F32) for b in range(3)]
        k2 = [k2_ref[a * 9 + b * 3 + c].astype(F32) for b in range(3)]
        forward = jnp.concatenate(k1, axis=1)
        back = jnp.concatenate([x.T for x in reversed(k1)], axis=1)
        strided = jnp.concatenate([x.T for x in k2], axis=1)
        even = jnp.concatenate([k2[2], k2[0]], axis=1)
        for h in range(10):
            t1_ref[t, h * 32 : (h + 1) * 32, :] = place(forward, 32 * h, 384).astype(BF16)
            if h % 2 == 0:
                strip = place(even, 32 * h, 384)
            else:
                strip = place(k2[1], 32 * (h + 1), 384)
            t2t_ref[t, h * 32 : (h + 1) * 32, :] = strip.astype(BF16)
        for h in range(8):
            t1t_ref[t, h * 32 : (h + 1) * 32, :] = place(back, 32 * h, 320).astype(BF16)
        for g in range(4):
            t2_ref[t, g * 64 : (g + 1) * 64, :] = place(strided, 64 * g, 320).astype(BF16)


def strip_sum(g, rows, blocks, jump):
    total = None
    for n in range(blocks):
        part = g[n * rows : (n + 1) * rows, n * jump : n * jump + 96]
        total = part if total is None else total + part
    return total


def first_kernel(
    x_ref, og_ref, up_ref, down_ref, bias_ref, t1_ref, t2t_ref, rows_ref,
    grads_ref, gp_ref, act_ref,
    xs_ref, ogs_ref, own_ref,
):
    j = lax.axis_index("sx")
    t = lax.axis_index("sy")
    low = t > 0
    high = t < NY - 1
    none = jnp.zeros((64, 256), BF16)
    for n, cls in enumerate(CLASSES):
        at = slice(n * 256, (n + 1) * 256)
        x = jnp.concatenate(
            [jnp.where(low, up_ref[:, at], none), x_ref[:, at], jnp.where(high, down_ref[:, at], none)],
            axis=0,
        )
        store_variants(xs_ref, x, cls)
    og_main = og_ref[...]
    at = slice(1024, 1280)
    og = jnp.concatenate(
        [jnp.where(low, up_ref[:, at], none), og_main, jnp.where(high, down_ref[:, at], none)], axis=0
    )
    ogs_ref[0] = og
    ogs_ref[1] = ahead(og, 1)
    ogs_ref[2] = ahead(og, 32)
    ogs_ref[3] = ahead(ogs_ref[1], 32)

    row = lax.broadcasted_iota(jnp.int32, (320, 256), 0)
    u = lax.rem(lax.broadcasted_iota(jnp.int32, (320, 256), 1), 32)
    row_ok = ((row >= 32) | low) & ((row < 288) | high)
    bias = bias_ref[...]
    for n, (pd, pw) in enumerate(CLASSES):
        pre = None
        for tap, (a, c) in enumerate(TAPS):
            part = dot(t1_ref[tap], xs_ref[variant(pd, pw, a - 1, c - 1)])
            pre = part if pre is None else pre + part
        pre = pre + bias
        local = 2 * u + pw
        wide = local + (32 * j - 2)
        ok = row_ok & (local >= 1) & (local <= 34) & (wide >= 0) & (wide < W)
        sigma = jax.nn.sigmoid(pre)
        act_ref[n] = jnp.where(ok, pre * sigma, 0.0).astype(BF16)
        grad = None
        for a, sd in ((1, 0),) if pd == 0 else ((2, 0), (0, 1)):
            for c, sw in ((1, 0),) if pw == 0 else ((2, 0), (0, 1)):
                part = dot(t2t_ref[a * 3 + c], ogs_ref[sd * 2 + sw])
                grad = part if grad is None else grad + part
        grad = jnp.where(ok, grad * sigma * (1.0 + pre * (1.0 - sigma)), 0.0)
        gp_ref[n] = grad.astype(BF16)
        mine = (u[32:288] >= 1) & (u[32:288] <= 16)
        own_ref[n] = jnp.where(mine, grad[32:288], 0.0).astype(BF16)

    lane = lax.rem(lax.broadcasted_iota(jnp.int32, (256, 256), 1), 32)
    og_own = jnp.where((lane >= 1) & (lane <= 16), og_main.astype(F32), 0.0).astype(BF16)
    blank = jnp.zeros((64, 32), F32)
    ones_hi = []
    for tap, (a, c) in enumerate(TAPS):
        g = dot_nt(og_own, act_variant(act_ref, a, c))
        two = jnp.concatenate([strip_sum(g, 64, 4, 64), blank], axis=1)
        for s in range(NX):
            grads_ref[s, tap * 8 : (tap + 1) * 8, :] = two[8 * s : 8 * s + 8]
        g = None
        for n, (pd, pw) in enumerate(CLASSES):
            part = dot_nt(own_ref[n], xs_ref[variant(pd, pw, a - 1, c - 1), 32:352, :])
            g = part if g is None else g + part
        ones_hi.append(jnp.concatenate([strip_sum(g, 32, 8, 32), blank[0:32]], axis=1))
    one = jnp.concatenate(ones_hi, axis=0)
    hi = one.astype(BF16)
    rest = one - hi.astype(F32)
    mid = rest.astype(BF16)
    low_part = (rest - mid.astype(F32)).astype(BF16)
    rows = rows_ref[...]
    one = (dot(rows, hi) + dot(rows, mid)) + dot(rows, low_part)
    for s in range(NX):
        grads_ref[s, 72:112, :] = one[s * 40 : (s + 1) * 40]


def act_variant(act_ref, a, c):
    pd, sd = step(0, a - 1)
    pw, sw = step(0, c - 1)
    x = act_ref[pd * 2 + pw]
    if sw:
        x = behind(x, 1)
    if sd:
        x = behind(x, 32)
    return x


def second_kernel(gp_ref, act_ref, t1t_ref, t2_ref, scol_ref, gcol_ref, out_ref, gs_ref):
    out = None
    for tap, (a, c) in enumerate(TAPS):
        part = dot(t2_ref[tap], act_variant(act_ref, a, c))
        out = part if out is None else out + part
    out = dot(out.astype(BF16), scol_ref[...])
    for s in range(NX):
        out_ref[s, 128:160, :] = jnp.concatenate(
            [out[g * 64 + 8 * s : g * 64 + 8 * s + 8] for g in range(4)], axis=0
        ).astype(BF16)
    for n, cls in enumerate(CLASSES):
        store_variants(gs_ref, gp_ref[n], cls)
    grads = []
    for pd, pw in CLASSES:
        vol = None
        for tap, (a, c) in enumerate(TAPS):
            part = dot(t1t_ref[tap], gs_ref[variant(pd, pw, 1 - a, 1 - c)])
            vol = part if vol is None else vol + part
        grads.append(vol.astype(BF16))
    for q in range(2):
        at = slice(q * 128, (q + 1) * 128)
        cat = jnp.concatenate(
            [grads[n][half * 128 : (half + 1) * 128, at] for half in range(2) for n in range(4)], axis=1
        )
        got = move(cat, gcol_ref[...])
        for e in range(4):
            out_ref[4 * q + e, 0:128, :] = got[:, e * 128 : (e + 1) * 128]


def sum_kernel(r_ref, out_ref):
    total = r_ref[0]
    for s in range(1, r_ref.shape[0]):
        total = total + r_ref[s]
    out_ref[...] = total


def append_kernel(g_ref, buf_ref, out_ref):
    one = g_ref[72:112, :]
    hi = one.astype(BF16).astype(F32)
    lo = one - hi
    both = jnp.concatenate([hi, lo], axis=0).astype(BF16)
    for s in range(NX):
        out_ref[s] = both


def last_kernel(
    r_ref, g_ref, fcol_ref, rows_ref, ecol_ref, og_rows_ref, krow_ref,
    strided_ref, two_ref, one_ref, vol_ref, *, out_scale, in_scale,
):
    halves = []
    for q in range(2):
        cat = jnp.concatenate([r_ref[4 * q + s, 0:128, :] for s in range(4)], axis=1)
        halves.append(move(cat, fcol_ref[...]))
    for pd in range(2):
        blocks = []
        for half in range(2):
            at = slice((pd * 2 + half) * 128, (pd * 2 + half + 1) * 128)
            blocks.append(jnp.concatenate([halves[0][:, at], halves[1][:, at]], axis=1))
        vol_ref[pd * 256 : (pd + 1) * 256, :] = move(rows_ref[...], jnp.concatenate(blocks, axis=0))
    cat = jnp.concatenate([r_ref[s, 128:160, :] for s in range(NX)], axis=1)
    got = move(cat, ecol_ref[...])
    got = jnp.concatenate([got[:, e * 128 : (e + 1) * 128] for e in range(8)], axis=0)
    strided_ref[...] = move(og_rows_ref[...], got)
    hi = jnp.concatenate([r_ref[s, 160:200, :].astype(F32) for s in range(NX)], axis=0).astype(BF16)
    lo = jnp.concatenate([r_ref[s, 200:240, :].astype(F32) for s in range(NX)], axis=0).astype(BF16)
    one = (dot(krow_ref[...], hi) + dot(krow_ref[...], lo)) * in_scale
    two = g_ref[0:72, :] * out_scale
    for tap, (a, c) in enumerate(TAPS):
        for b in range(3):
            at = slice(b * 32, (b + 1) * 32)
            one_ref[a * 9 + b * 3 + c] = one[tap * 32 : (tap + 1) * 32, at]
            two_ref[a * 9 + b * 3 + c] = two[tap * 8 : (tap + 1) * 8, at]


def call(body, outs, args, scratch=(), specs=None, out_specs=None, aliases=None, grid=()):
    return pl.pallas_call(
        body,
        out_shape=outs,
        grid=grid,
        in_specs=specs or [pl.BlockSpec(memory_space=pltpu.VMEM)] * len(args),
        out_specs=out_specs or jax.tree.map(lambda _: pl.BlockSpec(memory_space=pltpu.VMEM), outs),
        scratch_shapes=list(scratch),
        input_output_aliases=aliases or {},
        compiler_params=pltpu.CompilerParams(vmem_limit_bytes=VMEM),
    )(*args)


def shape(*dims, dtype=BF16):
    return jax.ShapeDtypeStruct(dims, dtype)


def per_device(volume, kernel_one, bias_one, kernel_two, out_grad):
    out_scale = (8 * 128 * 128) ** (-0.5)
    in_scale = (16 * 256 * 256) ** (-0.5)
    chunks = call(
        pack_kernel,
        shape(NX, 256, 128),
        (
            volume.reshape(512, 256),
            out_grad.reshape(256, 128),
            const(row_order(1, 32, 8)),
            const(row_order(8, 8, 4)),
            const(spread_columns()),
        ),
    )
    got = lax.all_to_all(chunks, "sx", 0, 0)
    t1, t1t, t2, t2t = call(
        weights_kernel,
        (shape(9, 320, 384), shape(9, 256, 320), shape(9, 256, 320), shape(9, 320, 384)),
        (
            kernel_one.transpose(2, 3, 4, 0, 1).reshape(27, C, C),
            kernel_two.transpose(2, 3, 4, 1, 0).reshape(27, C, K),
        ),
    )
    bias = jnp.tile(bias_one.astype(F32), 10)[:, None]
    x, og, up, down = call(
        unpack_kernel,
        (shape(256, 1024), shape(256, 256), shape(64, 1280), shape(64, 1280)),
        (got, const(class_columns()), const(cotangent_columns())),
    )
    up = lax.ppermute(up, "sy", [(i, (i + 1) % NY) for i in range(NY)])
    down = lax.ppermute(down, "sy", [((i + 1) % NY, i) for i in range(NY)])
    grads, gp, act = call(
        first_kernel,
        (shape(NX, 112, 128, dtype=F32), shape(4, 320, 256), shape(4, 320, 256)),
        (x, og, up, down, bias, t1, t2t, const(kernel_rows())),
        scratch=(
            pltpu.VMEM((16, 384, 256), BF16),
            pltpu.VMEM((4, 384, 256), BF16),
            pltpu.VMEM((4, 256, 256), BF16),
        ),
    )
    grads = lax.all_to_all(grads, "sx", 0, 0)
    buffer = call(
        second_kernel,
        shape(NX, 240, 128),
        (gp, act, t1t, t2, const(strided_columns()), const(gather_columns())),
        scratch=(pltpu.VMEM((16, 320, 256), BF16),),
    )
    grads = call(sum_kernel, shape(112, 128, dtype=F32), (grads,))
    for bit in (1, 2, 4, 8, 16):
        grads = grads + lax.ppermute(grads, "sy", [(i, i ^ bit) for i in range(NY)])
    buffer = call(
        append_kernel,
        shape(NX, 240, 128),
        (grads, buffer),
        specs=[pl.BlockSpec((112, 128), lambda n: (0, 0)), pl.BlockSpec(memory_space=pl.ANY)],
        out_specs=pl.BlockSpec((NX, 80, 128), lambda n: (0, 2, 0)),
        grid=(1,),
        aliases={1: 0},
    )
    got = lax.all_to_all(buffer, "sx", 0, 0)
    strided, two, one, vol = call(
        functools.partial(last_kernel, out_scale=out_scale, in_scale=in_scale),
        (shape(256, 128), shape(27, 8, C, dtype=F32), shape(27, C, C, dtype=F32), shape(512, 256)),
        (
            got,
            grads,
            const(plane_columns()),
            const(row_order(1, 8, 32)),
            const(strided_planes()),
            const(row_order(8, 4, 8)),
            const(kernel_rows().T),
        ),
    )
    return (
        strided.reshape(8, 8, 4, 128),
        two.reshape(3, 3, 3, 8, C).transpose(3, 4, 0, 1, 2),
        one.reshape(3, 3, 3, C, C).transpose(3, 4, 0, 1, 2),
        vol.reshape(2, C, 8, W),
    )


def solution(mesh):
    return jax.shard_map(
        per_device,
        mesh=mesh,
        in_specs=(P("sx", None, "sy", None), P(), P(), P(), P(None, "sx", "sy", None)),
        out_specs=(
            P(None, "sx", "sy", None),
            P("sx", None, None, None, None),
            P(),
            P("sx", None, "sy", None),
        ),
        check_vma=False,
    )
```

time: 479 us -> 97.5 us (0.20); the launches traced: 471 us -> 96.7 us
  waiting for transfers between devices: 244 us -> 8.38 us
  local copies, waits for them, and re-layouts: 91.1 us -> 6.37 us
  matrix products: 55.9 us -> 0 us
  blocking collectives: 0 us -> 38.7 us
  starting transfers between devices: 51.5 us -> 20.2 us
  Pallas kernels: 0 us -> 22.2 us
  other arithmetic: 14.1 us -> 0.04 us
  between operations: 14.9 us -> 0.84 us
    psum x1 -> x0, waiting for transfers between devices: 242 us -> none  [per_device(): summed = lax.psum((kernel_one_part, kernel_part), ('sx', 'sy'))]
    conv_general_dilated x6 -> x0, matrix products: 55.9 us -> none  [the longest x2 41.2 us: kernel_conv(): lax.conv_general_dilated(inputs[None], grads[None], (1, 1, 1), pads, rhs_...]
    conv_general_dilated x22 -> x0, local copies, waits for them, and re-layouts: 42.8 us -> none  [the longest x9 21.5 us: forward_conv(): lax.conv_general_dilated(inputs[None], weights, strides, pads, dimension_...]
    all_to_all x0 -> x3, blocking collectives: none -> 38.7 us  [the longest x1 14.7 us: per_device(): got = lax.all_to_all(chunks, 'sx', 0, 0)]
    pallas_call x0 -> x8, Pallas kernels: none -> 22.2 us  [call(): pl.pallas_call(body, out_shape=outs, grid=grid, in_specs=specs or [pl.Blo...]
    ppermute x12 -> x7, starting transfers between devices: 42.2 us -> 20.2 us  [the longest x5 16.8 us: per_device(): grads = grads + lax.ppermute(grads, 'sy', [(i, i ^ bit) for i in range(NY)])]
    broadcast_in_dim x7 -> x0, local copies, waits for them, and re-layouts: 18.5 us -> none  [the longest x4 16.2 us: forward_conv(): inputs[None]]
    all_to_all x2 -> x0, starting transfers between devices: 9.32 us -> none  [the longest x1 5.02 us: per_device(): lax.all_to_all(out_grad, 'sx', split_axis=0, concat_axis=1, tiled=True)]
  transfers between devices with their start and end apart: 15 -> 7, of which waited for: 2 -> 4; matrix products, arithmetic and copies ran while one was open for 33% -> 0% of each run, Pallas kernels for 0% -> 9%
where the time goes in v1:
time: 97.5 us; the launch traced here: 96.7 us
  blocking collectives  38.7 us (40%)
  Pallas kernels  22.2 us (23%)
  starting transfers between devices  20.2 us (21%)
  waiting for transfers between devices  8.38 us (9%)
  local copies, waits for them, and re-layouts  6.37 us (7%)
    pallas_call x8, Pallas kernels, call(): pl.pallas_call(body, out_shape=outs, grid=grid, in_specs=specs or [pl.Blo...  22.2 us
    ppermute x5, starting transfers between devices, per_device(): grads = grads + lax.ppermute(grads, 'sy', [(i, i ^ bit) for i in range(NY)])  16.8 us
    all_to_all x1, blocking collectives, per_device(): got = lax.all_to_all(chunks, 'sx', 0, 0)  14.7 us
    all_to_all x1, blocking collectives, per_device(): grads = lax.all_to_all(grads, 'sx', 0, 0)  12.6 us
    all_to_all x1, blocking collectives, per_device(): got = lax.all_to_all(buffer, 'sx', 0, 0)  11.4 us
    ppermute x5, waiting for transfers between devices, per_device(): grads = grads + lax.ppermute(grads, 'sy', [(i, i ^ bit) for i in range(NY)])  8.37 us
    unnamed x38, local copies, waits for them, and re-layouts  6.21 us
    ppermute x1, starting transfers between devices, per_device(): down = lax.ppermute(down, 'sy', [((i + 1) % NY, i) for i in range(NY)])  3.24 us
  transfers between devices with their start and end apart: 7, of which 4 were waited for; matrix products, arithmetic and copies ran while one was open for 0% of the time, Pallas kernels for 9%

profile of v1, /device:TPU:16, one launch (start us, length us, event | category | flops | bytes accessed | tf_op | source)
XLA Modules:
  0.0 96.7 jit_solution(14020605647382103958)
XLA Ops:
  0.6 0.0 copy-start.2
  0.6 1.3 %copy-done.2 = bf16[640,1024]{1,0:T(8,128)(2,1)S(1)} copy-done((bf16[640,1024]{1,0:T(8,128)(2,1)S(1)}, bf16[640,1024]{1,0:T(8,128)(2,1)}, u32[]{:S(2)}) %copy-start.2) | copy-done | bytes 1310744
  2.0 0.0 copy-start.7
  2.0 0.9 copy-done.7
  2.9 0.0 copy-start.14
  2.9 0.9 copy-done.14
  3.8 0.0 copy-start.15
  3.8 0.9 copy-done.15
  4.7 0.0 copy-start.17
  4.7 0.8 copy-done.17
  5.6 0.0 copy-start.5
  5.6 0.0 copy-start.6
  5.6 0.0 copy-start.18
  5.6 0.0 copy-start.10
  5.6 0.0 copy-start.11
  5.6 1.0 %shard_map.201 = bf16[8,256,128]{2,1,0:T(8,128)(2,1)S(1)} custom-call(bf16[512,256]{1,0:T(8,128)(2,1)S(1)} %bitcast.16, bf16[256,128]{1,0:T(8,128)(2,1)S(1)} %bitcast.19, bf16[256,256]{1,0:T(8,128)(2,1)S(1)} %copy-done.15, bf16[256,256]{1,0:T(8,128)(2,1)S(1)} %copy-done.14, bf16[640,1024]{1,0:T(8,128)(2,1)S(1)} %copy-done.2), custom_call_target="tpu_custom_call" | custom-call | tf_op jit(solution)/shard_map/pallas_call | solution.py:392
  6.6 0.0 copy-start.8
  6.6 14.7 %all_to_all.15.r_ref = bf16[8,256,128]{2,1,0:T(8,128)(2,1)S(1)} all-to-all(bf16[8,256,128]{2,1,0:T(8,128)(2,1)S(1)} %shard_map.201), channel_id=1, replica_groups=mesh['sx'=8,'sy'=32] {'sx'}, dimensions={0} | all-to-all | bytes 1048576 | tf_op jit(solution)/shard_map/all_to_all | solution.py:422
  21.3 0.0 copy-done.5
  21.3 0.0 copy-done.6
  21.3 0.6 shard_map.202
  21.9 0.1 collective-permute-start
  22.0 3.2 %collective-permute-start.1 = (bf16[64,1280]{1,0:T(8,128)(2,1)S(1)}, bf16[64,1280]{1,0:T(8,128)(2,1)S(1)}, u32[]{:S(2)}, u32[]{:S(2)}) collective-permute-start(bf16[64,1280]{1,0:T(8,128)(2,1)S(1)} %get-tuple-element.22), channel_id=1, source_target_pairs={{1,0},{2,1},{3,2},{4,3},{5,4},{6,5},{7,6},{8,7},{9,8},{10,9},{11,1... | collective-permute-start | bytes 491528 | tf_op jit(solution)/shard_map/ppermute | solution.py:438
  25.2 0.0 copy-done.18
  25.2 0.2 broadcast_in_dim_tile.4.bias_ref
  25.4 0.0 copy-done.10
  25.4 0.0 copy-done.11
  25.4 3.1 %shard_map.203 = (bf16[9,320,384]{2,1,0:T(8,128)(2,1)S(1)}, bf16[9,256,320]{2,1,0:T(8,128)(2,1)S(1)}, bf16[9,256,320]{2,1,0:T(8,128)(2,1)S(1)}, bf16[9,320,384]{2,1,0:T(8,128)(2,1)}) custom-call(bf16[27,32,32]{2,1,0:T(8,128)(2,1)S(1)} %bitcast.17, bf16[27,32,64]{2,1,0:T(8,128)(2,1)S(1)} %bitcast.18), custom_call_target="tpu_custom_call" | custom-call | tf_op jit(solution)/shard_map/pallas_call | solution.py:392
  28.5 0.0 copy-start.1
  28.6 1.2 %copy-done.1 = bf16[9,256,320]{2,1,0:T(8,128)(2,1)} copy-done((bf16[9,256,320]{2,1,0:T(8,128)(2,1)}, bf16[9,256,320]{2,1,0:T(8,128)(2,1)S(1)}, u32[]{:S(2)}) %copy-start.1) | copy-done | bytes 1474584
  29.8 0.0 collective-permute-done.up_ref
  29.8 0.0 collective-permute-done.1.down_ref
  29.8 0.0 copy-done.8
  29.8 9.6 %shard_map.204 = (f32[8,112,128]{2,1,0:T(8,128)S(1)}, bf16[4,320,256]{2,1,0:T(8,128)(2,1)S(1)}, bf16[4,320,256]{2,1,0:T(8,128)(2,1)S(1)}) custom-call(bf16[256,1024]{1,0:T(8,128)(2,1)S(1)} %get-tuple-element.19.x_ref, bf16[256,256]{1,0:T(8,128)(2,1)S(1)} %get-tuple-element.20.og_ref, bf16[64,1280]{1,0:T(8,128)(2,1)S(1)} %collective-permute-done.up_ref, ...), custom_call_target="tpu_custom_call" | custom-call | tf_op jit(solution)/shard_map/pallas_call | solution.py:392
  39.4 0.0 copy-start.3
  39.4 0.0 copy-start.16
  39.4 12.6 %all_to_all.16.r_ref = f32[8,112,128]{2,1,0:T(8,128)S(1)} all-to-all(f32[8,112,128]{2,1,0:T(8,128)S(1)} %get-tuple-element.25), channel_id=1, replica_groups=mesh['sx'=8,'sy'=32] {'sx'}, dimensions={0} | all-to-all | bytes 917504 | tf_op jit(solution)/shard_map/all_to_all | solution.py:449
  52.0 1.1 %collective-permute-start.2 = (f32[112,128]{1,0:T(8,128)S(1)}, f32[112,128]{1,0:T(8,128)S(1)}, u32[]{:S(2)}, u32[]{:S(2)}) collective-permute-start(f32[112,128]{1,0:T(8,128)S(1)} %shard_map.205), channel_id=1, source_target_pairs={{0,1},{1,0},{2,3},{3,2},{4,5},{5,4},{6,7},{7,6},{8,9},{9,8},{10,11... | collective-permute-start | bytes 172040 | tf_op jit(solution)/shard_map/ppermute | solution.py:458
  53.1 0.9 collective-permute-done.2
  54.0 2.8 %collective-permute-start.3 = (f32[112,128]{1,0:T(8,128)S(1)}, f32[112,128]{1,0:T(8,128)S(1)}, u32[]{:S(2)}, u32[]{:S(2)}) collective-permute-start(f32[112,128]{1,0:T(8,128)S(1)} %add.15), channel_id=1, source_target_pairs={{0,2},{1,3},{2,0},{3,1},{4,6},{5,7},{6,4},{7,5},{8,10},{9,11},{10,... | collective-permute-start | bytes 172040 | tf_op jit(solution)/shard_map/ppermute | solution.py:458
  56.7 3.0 %collective-permute-done.3 = f32[112,128]{1,0:T(8,128)S(1)} collective-permute-done((f32[112,128]{1,0:T(8,128)S(1)}, f32[112,128]{1,0:T(8,128)S(1)}, u32[]{:S(2)}, u32[]{:S(2)}) %collective-permute-start.3) | collective-permute-done | bytes 57376 | tf_op jit(solution)/shard_map/ppermute | solution.py:458
  59.8 2.0 %collective-permute-start.4 = (f32[112,128]{1,0:T(8,128)S(1)}, f32[112,128]{1,0:T(8,128)S(1)}, u32[]{:S(2)}, u32[]{:S(2)}) collective-permute-start(f32[112,128]{1,0:T(8,128)S(1)} %add.16), channel_id=1, source_target_pairs={{0,4},{1,5},{2,6},{3,7},{4,0},{5,1},{6,2},{7,3},{8,12},{9,13},{10,... | collective-permute-start | bytes 172040 | tf_op jit(solution)/shard_map/ppermute | solution.py:458
  61.8 2.3 %collective-permute-done.4 = f32[112,128]{1,0:T(8,128)S(1)} collective-permute-done((f32[112,128]{1,0:T(8,128)S(1)}, f32[112,128]{1,0:T(8,128)S(1)}, u32[]{:S(2)}, u32[]{:S(2)}) %collective-permute-start.4) | collective-permute-done | bytes 57376 | tf_op jit(solution)/shard_map/ppermute | solution.py:458
  64.1 4.0 %collective-permute-start.5 = (f32[112,128]{1,0:T(8,128)S(1)}, f32[112,128]{1,0:T(8,128)S(1)}, u32[]{:S(2)}, u32[]{:S(2)}) collective-permute-start(f32[112,128]{1,0:T(8,128)S(1)} %add.17), channel_id=1, source_target_pairs={{0,8},{1,9},{2,10},{3,11},{4,12},{5,13},{6,14},{7,15},{8,0},{9,1},... | collective-permute-start | bytes 172040 | tf_op jit(solution)/shard_map/ppermute | solution.py:458
  68.0 2.2 %collective-permute-done.5 = f32[112,128]{1,0:T(8,128)S(1)} collective-permute-done((f32[112,128]{1,0:T(8,128)S(1)}, f32[112,128]{1,0:T(8,128)S(1)}, u32[]{:S(2)}, u32[]{:S(2)}) %collective-permute-start.5) | collective-permute-done | bytes 57376 | tf_op jit(solution)/shard_map/ppermute | solution.py:458
  70.2 7.0 %collective-permute-start.6 = (f32[112,128]{1,0:T(8,128)S(1)}, f32[112,128]{1,0:T(8,128)S(1)}, u32[]{:S(2)}, u32[]{:S(2)}) collective-permute-start(f32[112,128]{1,0:T(8,128)S(1)} %add.18), channel_id=1, source_target_pairs={{0,16},{1,17},{2,18},{3,19},{4,20},{5,21},{6,22},{7,23},{8,24},{9,... | collective-permute-start | bytes 172040 | tf_op jit(solution)/shard_map/ppermute | solution.py:458
  77.2 0.0 copy-done.3
  77.2 0.0 copy-done.16
  77.2 0.0 copy-start.4
  77.3 0.0 copy-start.9
  77.3 0.0 copy-start.12
  77.3 0.0 copy-start.13
  77.3 5.9 %shard_map.206.buf_ref = bf16[8,240,128]{2,1,0:T(8,128)(2,1)S(1)} custom-call(bf16[4,320,256]{2,1,0:T(8,128)(2,1)S(1)} %get-tuple-element.26.gp_ref, bf16[4,320,256]{2,1,0:T(8,128)(2,1)S(1)} %get-tuple-element.27.act_ref, bf16[9,256,320]{2,1,0:T(8,128)(2,1)S(1)} %get-tuple-element.28.t1t_ref, bf16[9,256,320]{2,1,0:T(8,128)(2,1)} %copy-done.1, ...), custom_call_target="tpu_custom_call" | custom-call | tf_op jit(solution)/shard_map/pallas_call | solution.py:392
  83.2 0.0 copy-start
  83.2 0.0 collective-permute-done.6
  83.2 11.4 %all_to_all.17.r_ref = bf16[8,240,128]{2,1,0:T(8,128)(2,1)S(1)} all-to-all(bf16[8,240,128]{2,1,0:T(8,128)(2,1)S(1)} %shard_map.207), channel_id=1, replica_groups=mesh['sx'=8,'sy'=32] {'sx'}, dimensions={0} | all-to-all | bytes 983040 | tf_op jit(solution)/shard_map/all_to_all | solution.py:468
  94.7 0.0 copy-done.4
  94.7 0.0 copy-done.9
  94.7 0.0 copy-done.12
  94.7 0.0 copy-done.13
  94.7 0.0 copy-done
  94.7 2.0 %shard_map.208 = (bf16[256,128]{1,0:T(8,128)(2,1)}, f32[27,8,32]{2,1,0:T(8,128)}, f32[27,32,32]{2,1,0:T(8,128)}, bf16[512,256]{1,0:T(8,128)(2,1)}) custom-call(bf16[8,240,128]{2,1,0:T(8,128)(2,1)S(1)} %all_to_all.17.r_ref, f32[112,128]{1,0:T(8,128)S(1)} %add.19.g_ref, bf16[512,512]{1,0:T(8,128)(2,1)S(1)} %copy-done.4, bf16[256,256]{1,0:T(8,128)(2,1)S(1)} %copy-done.13, ...), custom_call_target="tpu_custom_call" | custom-call | tf_op jit(solution)/shard_map/pallas_call | solution.py:392
  (8 shorter events, 0.1 us)
Async XLA Ops:
  0.6 1.3 %copy-start.2 = (bf16[640,1024]{1,0:T(8,128)(2,1)S(1)}, bf16[640,1024]{1,0:T(8,128)(2,1)}, u32[]{:S(2)}) copy-start(bf16[640,1024]{1,0:T(8,128)(2,1)} %constant.28.clone.cols_ref) | copy-start | bytes 3932164
  2.0 0.9 copy-start.7
  2.9 0.9 copy-start.14
  3.8 0.9 copy-start.15
  4.7 0.8 copy-start.17
  5.6 15.8 %copy-start.5 = (bf16[1024,256]{1,0:T(8,128)(2,1)S(1)}, bf16[1024,256]{1,0:T(8,128)(2,1)}, u32[]{:S(2)}) copy-start(bf16[1024,256]{1,0:T(8,128)(2,1)} %constant.30.clone.og_cols_ref) | copy-start | bytes 1572868
  5.6 15.8 %copy-start.6 = (bf16[512,512]{1,0:T(8,128)(2,1)S(1)}, bf16[512,512]{1,0:T(8,128)(2,1)}, u32[]{:S(2)}) copy-start(bf16[512,512]{1,0:T(8,128)(2,1)} %constant.29.clone.cls_ref) | copy-start | bytes 1572868
  5.6 19.7 %copy-start.18 = (bf16[32]{0:T(256)(128)(2,1)S(1)}, bf16[32]{0:T(256)(128)(2,1)}, u32[]{:S(2)}) copy-start(bf16[32]{0:T(256)(128)(2,1)} %param.20) | copy-start | bytes 196
  5.6 19.8 %copy-start.10 = (bf16[32,32,3,3,3]{1,0,4,3,2:T(8,128)(2,1)S(1)}, bf16[32,32,3,3,3]{1,0,4,3,2:T(8,128)(2,1)}, u32[]{:S(2)}) copy-start(bf16[32,32,3,3,3]{1,0,4,3,2:T(8,128)(2,1)} %param.19) | copy-start | bytes 165892
  5.6 19.8 %copy-start.11 = (bf16[64,32,3,3,3]{0,1,4,3,2:T(8,128)(2,1)S(1)}, bf16[64,32,3,3,3]{0,1,4,3,2:T(8,128)(2,1)}, u32[]{:S(2)}) copy-start(bf16[64,32,3,3,3]{0,1,4,3,2:T(8,128)(2,1)} %param.21) | copy-start | bytes 331780
  6.6 23.2 %copy-start.8 = (bf16[320,288]{1,0:T(8,128)(2,1)S(1)}, bf16[320,288]{1,0:T(8,128)(2,1)}, u32[]{:S(2)}) copy-start(bf16[320,288]{1,0:T(8,128)(2,1)} %constant.31.clone.rows_ref) | copy-start | bytes 552964
  21.9 7.9 %collective-permute-start = (bf16[64,1280]{1,0:T(8,128)(2,1)S(1)}, bf16[64,1280]{1,0:T(8,128)(2,1)S(1)}, u32[]{:S(2)}, u32[]{:S(2)}) collective-permute-start(bf16[64,1280]{1,0:T(8,128)(2,1)S(1)} %get-tuple-element.21), channel_id=1, source_target_pairs={{0,1},{1,2},{2,3},{3,4},{4,5},{5,6},{6,7},{7,8},{8,9},{9,10},{10,1... | collective-permute-start | bytes 491528 | tf_op jit(solution)/shard_map/ppermute | solution.py:437
  22.0 7.8 %collective-permute-start.1 = (bf16[64,1280]{1,0:T(8,128)(2,1)S(1)}, bf16[64,1280]{1,0:T(8,128)(2,1)S(1)}, u32[]{:S(2)}, u32[]{:S(2)}) collective-permute-start(bf16[64,1280]{1,0:T(8,128)(2,1)S(1)} %get-tuple-element.22), channel_id=1, source_target_pairs={{1,0},{2,1},{3,2},{4,3},{5,4},{6,5},{7,6},{8,7},{9,8},{10,9},{11,1... | collective-permute-start | bytes 491528 | tf_op jit(solution)/shard_map/ppermute | solution.py:438
  28.5 1.2 %copy-start.1 = (bf16[9,256,320]{2,1,0:T(8,128)(2,1)}, bf16[9,256,320]{2,1,0:T(8,128)(2,1)S(1)}, u32[]{:S(2)}) copy-start(bf16[9,256,320]{2,1,0:T(8,128)(2,1)S(1)} %get-tuple-element.29.t2_ref) | copy-start | bytes 4423684
  39.4 37.9 %copy-start.3 = (bf16[1024,512]{1,0:T(8,128)(2,1)S(1)}, bf16[1024,512]{1,0:T(8,128)(2,1)}, u32[]{:S(2)}) copy-start(bf16[1024,512]{1,0:T(8,128)(2,1)} %constant.33.clone.gcol_ref) | copy-start | bytes 3145732
  39.4 37.9 %copy-start.16 = (bf16[256,128]{1,0:T(8,128)(2,1)S(1)}, bf16[256,128]{1,0:T(8,128)(2,1)}, u32[]{:S(2)}) copy-start(bf16[256,128]{1,0:T(8,128)(2,1)} %constant.32.clone.scol_ref) | copy-start | bytes 196612
  52.0 2.0 %collective-permute-start.2 = (f32[112,128]{1,0:T(8,128)S(1)}, f32[112,128]{1,0:T(8,128)S(1)}, u32[]{:S(2)}, u32[]{:S(2)}) collective-permute-start(f32[112,128]{1,0:T(8,128)S(1)} %shard_map.205), channel_id=1, source_target_pairs={{0,1},{1,0},{2,3},{3,2},{4,5},{5,4},{6,7},{7,6},{8,9},{9,8},{10,11... | collective-permute-start | bytes 172040 | tf_op jit(solution)/shard_map/ppermute | solution.py:458
  54.0 5.8 %collective-permute-start.3 = (f32[112,128]{1,0:T(8,128)S(1)}, f32[112,128]{1,0:T(8,128)S(1)}, u32[]{:S(2)}, u32[]{:S(2)}) collective-permute-start(f32[112,128]{1,0:T(8,128)S(1)} %add.15), channel_id=1, source_target_pairs={{0,2},{1,3},{2,0},{3,1},{4,6},{5,7},{6,4},{7,5},{8,10},{9,11},{10,... | collective-permute-start | bytes 172040 | tf_op jit(solution)/shard_map/ppermute | solution.py:458
  59.8 4.3 %collective-permute-start.4 = (f32[112,128]{1,0:T(8,128)S(1)}, f32[112,128]{1,0:T(8,128)S(1)}, u32[]{:S(2)}, u32[]{:S(2)}) collective-permute-start(f32[112,128]{1,0:T(8,128)S(1)} %add.16), channel_id=1, source_target_pairs={{0,4},{1,5},{2,6},{3,7},{4,0},{5,1},{6,2},{7,3},{8,12},{9,13},{10,... | collective-permute-start | bytes 172040 | tf_op jit(solution)/shard_map/ppermute | solution.py:458
  64.1 6.1 %collective-permute-start.5 = (f32[112,128]{1,0:T(8,128)S(1)}, f32[112,128]{1,0:T(8,128)S(1)}, u32[]{:S(2)}, u32[]{:S(2)}) collective-permute-start(f32[112,128]{1,0:T(8,128)S(1)} %add.17), channel_id=1, source_target_pairs={{0,8},{1,9},{2,10},{3,11},{4,12},{5,13},{6,14},{7,15},{8,0},{9,1},... | collective-permute-start | bytes 172040 | tf_op jit(solution)/shard_map/ppermute | solution.py:458
  70.2 13.0 %collective-permute-start.6 = (f32[112,128]{1,0:T(8,128)S(1)}, f32[112,128]{1,0:T(8,128)S(1)}, u32[]{:S(2)}, u32[]{:S(2)}) collective-permute-start(f32[112,128]{1,0:T(8,128)S(1)} %add.18), channel_id=1, source_target_pairs={{0,16},{1,17},{2,18},{3,19},{4,20},{5,21},{6,22},{7,23},{8,24},{9,... | collective-permute-start | bytes 172040 | tf_op jit(solution)/shard_map/ppermute | solution.py:458
  77.2 17.4 %copy-start.4 = (bf16[512,512]{1,0:T(8,128)(2,1)S(1)}, bf16[512,512]{1,0:T(8,128)(2,1)}, u32[]{:S(2)}) copy-start(bf16[512,512]{1,0:T(8,128)(2,1)} %constant.34.clone.fcol_ref) | copy-start | bytes 1572868
  77.3 17.4 %copy-start.9 = (bf16[288,320]{1,0:T(8,128)(2,1)S(1)}, bf16[288,320]{1,0:T(8,128)(2,1)}, u32[]{:S(2)}) copy-start(bf16[288,320]{1,0:T(8,128)(2,1)} %constant.38.clone.krow_ref) | copy-start | bytes 552964
  77.3 17.4 %copy-start.12 = (bf16[256,256]{1,0:T(8,128)(2,1)S(1)}, bf16[256,256]{1,0:T(8,128)(2,1)}, u32[]{:S(2)}) copy-start(bf16[256,256]{1,0:T(8,128)(2,1)} %constant.37.clone.og_rows_ref) | copy-start | bytes 393220
  77.3 17.4 %copy-start.13 = (bf16[256,256]{1,0:T(8,128)(2,1)S(1)}, bf16[256,256]{1,0:T(8,128)(2,1)}, u32[]{:S(2)}) copy-start(bf16[256,256]{1,0:T(8,128)(2,1)} %constant.35.clone.rows_ref) | copy-start | bytes 393220
  83.2 11.5 %copy-start = (bf16[1024,1024]{1,0:T(8,128)(2,1)S(1)}, bf16[1024,1024]{1,0:T(8,128)(2,1)}, u32[]{:S(2)}) copy-start(bf16[1024,1024]{1,0:T(8,128)(2,1)} %constant.36.clone.ecol_ref) | copy-start | bytes 6291460

commit v2 on v1

v2 whole, which is shorter than its diff:
```python
import functools

import jax
import jax.numpy as jnp
from jax import lax
from jax.experimental import pallas as pl
from jax.experimental.pallas import tpu as pltpu
from jax.sharding import PartitionSpec as P

F32 = jnp.float32
BF16 = jnp.bfloat16
NX = 8
NY = 32
C = 32
K = 64
W = 256
CLASSES = ((0, 0), (0, 1), (1, 0), (1, 1))
TAPS = tuple((a, c) for a in range(3) for c in range(3))


def iota(dims, axis):
    return lax.broadcasted_iota(jnp.int32, dims, axis)


def pick(mask):
    return jnp.where(mask, 1.0, 0.0).astype(BF16)


def dot(a, b):
    return jnp.dot(a, b, preferred_element_type=F32)


def move(a, b):
    return dot(a, b).astype(BF16)


def dot_nt(a, b):
    return lax.dot_general(a, b, (((1,), (1,)), ((), ())), preferred_element_type=F32)


def ahead(x, n):
    return jnp.concatenate([x[:, n:], jnp.zeros((x.shape[0], n), x.dtype)], axis=1)


def behind(x, n):
    return jnp.concatenate([jnp.zeros((x.shape[0], n), x.dtype), x[:, :-n]], axis=1)


def step(parity, offset):
    at = parity + offset
    return (1, 1) if at == -1 else (0, 1) if at == 2 else (at, 0)


def variant(pd, pw, da, dc):
    qd, sd = step(pd, da)
    qw, sw = step(pw, dc)
    return ((qd * 2 + qw) * 2 + sd) * 2 + sw


def variants(x, cls):
    move_d = behind if cls[0] else ahead
    move_w = behind if cls[1] else ahead
    along = move_w(x, 1)
    return x, along, move_d(x, 32), move_d(along, 32)


def store_variants(ref, x, cls):
    base = (cls[0] * 2 + cls[1]) * 4
    for n, form in enumerate(variants(x, cls)):
        ref[base + n] = form


def pack_kernel(vol_hbm, og_hbm, out_ref, vol_ref, og_ref, sems):
    copies = (
        pltpu.make_async_copy(vol_hbm, vol_ref, sems.at[0]),
        pltpu.make_async_copy(og_hbm, og_ref, sems.at[1]),
    )
    for copy in copies:
        copy.start()
    row = iota((256, 256), 0)
    col = iota((256, 256), 1)
    by_row = pick(col == (row & 31) * 8 + (row >> 5))
    by_kind = pick(col == (row & ~31) + (row & 7) * 4 + ((row >> 3) & 3))
    lane = iota((1, 128), 1)
    cls = jnp.where(lane >= 20, 1, 0) + jnp.where(lane >= 40, 1, 0) + jnp.where(lane >= 60, 1, 0)
    u = lane - 20 * cls
    at = iota((128, 128), 0)
    chosen = []
    for j in range(NX):
        w = jnp.where((lane < 80) & (u < 18), 32 * j - 2 + 2 * u + (cls & 1), -1)
        pieces = []
        for pd in range(2):
            from_plane = jnp.where(cls >> 1 == pd, w, -1)
            for block in range(max(0, 32 * j - 2) // 128, min(W - 1, 32 * j + 33) // 128 + 1):
                pieces.append((pd, block, pick(at + 128 * block == from_plane)))
        g = jnp.where((lane >= 80) & (lane < 98), 16 * j - 1 + lane - 80, -1)
        pieces.append((2, 0, pick(at == g)))
        chosen.append(pieces)
    for copy in copies:
        copy.wait()
    planes = (
        move(by_row, vol_ref[0:256]),
        move(by_row, vol_ref[256:512]),
        move(by_kind, og_ref[...]),
    )
    for j in range(NX):
        cat = jnp.concatenate(
            [planes[n][:, block * 128 : (block + 1) * 128] for n, block, _ in chosen[j]], axis=1
        )
        out_ref[j] = move(cat, jnp.concatenate([m for _, _, m in chosen[j]], axis=0))


def unpack_kernel(r_ref, cls_ref, og_cols_ref, x_ref, og_ref, up_ref, down_ref):
    for q in range(2):
        cat = jnp.concatenate([r_ref[4 * q + s] for s in range(4)], axis=1)
        got = move(cat, cls_ref[...])
        for cls in range(4):
            at = slice(cls * 256 + q * 128, cls * 256 + (q + 1) * 128)
            part = got[:, cls * 128 : (cls + 1) * 128]
            x_ref[:, at] = part
            up_ref[:, at] = part[192:256]
            down_ref[:, at] = part[0:64]
    parts = []
    for s in range(NX):
        parts.append(jnp.concatenate([r_ref[s, e * 32 : (e + 1) * 32, :] for e in range(8)], axis=1))
    og = dot(jnp.concatenate(parts, axis=0), og_cols_ref[...])
    og = jnp.concatenate(
        [og[s * 32 + g * 8 : s * 32 + g * 8 + 8] for g in range(4) for s in range(NX)], axis=0
    ).astype(BF16)
    og_ref[...] = og
    up_ref[:, 1024:1280] = og[192:256]
    down_ref[:, 1024:1280] = og[0:64]


def place(strip, offset, width):
    if offset >= width:
        return jnp.zeros((strip.shape[0], width), strip.dtype)
    first = max(0, -offset)
    strip = strip[:, first : min(strip.shape[1], width - offset)]
    offset += first
    parts = [strip]
    if offset:
        parts.insert(0, jnp.zeros((strip.shape[0], offset), strip.dtype))
    rest = width - offset - strip.shape[1]
    if rest:
        parts.append(jnp.zeros((strip.shape[0], rest), strip.dtype))
    return jnp.concatenate(parts, axis=1)


def from_row(rows, target):
    return pick(iota((rows, target.shape[1]), 0) == target)


def kernel_blocks(ref, a, c):
    return [ref[a * 9 + b * 3 + c].astype(F32) for b in range(3)]


def weights_kernel(
    k1_ref, k2_ref, strips_ref, even_ref, odd_ref, t1h_ref, t2th_ref, cls_ref, og_cols_ref
):
    col = iota((1, 512), 1)
    u = col & 31
    cls_ref[...] = from_row(512, jnp.where(u < 18, ((col >> 5) & 3) * 128 + (col >> 7) * 20 + u, -1))
    col, u = col[:, 0:256], u[:, 0:256]
    og_cols_ref[...] = from_row(1024, jnp.where(u < 18, (col >> 5) * 128 + 80 + u, -1))
    gap = jnp.zeros((C, C), F32)
    wide = jnp.zeros((C, K), F32)
    for t, (a, c) in enumerate(TAPS):
        k1 = kernel_blocks(k1_ref, a, c)
        k2 = kernel_blocks(k2_ref, a, c)
        forward = jnp.concatenate(k1, axis=1)
        even = jnp.concatenate([k2[2], k2[0]], axis=1)
        for r in range(4):
            strips_ref[t, r] = place(forward, 32 * r, 256).astype(BF16)
        for r in range(2):
            even_ref[t, r] = place(even, 64 * r, 256).astype(BF16)
            odd_ref[t, r] = place(k2[1], 64 * r, 128).astype(BF16)
        rim = (
            (k1[0], k1[1], gap, gap),
            (gap, k1[0], gap, gap),
            (gap, gap, k1[2], gap),
            (gap, gap, k1[1], k1[2]),
        )
        t1h_ref[:, t * 128 : (t + 1) * 128] = jnp.concatenate(
            [jnp.concatenate(r, axis=1) for r in rim], axis=0
        ).astype(BF16)
        rim = ((k2[2], wide), (wide, wide), (wide, k2[0]), (wide, k2[1]))
        t2th_ref[t] = jnp.concatenate([jnp.concatenate(r, axis=1) for r in rim], axis=0).astype(BF16)


def window(strip, at):
    if at == 0:
        return strip
    none = jnp.zeros((strip.shape[0], 128), strip.dtype)
    return jnp.concatenate([strip[:, 128:], none] if at < 0 else [none, strip[:, :128]], axis=1)


def build_forward(strips_ref, even_ref, odd_ref, t1_ref, t2t_ref):
    none = jnp.zeros((C, 128), BF16)
    for t in range(9):
        for h in range(10):
            at = slice(h * 32, (h + 1) * 32)
            r = (h + 2) % 4
            t1_ref[t, at, :] = window(strips_ref[t, r], (h - 2 - r) // 4)
            if h % 2 == 0:
                r = (h // 2 + 1) % 2
                t2t_ref[t, at, :] = window(even_ref[t, r], (h // 2 - 1 - r) // 2)
            else:
                n = h // 2
                strip = odd_ref[t, n % 2] if n < 4 else none
                t2t_ref[t, at, :] = jnp.concatenate([none, strip] if n > 1 else [strip, none], axis=1)


def build_back(k1_ref, k2_ref, t1t_ref, t2_ref):
    for t, (a, c) in enumerate(TAPS):
        back = jnp.concatenate([x.T for x in reversed(kernel_blocks(k1_ref, a, c))], axis=1)
        strided = jnp.concatenate([x.T for x in kernel_blocks(k2_ref, a, c)], axis=1)
        for h in range(8):
            t1t_ref[t, h * 32 : (h + 1) * 32, :] = place(back, 32 * h, 320).astype(BF16)
        for g in range(4):
            t2_ref[t, g * 64 : (g + 1) * 64, :] = place(strided, 64 * g, 320).astype(BF16)


def strip_sum(g, blocks, jump):
    width = g.shape[1] // blocks
    total = None
    for n in range(blocks):
        part = g[n * jump : n * jump + 96, n * width : (n + 1) * width]
        total = part if total is None else total + part
    return total


def conv_taps(pd, pw, sign):
    return [(tap, variant(pd, pw, sign * (a - 1), sign * (c - 1))) for tap, (a, c) in enumerate(TAPS)]


def spread_taps(pd, pw):
    depth = ((1, 0),) if pd == 0 else ((2, 0), (0, 1))
    width = ((1, 0),) if pw == 0 else ((2, 0), (0, 1))
    return [(a * 3 + c, sd * 2 + sw) for a, sd in depth for c, sw in width]


def tap_sum(weights_ref, inputs_ref, pairs):
    total = None
    for tap, at in pairs:
        part = dot(weights_ref[tap], inputs_ref[at])
        total = part if total is None else total + part
    return total


def store_cotangents(ref, og):
    along = ahead(og, 1)
    ref[0] = og
    ref[1] = along
    ref[2] = ahead(og, 32)
    ref[3] = ahead(along, 32)


def inner_kernel(
    x_ref, og_ref, strips_ref, even_ref, odd_ref,
    xs_ref, pre_ref, grad_ref,
    ogs_ref, t1_ref, t2t_ref,
):
    build_forward(strips_ref, even_ref, odd_ref, t1_ref, t2t_ref)
    for n, cls in enumerate(CLASSES):
        store_variants(xs_ref, x_ref[:, n * 256 : (n + 1) * 256], cls)
    store_cotangents(ogs_ref, og_ref[...])
    for n, (pd, pw) in enumerate(CLASSES):
        pre_ref[n] = tap_sum(t1_ref, xs_ref, conv_taps(pd, pw, 1))
        grad_ref[n] = tap_sum(t2t_ref, ogs_ref, spread_taps(pd, pw))


def first_kernel(
    xs_ref, pre_ref, ga_ref, og_ref, up_ref, down_ref, bias_ref, t1h_ref, t2th_ref,
    grads_ref, gp_ref, act_ref,
    rim_ref, ogs_ref, own_ref,
):
    j = lax.axis_index("sx")
    t = lax.axis_index("sy")
    low = t > 0
    high = t < NY - 1
    none = jnp.zeros((64, 256), BF16)

    def rim(at):
        return jnp.concatenate(
            [jnp.where(low, up_ref[:, at], none), jnp.where(high, down_ref[:, at], none)], axis=0
        )

    uses = [
        (n, tap, at) for n, (pd, pw) in enumerate(CLASSES) for tap, at in conv_taps(pd, pw, 1)
    ]
    for n, cls in enumerate(CLASSES):
        forms = variants(rim(slice(n * 256, (n + 1) * 256)), cls)
        for m, tap, at in uses:
            if at // 4 == n:
                rim_ref[m, tap * 128 : (tap + 1) * 128, :] = forms[at % 4]
    store_cotangents(ogs_ref, rim(slice(1024, 1280)))

    def with_rim(inner, outer):
        return jnp.concatenate(
            [inner[0:64] + outer[0:64], inner[64:256], inner[256:320] + outer[64:128]], axis=0
        )

    row = lax.broadcasted_iota(jnp.int32, (320, 256), 0)
    u = lax.rem(lax.broadcasted_iota(jnp.int32, (320, 256), 1), 32)
    row_ok = ((row >= 32) | low) & ((row < 288) | high)
    bias = bias_ref[...]
    for n, (pd, pw) in enumerate(CLASSES):
        pre = with_rim(pre_ref[n], dot(t1h_ref[...], rim_ref[n])) + bias
        local = 2 * u + pw
        wide = local + (32 * j - 2)
        ok = row_ok & (local >= 1) & (local <= 34) & (wide >= 0) & (wide < W)
        sigma = jax.nn.sigmoid(pre)
        act_ref[n] = jnp.where(ok, pre * sigma, 0.0).astype(BF16)
        grad = with_rim(ga_ref[n], tap_sum(t2th_ref, ogs_ref, spread_taps(pd, pw)))
        grad = jnp.where(ok, grad * sigma * (1.0 + pre * (1.0 - sigma)), 0.0)
        gp_ref[n] = grad.astype(BF16)
        mine = (u[32:288] >= 1) & (u[32:288] <= 16)
        own_ref[n] = jnp.where(mine, grad[32:288], 0.0).astype(BF16)

    lane = lax.rem(lax.broadcasted_iota(jnp.int32, (256, 256), 1), 32)
    og_own = jnp.where((lane >= 1) & (lane <= 16), og_ref[...].astype(F32), 0.0).astype(BF16)
    twos, ones = [], []
    for tap, (a, c) in enumerate(TAPS):
        twos.append(strip_sum(dot_nt(act_variant(act_ref, a, c), og_own), 4, 64))
        g = None
        for n, (pd, pw) in enumerate(CLASSES):
            at = variant(pd, pw, a - 1, c - 1)
            first = tap * 128 + 32
            x = jnp.concatenate(
                [
                    rim_ref[n, first : first + 32, :],
                    xs_ref[at],
                    rim_ref[n, first + 32 : first + 64, :],
                ],
                axis=0,
            )
            part = dot_nt(x, own_ref[n])
            g = part if g is None else g + part
        ones.append(strip_sum(g, 8, 32))
    twos.append(jnp.zeros((32, K), F32))
    ones.append(jnp.zeros((32, C), F32))
    twos = jnp.concatenate(twos, axis=0)
    ones = jnp.concatenate(ones, axis=0)
    twos = [twos[n * 128 : (n + 1) * 128].T for n in range(7)]
    ones = [ones[n * 128 : (n + 1) * 128].T for n in range(7)] + [jnp.zeros((C, 128), F32)] * 3
    for s in range(NX):
        for n in range(12):
            if n < 7:
                tile = twos[n][8 * s : 8 * s + 8]
            else:
                pair = ones[2 * n - 14], ones[2 * n - 13]
                tile = jnp.concatenate([x[4 * s : 4 * s + 4] for x in pair], axis=0)
            grads_ref[s * 2 + n // 6, n % 6 * 8 : n % 6 * 8 + 8, :] = tile


def act_variant(act_ref, a, c):
    pd, sd = step(0, a - 1)
    pw, sw = step(0, c - 1)
    x = act_ref[pd * 2 + pw]
    if sw:
        x = behind(x, 1)
    if sd:
        x = behind(x, 32)
    return x


def second_kernel(
    gp_ref, act_ref, k1_ref, k2_ref,
    out_ref, fcol_ref, rows_ref, og_rows_ref,
    gs_ref, t1t_ref, t2_ref,
):
    col = iota((1, 512), 1)
    half = (col >> 6) & 1
    gather_cols = from_row(
        1024, half * 512 + ((col >> 4) & 3) * 128 + (col >> 7) * 32 + 1 + (col & 15)
    )
    fcol_ref[...] = from_row(
        512,
        ((col >> 5) & 3) * 128
        + ((col >> 7) & 1) * 64
        + ((col >> 8) * 2 + (col & 1)) * 16
        + ((col & 31) >> 1),
    )
    col = col[:, 0:128]
    strided_cols = from_row(256, (col >> 4) * 32 + 1 + (col & 15))
    row = iota((256, 256), 0)
    col = iota((256, 256), 1)
    rows_ref[...] = pick(col == (row & 7) * 32 + (row >> 3))
    og_rows_ref[...] = pick(col == (row & ~31) + (row & 3) * 8 + ((row >> 2) & 7))
    build_back(k1_ref, k2_ref, t1t_ref, t2_ref)
    out = None
    for tap, (a, c) in enumerate(TAPS):
        part = dot(t2_ref[tap], act_variant(act_ref, a, c))
        out = part if out is None else out + part
    out = dot(out.astype(BF16), strided_cols)
    for s in range(NX):
        out_ref[s, 128:160, :] = jnp.concatenate(
            [out[g * 64 + 8 * s : g * 64 + 8 * s + 8] for g in range(4)], axis=0
        ).astype(BF16)
    for n, cls in enumerate(CLASSES):
        store_variants(gs_ref, gp_ref[n], cls)
    grads = [tap_sum(t1t_ref, gs_ref, conv_taps(pd, pw, -1)).astype(BF16) for pd, pw in CLASSES]
    for q in range(2):
        at = slice(q * 128, (q + 1) * 128)
        cat = jnp.concatenate(
            [grads[n][half * 128 : (half + 1) * 128, at] for half in range(2) for n in range(4)], axis=1
        )
        got = move(cat, gather_cols)
        for e in range(4):
            out_ref[4 * q + e, 0:128, :] = got[:, e * 128 : (e + 1) * 128]


def sum_kernel(r_ref, after_ref, out_ref):
    total = r_ref[0]
    for s in range(1, r_ref.shape[0]):
        total = total + r_ref[s]
    out_ref[...] = total


def pair_kernel(a_ref, b_ref, out_ref):
    total = a_ref[...] + b_ref[...]
    for n in range(out_ref.shape[0]):
        out_ref[n] = total


def append_kernel(mine_ref, other_ref, buf_ref, out_ref, two_ref):
    first = lax.rem(lax.axis_index("sy"), 2) == 0
    mine, other = mine_ref[...], other_ref[...]
    even = jnp.where(first, mine, other)
    odd = jnp.where(first, other, mine)
    total = jnp.concatenate([even, odd], axis=0)
    two_ref[...] = total[0:56]
    one = total[56:96]
    hi = one.astype(BF16).astype(F32)
    both = jnp.concatenate([hi, one - hi], axis=0).astype(BF16)
    for s in range(NX):
        out_ref[s] = both


def last_kernel(
    r_ref, g_ref, fcol_ref, rows_ref, og_rows_ref,
    strided_ref, two_ref, one_ref, vol_ref, *, out_scale, in_scale,
):
    halves = []
    for q in range(2):
        cat = jnp.concatenate([r_ref[4 * q + s, 0:128, :] for s in range(4)], axis=1)
        halves.append(move(cat, fcol_ref[...]))
    for pd in range(2):
        blocks = []
        for half in range(2):
            at = slice((pd * 2 + half) * 128, (pd * 2 + half + 1) * 128)
            blocks.append(jnp.concatenate([halves[0][:, at], halves[1][:, at]], axis=1))
        vol_ref[pd * 256 : (pd + 1) * 256, :] = move(rows_ref[...], jnp.concatenate(blocks, axis=0))
    parts = [r_ref[s, 128:160, :].astype(F32) for s in range(NX)]
    group = iota((32, 128), 1) >> 4
    blocks = []
    for e in range(8):
        block = None
        for j in range(NX):
            turned = pltpu.roll(parts[j], (j - e) * 16 % 128, 1) if j != e else parts[j]
            block = turned if block is None else jnp.where(group == j, turned, block)
        blocks.append(block)
    strided_ref[...] = move(og_rows_ref[...], jnp.concatenate(blocks, axis=0).astype(BF16))
    sums = [r_ref[s, 160:200, :].astype(F32) + r_ref[s, 200:240, :].astype(F32) for s in range(NX)]
    two = g_ref[...] * out_scale
    for n in range(7):
        one = jnp.concatenate([x[4 * n : 4 * n + 4] for x in sums], axis=0) * in_scale
        for m in range(4 * n, min(4 * n + 4, 27)):
            a, c = TAPS[m // 3]
            tap = a * 9 + m % 3 * 3 + c
            at = slice((m - 4 * n) * 32, (m - 4 * n + 1) * 32)
            one_ref[tap] = one[:, at]
            two_ref[tap] = two[n * 8 : (n + 1) * 8, at]


def call(body, outs, args, scratch=(), specs=None, out_specs=None, aliases=None, grid=(), us=1, vmem=16):
    return pl.pallas_call(
        body,
        out_shape=outs,
        grid=grid,
        in_specs=specs or [pl.BlockSpec(memory_space=pltpu.VMEM)] * len(args),
        out_specs=out_specs or jax.tree.map(lambda _: pl.BlockSpec(memory_space=pltpu.VMEM), outs),
        scratch_shapes=list(scratch),
        input_output_aliases=aliases or {},
        compiler_params=pltpu.CompilerParams(vmem_limit_bytes=vmem * 1024 * 1024),
        cost_estimate=pl.CostEstimate(flops=us * 10**9, bytes_accessed=0, transcendentals=0),
    )(*args)


def whole(*dims):
    return pl.BlockSpec(dims, lambda n: (0,) * len(dims))


def shape(*dims, dtype=BF16):
    return jax.ShapeDtypeStruct(dims, dtype)


def per_device(volume, kernel_one, bias_one, kernel_two, out_grad):
    out_scale = (8 * 128 * 128) ** (-0.5)
    in_scale = (16 * 256 * 256) ** (-0.5)
    chunks = call(
        pack_kernel,
        shape(NX, 256, 128),
        (volume.reshape(512, 256), out_grad.reshape(256, 128)),
        specs=[pl.BlockSpec(memory_space=pl.ANY)] * 2,
        scratch=(
            pltpu.VMEM((512, 256), BF16),
            pltpu.VMEM((256, 128), BF16),
            pltpu.SemaphoreType.DMA((2,)),
        ),
        vmem=60,
    )
    got = lax.all_to_all(chunks, "sx", 0, 0)
    k1 = kernel_one.transpose(2, 3, 4, 0, 1).reshape(27, C, C)
    k2 = kernel_two.transpose(2, 3, 4, 1, 0).reshape(27, C, K)
    strips, even, odd, t1h, t2th, class_cols, og_cols = call(
        weights_kernel,
        (
            shape(9, 4, 32, 256), shape(9, 2, 32, 256), shape(9, 2, 32, 128),
            shape(128, 9 * 128), shape(9, 128, 128), shape(512, 512), shape(1024, 256),
        ),
        (k1, k2),
        us=3,
    )
    bias = jnp.tile(bias_one.astype(F32), 10)[:, None]
    x, og, up, down = call(
        unpack_kernel,
        (shape(256, 1024), shape(256, 256), shape(64, 1280), shape(64, 1280)),
        (got, class_cols, og_cols),
    )
    up = lax.ppermute(up, "sy", [(i, (i + 1) % NY) for i in range(NY)])
    down = lax.ppermute(down, "sy", [((i + 1) % NY, i) for i in range(NY)])
    xs, pre, grad_act = call(
        inner_kernel,
        (shape(16, 256, 256), shape(4, 320, 256, dtype=F32), shape(4, 320, 256, dtype=F32)),
        (x, og, strips, even, odd),
        scratch=(
            pltpu.VMEM((4, 256, 256), BF16),
            pltpu.VMEM((9, 320, 256), BF16),
            pltpu.VMEM((9, 320, 256), BF16),
        ),
        us=5,
    )
    grads, gp, act = call(
        first_kernel,
        (shape(2 * NX, 48, 128, dtype=F32), shape(4, 320, 256), shape(4, 320, 256)),
        (xs, pre, grad_act, og, up, down, bias, t1h, t2th),
        scratch=(
            pltpu.VMEM((4, 9 * 128, 256), BF16),
            pltpu.VMEM((4, 128, 256), BF16),
            pltpu.VMEM((4, 256, 256), BF16),
        ),
        us=5,
    )
    grads = lax.all_to_all(
        grads,
        ("sx", "sy"),
        0,
        0,
        axis_index_groups=[
            [s * NY + 2 * q + r for s in range(NX) for r in range(2)] for q in range(NY // 2)
        ],
    )
    buffer, plane_cols, rows_back, og_rows_back = call(
        second_kernel,
        (shape(NX, 240, 128), shape(512, 512), shape(256, 256), shape(256, 256)),
        (gp, act, k1, k2),
        scratch=(
            pltpu.VMEM((16, 320, 256), BF16),
            pltpu.VMEM((9, 256, 320), BF16),
            pltpu.VMEM((9, 256, 320), BF16),
        ),
        us=6,
        vmem=20,
    )
    both = [pl.BlockSpec(memory_space=pltpu.VMEM), pl.BlockSpec(memory_space=pl.ANY)]
    keep = call(sum_kernel, shape(48, 128, dtype=F32), (grads, buffer), specs=both)
    keep = call(
        pair_kernel,
        shape(8, 48, 128, dtype=F32),
        (keep, lax.ppermute(keep, "sy", [(i, i ^ 2) for i in range(NY)])),
    )
    keep = lax.all_to_all(
        keep, "sy", 0, 0, axis_index_groups=[list(range(r, NY, 4)) for r in range(4)]
    )
    keep = call(sum_kernel, shape(48, 128, dtype=F32), (keep, buffer), specs=both)
    other = lax.ppermute(keep, "sy", [(i, i ^ 1) for i in range(NY)])
    buffer, two = call(
        append_kernel,
        (shape(NX, 240, 128), shape(56, 128, dtype=F32)),
        (keep, other, buffer),
        specs=[whole(48, 128), whole(48, 128), pl.BlockSpec(memory_space=pl.ANY)],
        out_specs=(pl.BlockSpec((NX, 80, 128), lambda n: (0, 2, 0)), whole(56, 128)),
        grid=(1,),
        aliases={2: 0},
    )
    got = lax.all_to_all(buffer, "sx", 0, 0)
    strided, two, one, vol = call(
        functools.partial(last_kernel, out_scale=out_scale, in_scale=in_scale),
        (shape(256, 128), shape(27, 8, C, dtype=F32), shape(27, C, C, dtype=F32), shape(512, 256)),
        (got, two, plane_cols, rows_back, og_rows_back),
    )
    return (
        strided.reshape(8, 8, 4, 128),
        two.reshape(3, 3, 3, 8, C).transpose(3, 4, 0, 1, 2),
        one.reshape(3, 3, 3, C, C).transpose(3, 4, 0, 1, 2),
        vol.reshape(2, C, 8, W),
    )


def solution(mesh):
    return jax.shard_map(
        per_device,
        mesh=mesh,
        in_specs=(P("sx", None, "sy", None), P(), P(), P(), P(None, "sx", "sy", None)),
        out_specs=(
            P(None, "sx", "sy", None),
            P("sx", None, None, None, None),
            P(),
            P("sx", None, "sy", None),
        ),
        check_vma=False,
    )
```

time: 97.5 us -> 84 us (0.86)
  waiting for transfers between devices: 8.38 us -> 17.6 us
  blocking collectives: 38.7 us -> 30.3 us
  starting transfers between devices: 20.2 us -> 14.8 us
  local copies, waits for them, and re-layouts: 6.37 us -> 1.59 us
  Pallas kernels: 22.2 us -> 18.3 us
    ppermute x5 -> x2, starting transfers between devices: 16.8 us -> 1.36 us  [the longest x1 1.27 us: per_device(): lax.ppermute(keep, 'sy', [(i, i ^ 2) for i in range(NY)])]
    all_to_all x0 -> x2, starting transfers between devices: none -> 10.1 us  [the longest x1 5.07 us: per_device(): lax.all_to_all(grads, ('sx', 'sy'), 0, 0, axis_index_groups=[[s * NY + 2...]
    all_to_all x0 -> x2, waiting for transfers between devices: none -> 9.89 us  [the longest x1 6.67 us: per_device(): got = lax.all_to_all(chunks, 'sx', 0, 0)]
    all_to_all x2 -> x1, blocking collectives: 27.2 us -> 17.9 us  [per_device(): lax.all_to_all(keep, 'sy', 0, 0, axis_index_groups=[list(range(r, NY, 4))...]
    unnamed x38 -> x14, local copies, waits for them, and re-layouts: 6.21 us -> 1.43 us
    pallas_call x8 -> x11, Pallas kernels: 22.2 us -> 18.3 us  [call(): pl.pallas_call(body, out_shape=outs, grid=grid, in_specs=specs or [pl.Blo...]
    ppermute x5 -> x2, waiting for transfers between devices: 8.37 us -> 5.33 us  [the longest x1 4.15 us: per_device(): lax.ppermute(keep, 'sy', [(i, i ^ 2) for i in range(NY)])]
    ppermute x1, waiting for transfers between devices: 0.01 us -> 1.6 us  [per_device(): down = lax.ppermute(down, 'sy', [((i + 1) % NY, i) for i in range(NY)])]
  transfers between devices with their start and end apart: 7 -> 6, of which waited for: 4 -> 6; matrix products, arithmetic and copies ran while one was open for 0% -> 0% of each run, Pallas kernels for 9% -> 11%
where the time goes in v2:
time: 84 us; the launch traced here: 83.4 us
  blocking collectives  30.3 us (36%)
  Pallas kernels  18.3 us (22%)
  waiting for transfers between devices  17.6 us (21%)
  starting transfers between devices  14.8 us (18%)
  local copies, waits for them, and re-layouts  1.59 us (2%)
    pallas_call x11, Pallas kernels, call(): pl.pallas_call(body, out_shape=outs, grid=grid, in_specs=specs or [pl.Blo...  18.3 us
    all_to_all x1, blocking collectives, per_device(): lax.all_to_all(keep, 'sy', 0, 0, axis_index_groups=[list(range(r, NY, 4))...  17.9 us
    all_to_all x1, blocking collectives, per_device(): got = lax.all_to_all(buffer, 'sx', 0, 0)  12.4 us
    all_to_all x1, waiting for transfers between devices, per_device(): got = lax.all_to_all(chunks, 'sx', 0, 0)  6.67 us
    all_to_all x1, starting transfers between devices, per_device(): lax.all_to_all(grads, ('sx', 'sy'), 0, 0, axis_index_groups=[[s * NY + 2...  5.07 us
    all_to_all x1, starting transfers between devices, per_device(): got = lax.all_to_all(chunks, 'sx', 0, 0)  5.03 us
    ppermute x1, waiting for transfers between devices, per_device(): lax.ppermute(keep, 'sy', [(i, i ^ 2) for i in range(NY)])  4.15 us
    ppermute x1, starting transfers between devices, per_device(): down = lax.ppermute(down, 'sy', [((i + 1) % NY, i) for i in range(NY)])  3.24 us
  transfers between devices with their start and end apart: 6, of which 6 were waited for; matrix products, arithmetic and copies ran while one was open for 0% of the time, Pallas kernels for 11%

profile of v2, /device:TPU:16, one launch (start us, length us, event | category | flops | bytes accessed | tf_op | source)
XLA Modules:
  0.0 83.4 jit_solution(447209799682982045)
XLA Ops:
  0.6 0.0 copy-start.6
  0.6 0.0 copy-start
  0.7 0.0 copy-start.1
  0.7 2.7 %shard_map.84 = bf16[8,256,128]{2,1,0:T(8,128)(2,1)} custom-call(bf16[512,256]{1,0:T(8,128)(2,1)} %bitcast.20, bf16[256,128]{1,0:T(8,128)(2,1)} %bitcast.21), custom_call_target="tpu_custom_call" | custom-call | flops 1000000000 | tf_op jit(solution)/shard_map/pallas_call | solution.py:478
  3.3 5.0 %all-to-all-start = ((bf16[8,256,128]{2,1,0:T(8,128)(2,1)}), bf16[8,256,128]{2,1,0:T(8,128)(2,1)S(1)}, u32[]{:S(2)}, u32[]{:S(2)}) async-start(bf16[8,256,128]{2,1,0:T(8,128)(2,1)} %shard_map.84), calls=%async_computation | async-start | bytes 1048576 | tf_op jit(solution)/shard_map/all_to_all | solution.py:514
  8.4 0.0 copy-done.6
  8.4 0.2 broadcast_in_dim_tile.4.bias_ref
  8.5 0.0 copy-done
  8.6 0.0 copy-done.1
  8.6 1.2 %shard_map.85 = (bf16[9,4,32,256]{3,2,1,0:T(8,128)(2,1)S(1)}, bf16[9,2,32,256]{3,2,1,0:T(8,128)(2,1)S(1)}, bf16[9,2,32,128]{3,2,1,0:T(8,128)(2,1)S(1)}, bf16[128...) custom-call(bf16[27,32,32]{2,1,0:T(8,128)(2,1)S(1)} %bitcast.16, ...), custom_call_target="tpu_custom_call" | custom-call | flops 3000000000 | tf_op jit(solution)/shard_map/pallas_call | solution.py:478
  9.8 0.0 copy-start.2
  9.8 0.7 copy-done.2
  10.5 0.0 copy-start.4
  10.5 0.7 copy-done.4
  11.2 6.7 %all-to-all-done.r_ref = bf16[8,256,128]{2,1,0:T(8,128)(2,1)S(1)} async-done(((bf16[8,256,128]{2,1,0:T(8,128)(2,1)}), bf16[8,256,128]{2,1,0:T(8,128)(2,1)S(1)}, u32[]{:S(2)}, u32[]{:S(2)}) %all-to-all-start) | async-done | bytes 524320 | tf_op jit(solution)/shard_map/all_to_all | solution.py:514
  17.8 0.6 shard_map.86
  18.4 0.1 collective-permute-start
  18.5 3.2 %collective-permute-start.1 = (bf16[64,1280]{1,0:T(8,128)(2,1)S(1)}, bf16[64,1280]{1,0:T(8,128)(2,1)S(1)}, u32[]{:S(2)}, u32[]{:S(2)}) collective-permute-start(bf16[64,1280]{1,0:T(8,128)(2,1)S(1)} %get-tuple-element.42), channel_id=1, source_target_pairs={{1,0},{2,1},{3,2},{4,3},{5,4},{6,5},{7,6},{8,7},{9,8},{10,9},{11,1... | collective-permute-start | bytes 491528 | tf_op jit(solution)/shard_map/ppermute | solution.py:533
  21.7 0.0 copy-start.3
  21.7 0.0 copy-start.5
  21.7 2.2 %shard_map.87 = (bf16[16,256,256]{2,1,0:T(8,128)(2,1)S(1)}, f32[4,320,256]{2,1,0:T(8,128)S(1)}, f32[4,320,256]{2,1,0:T(8,128)S(1)}) custom-call(bf16[256,1024]{1,0:T(8,128)(2,1)S(1)} %get-tuple-element.33.x_ref, bf16[256,256]{1,0:T(8,128)(2,1)S(1)} %get-tuple-element.34.og_ref, bf16[9,4,32,256]{3,2,1,0:T(8,128)(2,1)S(1)} %get-tuple-element.35.strips_ref, ...), custom_call_target="tpu_custom_call" | custom-call | flops 5000000000 | tf_op jit(solution)/shard_map/pallas_call | solution.py:478
  23.9 0.8 collective-permute-done.up_ref
  24.7 1.6 %collective-permute-done.1.down_ref = bf16[64,1280]{1,0:T(8,128)(2,1)S(1)} collective-permute-done((bf16[64,1280]{1,0:T(8,128)(2,1)S(1)}, bf16[64,1280]{1,0:T(8,128)(2,1)S(1)}, u32[]{:S(2)}, u32[]{:S(2)}) %collective-permute-start.1) | collective-permute-done | bytes 163872 | tf_op jit(solution)/shard_map/ppermute | solution.py:533
  26.3 0.0 copy-done.3
  26.3 0.0 copy-done.5
  26.3 4.3 %shard_map.88 = (f32[16,48,128]{2,1,0:T(8,128)}, bf16[4,320,256]{2,1,0:T(8,128)(2,1)S(1)}, bf16[4,320,256]{2,1,0:T(8,128)(2,1)S(1)}) custom-call(bf16[16,256,256]{2,1,0:T(8,128)(2,1)S(1)} %get-tuple-element.38.xs_ref, f32[4,320,256]{2,1,0:T(8,128)S(1)} %get-tuple-element.39.pre_ref, f32[4,320,256]{2,1,0:T(8,128)S(1)} %get-tuple-element.40.ga_ref, ...), custom_call_target="tpu_custom_call" | custom-call | flops 5000000000 | tf_op jit(solution)/shard_map/pallas_call | solution.py:478
  30.6 5.1 %all-to-all-start.1 = ((f32[16,48,128]{2,1,0:T(8,128)}), f32[16,48,128]{2,1,0:T(8,128)S(1)}, u32[]{:S(2)}, u32[]{:S(2)}) async-start(f32[16,48,128]{2,1,0:T(8,128)} %get-tuple-element.45), calls=%async_computation.1 | async-start | bytes 786432 | tf_op jit(solution)/shard_map/all_to_all | solution.py:556
  35.7 6.0 %shard_map.89 = (bf16[8,240,128]{2,1,0:T(8,128)(2,1)S(1)}, bf16[512,512]{1,0:T(8,128)(2,1)S(1)}, bf16[256,256]{1,0:T(8,128)(2,1)S(1)}, bf16[256,256]{1,0:T(8,128)(2,1)S(1)}) custom-call(bf16[4,320,256]{2,1,0:T(8,128)(2,1)S(1)} %get-tuple-element.46.gp_ref, bf16[4,320,256]{2,1,0:T(8,128)(2,1)S(1)} %get-tuple-element.47.act_ref, ...), custom_call_target="tpu_custom_call" | custom-call | flops 6000000000 | tf_op jit(solution)/shard_map/pallas_call | solution.py:478
  41.7 3.2 %all-to-all-done.1.r_ref = f32[16,48,128]{2,1,0:T(8,128)S(1)} async-done(((f32[16,48,128]{2,1,0:T(8,128)}), f32[16,48,128]{2,1,0:T(8,128)S(1)}, u32[]{:S(2)}, u32[]{:S(2)}) %all-to-all-start.1) | async-done | bytes 393248 | tf_op jit(solution)/shard_map/all_to_all | solution.py:556
  44.9 1.3 %collective-permute-start.2 = (f32[48,128]{1,0:T(8,128)S(1)}, f32[48,128]{1,0:T(8,128)S(1)}, u32[]{:S(2)}, u32[]{:S(2)}) collective-permute-start(f32[48,128]{1,0:T(8,128)S(1)} %shard_map.90.a_ref), channel_id=1, source_target_pairs={{0,2},{1,3},{2,0},{3,1},{4,6},{5,7},{6,4},{7,5},{8,10},{9,11},{10,... | collective-permute-start | bytes 73736 | tf_op jit(solution)/shard_map/ppermute | solution.py:582
  46.2 4.2 %collective-permute-done.2.b_ref = f32[48,128]{1,0:T(8,128)S(1)} collective-permute-done((f32[48,128]{1,0:T(8,128)S(1)}, f32[48,128]{1,0:T(8,128)S(1)}, u32[]{:S(2)}, u32[]{:S(2)}) %collective-permute-start.2) | collective-permute-done | bytes 24608 | tf_op jit(solution)/shard_map/ppermute | solution.py:582
  50.4 17.9 %all_to_all.20.r_ref = f32[8,48,128]{2,1,0:T(8,128)S(1)} all-to-all(f32[8,48,128]{2,1,0:T(8,128)S(1)} %shard_map.91), channel_id=1, replica_groups={{0,4,8,12,16,20,24,28},{1,5,9,13,17,21,25,29},{2,6,10,14,18,22,26,30},{..., dimensions={0} | all-to-all | bytes 393216 | tf_op jit(solution)/shard_map/all_to_all | solution.py:584
  68.3 0.1 collective-permute-start.3
  68.4 1.2 %collective-permute-done.3.other_ref = f32[48,128]{1,0:T(8,128)S(1)} collective-permute-done((f32[48,128]{1,0:T(8,128)S(1)}, f32[48,128]{1,0:T(8,128)S(1)}, u32[]{:S(2)}, u32[]{:S(2)}) %collective-permute-start.3) | collective-permute-done | bytes 24608 | tf_op jit(solution)/shard_map/ppermute | solution.py:588
  69.6 12.4 %all_to_all.21.r_ref = bf16[8,240,128]{2,1,0:T(8,128)(2,1)S(1)} all-to-all(bf16[8,240,128]{2,1,0:T(8,128)(2,1)S(1)} %get-tuple-element.49), channel_id=1, replica_groups=mesh['sx'=8,'sy'=32] {'sx'}, dimensions={0} | all-to-all | bytes 983040 | tf_op jit(solution)/shard_map/all_to_all | solution.py:598
  82.1 1.4 %shard_map.94 = (bf16[256,128]{1,0:T(8,128)(2,1)}, f32[27,8,32]{2,1,0:T(8,128)}, f32[27,32,32]{2,1,0:T(8,128)}, bf16[512,256]{1,0:T(8,128)(2,1)}) custom-call(bf16[8,240,128]{2,1,0:T(8,128)(2,1)S(1)} %all_to_all.21.r_ref, f32[56,128]{1,0:T(8,128)S(1)} %get-tuple-element.50.g_ref, bf16[512,512]{1,0:T(8,128)(2,1)S(1)} %get-tuple-element.51.fcol_ref, ...), custom_call_target="tpu_custom_call" | custom-call | flops 1000000000 | tf_op jit(solution)/shard_map/pallas_call | solution.py:478
  (5 shorter events, 0.1 us)
Async XLA Ops:
  0.6 7.7 %copy-start.6 = (bf16[32]{0:T(256)(128)(2,1)S(1)}, bf16[32]{0:T(256)(128)(2,1)}, u32[]{:S(2)}) copy-start(bf16[32]{0:T(256)(128)(2,1)} %param.7) | copy-start | bytes 196
  0.6 7.9 %copy-start = (bf16[32,32,3,3,3]{1,0,4,3,2:T(8,128)(2,1)S(1)}, bf16[32,32,3,3,3]{1,0,4,3,2:T(8,128)(2,1)}, u32[]{:S(2)}) copy-start(bf16[32,32,3,3,3]{1,0,4,3,2:T(8,128)(2,1)} %param.6) | copy-start | bytes 165892
  0.7 7.9 %copy-start.1 = (bf16[64,32,3,3,3]{0,1,4,3,2:T(8,128)(2,1)S(1)}, bf16[64,32,3,3,3]{0,1,4,3,2:T(8,128)(2,1)}, u32[]{:S(2)}) copy-start(bf16[64,32,3,3,3]{0,1,4,3,2:T(8,128)(2,1)} %param.8) | copy-start | bytes 331780
  3.3 14.5 %all-to-all-start = ((bf16[8,256,128]{2,1,0:T(8,128)(2,1)}), bf16[8,256,128]{2,1,0:T(8,128)(2,1)S(1)}, u32[]{:S(2)}, u32[]{:S(2)}) async-start(bf16[8,256,128]{2,1,0:T(8,128)(2,1)} %shard_map.84), calls=%async_computation | async-start | bytes 1048576 | tf_op jit(solution)/shard_map/all_to_all | solution.py:514
  9.8 0.7 copy-start.2
  10.5 0.7 copy-start.4
  18.4 6.3 %collective-permute-start = (bf16[64,1280]{1,0:T(8,128)(2,1)S(1)}, bf16[64,1280]{1,0:T(8,128)(2,1)S(1)}, u32[]{:S(2)}, u32[]{:S(2)}) collective-permute-start(bf16[64,1280]{1,0:T(8,128)(2,1)S(1)} %get-tuple-element.41), channel_id=1, source_target_pairs={{0,1},{1,2},{2,3},{3,4},{4,5},{5,6},{6,7},{7,8},{8,9},{9,10},{10,1... | collective-permute-start | bytes 491528 | tf_op jit(solution)/shard_map/ppermute | solution.py:532
  18.5 7.8 %collective-permute-start.1 = (bf16[64,1280]{1,0:T(8,128)(2,1)S(1)}, bf16[64,1280]{1,0:T(8,128)(2,1)S(1)}, u32[]{:S(2)}, u32[]{:S(2)}) collective-permute-start(bf16[64,1280]{1,0:T(8,128)(2,1)S(1)} %get-tuple-element.42), channel_id=1, source_target_pairs={{1,0},{2,1},{3,2},{4,3},{5,4},{6,5},{7,6},{8,7},{9,8},{10,9},{11,1... | collective-permute-start | bytes 491528 | tf_op jit(solution)/shard_map/ppermute | solution.py:533
  21.7 4.6 %copy-start.3 = (bf16[128,1152]{1,0:T(8,128)(2,1)S(1)}, bf16[128,1152]{1,0:T(8,128)(2,1)}, u32[]{:S(2)}) copy-start(bf16[128,1152]{1,0:T(8,128)(2,1)} %copy-done.2) | copy-start | bytes 884740
  21.7 4.6 %copy-start.5 = (bf16[9,128,128]{2,1,0:T(8,128)(2,1)S(1)}, bf16[9,128,128]{2,1,0:T(8,128)(2,1)}, u32[]{:S(2)}) copy-start(bf16[9,128,128]{2,1,0:T(8,128)(2,1)} %copy-done.4) | copy-start | bytes 884740
  30.6 14.3 %all-to-all-start.1 = ((f32[16,48,128]{2,1,0:T(8,128)}), f32[16,48,128]{2,1,0:T(8,128)S(1)}, u32[]{:S(2)}, u32[]{:S(2)}) async-start(f32[16,48,128]{2,1,0:T(8,128)} %get-tuple-element.45), calls=%async_computation.1 | async-start | bytes 786432 | tf_op jit(solution)/shard_map/all_to_all | solution.py:556
  44.9 5.4 %collective-permute-start.2 = (f32[48,128]{1,0:T(8,128)S(1)}, f32[48,128]{1,0:T(8,128)S(1)}, u32[]{:S(2)}, u32[]{:S(2)}) collective-permute-start(f32[48,128]{1,0:T(8,128)S(1)} %shard_map.90.a_ref), channel_id=1, source_target_pairs={{0,2},{1,3},{2,0},{3,1},{4,6},{5,7},{6,4},{7,5},{8,10},{9,11},{10,... | collective-permute-start | bytes 73736 | tf_op jit(solution)/shard_map/ppermute | solution.py:582
  68.3 1.3 %collective-permute-start.3 = (f32[48,128]{1,0:T(8,128)S(1)}, f32[48,128]{1,0:T(8,128)S(1)}, u32[]{:S(2)}, u32[]{:S(2)}) collective-permute-start(f32[48,128]{1,0:T(8,128)S(1)} %shard_map.92.mine_ref), channel_id=1, source_target_pairs={{0,1},{1,0},{2,3},{3,2},{4,5},{5,4},{6,7},{7,6},{8,9},{9,8},{10,11... | collective-permute-start | bytes 73736 | tf_op jit(solution)/shard_map/ppermute | solution.py:588

commit v3 on v2

--- a/solution.py
+++ b/solution.py
@@ -70,7 +70,7 @@
         ref[base + n] = form
 
 
-def pack_kernel(vol_hbm, og_hbm, out_ref, vol_ref, og_ref, sems):
+def pack_kernel(vol_hbm, og_hbm, out_hbm, vol_ref, og_ref, out_ref, sems):
     copies = (
         pltpu.make_async_copy(vol_hbm, vol_ref, sems.at[0]),
         pltpu.make_async_copy(og_hbm, og_ref, sems.at[1]),
@@ -80,7 +80,7 @@
     row = iota((256, 256), 0)
     col = iota((256, 256), 1)
     by_row = pick(col == (row & 31) * 8 + (row >> 5))
-    by_kind = pick(col == (row & ~31) + (row & 7) * 4 + ((row >> 3) & 3))
+    by_kind = pick(col == ((row >> 3) & 7) * 32 + (row & 7) * 4 + (row >> 6))
     lane = iota((1, 128), 1)
     cls = jnp.where(lane >= 20, 1, 0) + jnp.where(lane >= 40, 1, 0) + jnp.where(lane >= 60, 1, 0)
     u = lane - 20 * cls
@@ -108,28 +108,36 @@
             [planes[n][:, block * 128 : (block + 1) * 128] for n, block, _ in chosen[j]], axis=1
         )
         out_ref[j] = move(cat, jnp.concatenate([m for _, _, m in chosen[j]], axis=0))
-
-
-def unpack_kernel(r_ref, cls_ref, og_cols_ref, x_ref, og_ref, up_ref, down_ref):
-    for q in range(2):
-        cat = jnp.concatenate([r_ref[4 * q + s] for s in range(4)], axis=1)
-        got = move(cat, cls_ref[...])
-        for cls in range(4):
-            at = slice(cls * 256 + q * 128, cls * 256 + (q + 1) * 128)
-            part = got[:, cls * 128 : (cls + 1) * 128]
-            x_ref[:, at] = part
-            up_ref[:, at] = part[192:256]
-            down_ref[:, at] = part[0:64]
-    parts = []
+        copies += (pltpu.make_async_copy(out_ref.at[j], out_hbm.at[j], sems.at[2 + j]),)
+        copies[-1].start()
+    for copy in copies[2:]:
+        copy.wait()
+
+
+def split_kernel(r_ref, cross_ref, pair_ref):
+    even = lax.rem(lax.axis_index("sy"), 2) == 0
     for s in range(NX):
-        parts.append(jnp.concatenate([r_ref[s, e * 32 : (e + 1) * 32, :] for e in range(8)], axis=1))
-    og = dot(jnp.concatenate(parts, axis=0), og_cols_ref[...])
-    og = jnp.concatenate(
-        [og[s * 32 + g * 8 : s * 32 + g * 8 + 8] for g in range(4) for s in range(NX)], axis=0
-    ).astype(BF16)
-    og_ref[...] = og
-    up_ref[:, 1024:1280] = og[192:256]
-    down_ref[:, 1024:1280] = og[0:64]
+        top, bottom = r_ref[s, 0:64, :], r_ref[s, 192:256, :]
+        cross_ref[s] = jnp.where(even, top, bottom)
+        pair_ref[s] = jnp.where(even, bottom, top)
+
+
+def by_class(parts, cls_cols):
+    got = [move(jnp.concatenate(parts[4 * q : 4 * q + 4], axis=1), cls_cols) for q in range(2)]
+    return [
+        jnp.concatenate([x[:, n * 128 : (n + 1) * 128] for x in got], axis=1) for n in range(4)
+    ]
+
+
+def cotangents(parts, groups, og_cols):
+    parts = [x.astype(F32) for x in parts]
+    cat = [
+        jnp.concatenate(
+            [x[g * 64 + e * 8 : g * 64 + e * 8 + 8] for g in range(groups) for x in parts], axis=0
+        )
+        for e in range(8)
+    ]
+    return move(jnp.concatenate(cat, axis=1).astype(BF16), og_cols)
 
 
 def place(strip, offset, width):
@@ -156,15 +164,13 @@
 
 
 def weights_kernel(
-    k1_ref, k2_ref, strips_ref, even_ref, odd_ref, t1h_ref, t2th_ref, cls_ref, og_cols_ref
+    k1_ref, k2_ref, strips_ref, even_ref, odd_ref, cls_ref, og_cols_ref
 ):
     col = iota((1, 512), 1)
     u = col & 31
     cls_ref[...] = from_row(512, jnp.where(u < 18, ((col >> 5) & 3) * 128 + (col >> 7) * 20 + u, -1))
     col, u = col[:, 0:256], u[:, 0:256]
     og_cols_ref[...] = from_row(1024, jnp.where(u < 18, (col >> 5) * 128 + 80 + u, -1))
-    gap = jnp.zeros((C, C), F32)
-    wide = jnp.zeros((C, K), F32)
     for t, (a, c) in enumerate(TAPS):
         k1 = kernel_blocks(k1_ref, a, c)
         k2 = kernel_blocks(k2_ref, a, c)
@@ -175,6 +181,14 @@
         for r in range(2):
             even_ref[t, r] = place(even, 64 * r, 256).astype(BF16)
             odd_ref[t, r] = place(k2[1], 64 * r, 128).astype(BF16)
+
+
+def rim_kernel(k1_ref, k2_ref, t1h_ref, t2th_ref):
+    gap = jnp.zeros((C, C), F32)
+    wide = jnp.zeros((C, K), F32)
+    for t, (a, c) in enumerate(TAPS):
+        k1 = kernel_blocks(k1_ref, a, c)
+        k2 = kernel_blocks(k2_ref, a, c)
         rim = (
             (k1[0], k1[1], gap, gap),
             (gap, k1[0], gap, gap),
@@ -257,13 +271,15 @@
 
 
 def inner_kernel(
-    x_ref, og_ref, strips_ref, even_ref, odd_ref,
-    xs_ref, pre_ref, grad_ref,
+    r_ref, cls_ref, og_cols_ref, strips_ref, even_ref, odd_ref,
+    og_ref, xs_ref, pre_ref, grad_ref,
     ogs_ref, t1_ref, t2t_ref,
 ):
     build_forward(strips_ref, even_ref, odd_ref, t1_ref, t2t_ref)
-    for n, cls in enumerate(CLASSES):
-        store_variants(xs_ref, x_ref[:, n * 256 : (n + 1) * 256], cls)
+    parts = [r_ref[s] for s in range(NX)]
+    for x, cls in zip(by_class(parts, cls_ref[...]), CLASSES):
+        store_variants(xs_ref, x, cls)
+    og_ref[...] = cotangents(parts, 4, og_cols_ref[...])
     store_cotangents(ogs_ref, og_ref[...])
     for n, (pd, pw) in enumerate(CLASSES):
         pre_ref[n] = tap_sum(t1_ref, xs_ref, conv_taps(pd, pw, 1))
@@ -271,7 +287,8 @@
 
 
 def first_kernel(
-    xs_ref, pre_ref, ga_ref, og_ref, up_ref, down_ref, bias_ref, t1h_ref, t2th_ref,
+    xs_ref, pre_ref, ga_ref, og_ref, cross_ref, pair_ref, cls_ref, og_cols_ref, bias_ref, t1h_ref,
+    t2th_ref,
     grads_ref, gp_ref, act_ref,
     rim_ref, ogs_ref, own_ref,
 ):
@@ -279,22 +296,22 @@
     t = lax.axis_index("sy")
     low = t > 0
     high = t < NY - 1
-    none = jnp.zeros((64, 256), BF16)
-
-    def rim(at):
-        return jnp.concatenate(
-            [jnp.where(low, up_ref[:, at], none), jnp.where(high, down_ref[:, at], none)], axis=0
-        )
-
+    even = lax.rem(t, 2) == 0
+    none = jnp.zeros((64, 128), BF16)
+    ups = [jnp.where(even, cross_ref[s], pair_ref[s]) for s in range(NX)]
+    downs = [jnp.where(even, pair_ref[s], cross_ref[s]) for s in range(NX)]
+    ups = [jnp.where(low, x, none) for x in ups]
+    downs = [jnp.where(high, x, none) for x in downs]
+    rims = [jnp.concatenate([x, y], axis=0) for x, y in zip(ups, downs)]
     uses = [
         (n, tap, at) for n, (pd, pw) in enumerate(CLASSES) for tap, at in conv_taps(pd, pw, 1)
     ]
-    for n, cls in enumerate(CLASSES):
-        forms = variants(rim(slice(n * 256, (n + 1) * 256)), cls)
+    for n, x in enumerate(by_class(rims, cls_ref[...])):
+        forms = variants(x, CLASSES[n])
         for m, tap, at in uses:
             if at // 4 == n:
                 rim_ref[m, tap * 128 : (tap + 1) * 128, :] = forms[at % 4]
-    store_cotangents(ogs_ref, rim(slice(1024, 1280)))
+    store_cotangents(ogs_ref, cotangents(rims, 2, og_cols_ref[...]))
 
     def with_rim(inner, outer):
         return jnp.concatenate(
@@ -504,37 +521,40 @@
         shape(NX, 256, 128),
         (volume.reshape(512, 256), out_grad.reshape(256, 128)),
         specs=[pl.BlockSpec(memory_space=pl.ANY)] * 2,
+        out_specs=pl.BlockSpec(memory_space=pl.ANY),
         scratch=(
             pltpu.VMEM((512, 256), BF16),
             pltpu.VMEM((256, 128), BF16),
-            pltpu.SemaphoreType.DMA((2,)),
+            pltpu.VMEM((NX, 256, 128), BF16),
+            pltpu.SemaphoreType.DMA((2 + NX,)),
         ),
         vmem=60,
     )
     got = lax.all_to_all(chunks, "sx", 0, 0)
     k1 = kernel_one.transpose(2, 3, 4, 0, 1).reshape(27, C, C)
     k2 = kernel_two.transpose(2, 3, 4, 1, 0).reshape(27, C, K)
-    strips, even, odd, t1h, t2th, class_cols, og_cols = call(
+    strips, even, odd, class_cols, og_cols = call(
         weights_kernel,
         (
             shape(9, 4, 32, 256), shape(9, 2, 32, 256), shape(9, 2, 32, 128),
-            shape(128, 9 * 128), shape(9, 128, 128), shape(512, 512), shape(1024, 256),
+            shape(512, 512), shape(1024, 256),
         ),
         (k1, k2),
         us=3,
     )
     bias = jnp.tile(bias_one.astype(F32), 10)[:, None]
-    x, og, up, down = call(
-        unpack_kernel,
-        (shape(256, 1024), shape(256, 256), shape(64, 1280), shape(64, 1280)),
-        (got, class_cols, og_cols),
-    )
-    up = lax.ppermute(up, "sy", [(i, (i + 1) % NY) for i in range(NY)])
-    down = lax.ppermute(down, "sy", [((i + 1) % NY, i) for i in range(NY)])
-    xs, pre, grad_act = call(
+    cross, pair = call(split_kernel, (shape(NX, 64, 128), shape(NX, 64, 128)), (got,))
+    k1, k2, cross = lax.optimization_barrier((k1, k2, cross))
+    t1h, t2th = call(rim_kernel, (shape(128, 9 * 128), shape(9, 128, 128)), (k1, k2))
+    ends = (0, NY - 1)
+    cross = lax.ppermute(
+        cross, "sy", [(i, i if i in ends else ((i - 1) ^ 1) + 1) for i in range(NY)]
+    )
+    pair = lax.ppermute(pair, "sy", [(i, i ^ 1) for i in range(NY)])
+    og, xs, pre, grad_act = call(
         inner_kernel,
-        (shape(16, 256, 256), shape(4, 320, 256, dtype=F32), shape(4, 320, 256, dtype=F32)),
-        (x, og, strips, even, odd),
+        (shape(256, 256), shape(16, 256, 256), shape(4, 320, 256, dtype=F32), shape(4, 320, 256, dtype=F32)),
+        (got, class_cols, og_cols, strips, even, odd),
         scratch=(
             pltpu.VMEM((4, 256, 256), BF16),
             pltpu.VMEM((9, 320, 256), BF16),
@@ -545,7 +565,7 @@
     grads, gp, act = call(
         first_kernel,
         (shape(2 * NX, 48, 128, dtype=F32), shape(4, 320, 256), shape(4, 320, 256)),
-        (xs, pre, grad_act, og, up, down, bias, t1h, t2th),
+        (xs, pre, grad_act, og, cross, pair, class_cols, og_cols, bias, t1h, t2th),
         scratch=(
             pltpu.VMEM((4, 9 * 128, 256), BF16),
             pltpu.VMEM((4, 128, 256), BF16),
@@ -582,7 +602,7 @@
         (keep, lax.ppermute(keep, "sy", [(i, i ^ 2) for i in range(NY)])),
     )
     keep = lax.all_to_all(
-        keep, "sy", 0, 0, axis_index_groups=[list(range(r, NY, 4)) for r in range(4)]
+        keep, "sy", 0, 0, axis_index_groups=[[4 * z + r for z in (0, 4, 2, 6, 1, 5, 3, 7)] for r in range(4)]
     )
     keep = call(sum_kernel, shape(48, 128, dtype=F32), (keep, buffer), specs=both)
     other = lax.ppermute(keep, "sy", [(i, i ^ 1) for i in range(NY)])

time: 84 us -> 82.8 us (0.986); the launches traced: 83.4 us -> 81.1 us
  waiting for transfers between devices: 17.6 us -> 19.4 us
  blocking collectives: 30.3 us -> 28.8 us
  local copies, waits for them, and re-layouts: 1.59 us -> 0.19 us
  starting transfers between devices: 14.8 us -> 13.5 us
    all_to_all x1, waiting for transfers between devices: 6.67 us -> 8.28 us  [per_device(): got = lax.all_to_all(chunks, 'sx', 0, 0)]
    all_to_all x1, blocking collectives: 17.9 us -> 16.4 us  [per_device(): lax.all_to_all(keep, 'sy', 0, 0, axis_index_groups=[[4 * z + r for z in (...]
    unnamed x14, local copies, waits for them, and re-layouts: 1.43 us -> 0.03 us
    all_to_all x1, starting transfers between devices: 5.07 us -> 3.73 us  [per_device(): lax.all_to_all(grads, ('sx', 'sy'), 0, 0, axis_index_groups=[[s * NY + 2...]
    pallas_call x11 -> x12, Pallas kernels: 18.3 us -> 18.4 us  [call(): pl.pallas_call(body, out_shape=outs, grid=grid, in_specs=specs or [pl.Blo...]
  transfers between devices with their start and end apart: 6 -> 6, of which waited for: 6 -> 5; matrix products, arithmetic and copies ran while one was open for 0% -> 0% of each run, Pallas kernels for 11% -> 12%
where the time goes in v3:
time: 82.8 us; the launch traced here: 81.1 us
  blocking collectives  28.8 us (35%)
  waiting for transfers between devices  19.4 us (23%)
  Pallas kernels  18.4 us (22%)
  starting transfers between devices  13.5 us (16%)
    pallas_call x12, Pallas kernels, call(): pl.pallas_call(body, out_shape=outs, grid=grid, in_specs=specs or [pl.Blo...  18.4 us
    all_to_all x1, blocking collectives, per_device(): lax.all_to_all(keep, 'sy', 0, 0, axis_index_groups=[[4 * z + r for z in (...  16.4 us
    all_to_all x1, blocking collectives, per_device(): got = lax.all_to_all(buffer, 'sx', 0, 0)  12.4 us
    all_to_all x1, waiting for transfers between devices, per_device(): got = lax.all_to_all(chunks, 'sx', 0, 0)  8.28 us
    all_to_all x1, starting transfers between devices, per_device(): got = lax.all_to_all(chunks, 'sx', 0, 0)  5.03 us
    ppermute x1, waiting for transfers between devices, per_device(): lax.ppermute(keep, 'sy', [(i, i ^ 2) for i in range(NY)])  4.85 us
    all_to_all x1, starting transfers between devices, per_device(): lax.all_to_all(grads, ('sx', 'sy'), 0, 0, axis_index_groups=[[s * NY + 2...  3.73 us
    all_to_all x1, waiting for transfers between devices, per_device(): lax.all_to_all(grads, ('sx', 'sy'), 0, 0, axis_index_groups=[[s * NY + 2...  3.05 us
  transfers between devices with their start and end apart: 6, of which 5 were waited for; matrix products, arithmetic and copies ran while one was open for 0% of the time, Pallas kernels for 12%

profile of v3, /device:TPU:16, one launch (start us, length us, event | category | flops | bytes accessed | tf_op | source)
XLA Modules:
  0.0 81.1 jit_solution(10721401115599832940)
XLA Ops:
  0.6 0.0 copy-start.6
  0.6 0.0 copy-start
  0.7 0.0 copy-start.1
  0.7 2.6 %shard_map.84 = bf16[8,256,128]{2,1,0:T(8,128)(2,1)} custom-call(bf16[512,256]{1,0:T(8,128)(2,1)} %bitcast.22, bf16[256,128]{1,0:T(8,128)(2,1)} %bitcast.23), custom_call_target="tpu_custom_call" | custom-call | flops 1000000000 | tf_op jit(solution)/shard_map/pallas_call | solution.py:495
  3.2 5.0 %all-to-all-start = ((bf16[8,256,128]{2,1,0:T(8,128)(2,1)}), bf16[8,256,128]{2,1,0:T(8,128)(2,1)S(1)}, u32[]{:S(2)}, u32[]{:S(2)}) async-start(bf16[8,256,128]{2,1,0:T(8,128)(2,1)} %shard_map.84), calls=%async_computation | async-start | bytes 1048576 | tf_op jit(solution)/shard_map/all_to_all | solution.py:533
  8.3 0.0 copy-done.6
  8.3 0.2 broadcast_in_dim_tile.4.bias_ref
  8.4 0.0 copy-done
  8.5 0.0 copy-done.1
  8.5 1.0 %shard_map.85 = (bf16[9,4,32,256]{3,2,1,0:T(8,128)(2,1)S(1)}, bf16[9,2,32,256]{3,2,1,0:T(8,128)(2,1)S(1)}, bf16[9,2,32,128]{3,2,1,0:T(8,128)(2,1)S(1)}, bf16[512...) custom-call(bf16[27,32,32]{2,1,0:T(8,128)(2,1)S(1)} %bitcast.16, bf16[27,32,64]{2,1,0:T(8,128)(2,1)S(1)} %bitcast.19), custom_call_target="tpu_custom_call" | custom-call | flops 3000000000 | tf_op jit(solution)/shard_map/pallas_call | solution.py:495
  9.4 0.0 copy-start.2
  9.4 0.0 copy-start.4
  9.5 8.3 %all-to-all-done.r_ref = bf16[8,256,128]{2,1,0:T(8,128)(2,1)S(1)} async-done(((bf16[8,256,128]{2,1,0:T(8,128)(2,1)}), bf16[8,256,128]{2,1,0:T(8,128)(2,1)S(1)}, u32[]{:S(2)}, u32[]{:S(2)}) %all-to-all-start) | async-done | bytes 524320 | tf_op jit(solution)/shard_map/all_to_all | solution.py:533
  17.7 0.1 shard_map.87
  17.8 1.9 %collective-permute-start = (bf16[8,64,128]{2,1,0:T(8,128)(2,1)S(1)}, bf16[8,64,128]{2,1,0:T(8,128)(2,1)S(1)}, u32[]{:S(2)}, u32[]{:S(2)}) collective-permute-start(bf16[8,64,128]{2,1,0:T(8,128)(2,1)S(1)} %get-tuple-element.43), channel_id=1, source_target_pairs={{0,0},{1,2},{2,1},{3,4},{4,3},{5,6},{6,5},{7,8},{8,7},{9,10},{10,9... | collective-permute-start | bytes 393224 | tf_op jit(solution)/shard_map/ppermute | solution.py:550
  19.7 2.2 %collective-permute-start.1 = (bf16[8,64,128]{2,1,0:T(8,128)(2,1)S(1)}, bf16[8,64,128]{2,1,0:T(8,128)(2,1)S(1)}, u32[]{:S(2)}, u32[]{:S(2)}) collective-permute-start(bf16[8,64,128]{2,1,0:T(8,128)(2,1)S(1)} %get-tuple-element.44), channel_id=1, source_target_pairs={{0,1},{1,0},{2,3},{3,2},{4,5},{5,4},{6,7},{7,6},{8,9},{9,8},{10,11... | collective-permute-start | bytes 393224 | tf_op jit(solution)/shard_map/ppermute | solution.py:553
  21.9 0.0 copy-done.2
  21.9 0.0 copy-done.4
  21.9 2.7 %shard_map.86 = (bf16[256,256]{1,0:T(8,128)(2,1)S(1)}, bf16[16,256,256]{2,1,0:T(8,128)(2,1)S(1)}, f32[4,320,256]{2,1,0:T(8,128)S(1)}, f32[4,320,256]{2,1,0:T(8,128)S(1)}) custom-call(bf16[8,256,128]{2,1,0:T(8,128)(2,1)S(1)} %all-to-all-done.r_ref, bf16[512,512]{1,0:T(8,128)(2,1)S(1)} %get-tuple-element.33.cls_ref, ...), custom_call_target="tpu_custom_call" | custom-call | flops 5000000000 | tf_op jit(solution)/shard_map/pallas_call | solution.py:495
  24.6 0.0 copy-start.3
  24.6 0.0 copy-start.5
  24.6 0.2 shard_map.88
  24.8 2.0 %collective-permute-done.cross_ref = bf16[8,64,128]{2,1,0:T(8,128)(2,1)S(1)} collective-permute-done((bf16[8,64,128]{2,1,0:T(8,128)(2,1)S(1)}, bf16[8,64,128]{2,1,0:T(8,128)(2,1)S(1)}, u32[]{:S(2)}, u32[]{:S(2)}) %collective-permute-start) | collective-permute-done | bytes 131104 | tf_op jit(solution)/shard_map/ppermute | solution.py:550
  26.8 0.0 collective-permute-done.1.pair_ref
  26.8 0.0 copy-done.3
  26.8 0.0 copy-done.5
  26.9 4.5 %shard_map.89 = (f32[16,48,128]{2,1,0:T(8,128)}, bf16[4,320,256]{2,1,0:T(8,128)(2,1)S(1)}, bf16[4,320,256]{2,1,0:T(8,128)(2,1)S(1)}) custom-call(bf16[16,256,256]{2,1,0:T(8,128)(2,1)S(1)} %get-tuple-element.38.xs_ref, f32[4,320,256]{2,1,0:T(8,128)S(1)} %get-tuple-element.39.pre_ref, f32[4,320,256]{2,1,0:T(8,128)S(1)} %get-tuple-element.40.ga_ref, ...), custom_call_target="tpu_custom_call" | custom-call | flops 5000000000 | tf_op jit(solution)/shard_map/pallas_call | solution.py:495
  31.3 3.7 %all-to-all-start.1 = ((f32[16,48,128]{2,1,0:T(8,128)}), f32[16,48,128]{2,1,0:T(8,128)S(1)}, u32[]{:S(2)}, u32[]{:S(2)}) async-start(f32[16,48,128]{2,1,0:T(8,128)} %get-tuple-element.49), calls=%async_computation.1 | async-start | bytes 786432 | tf_op jit(solution)/shard_map/all_to_all | solution.py:576
  35.1 6.0 %shard_map.90 = (bf16[8,240,128]{2,1,0:T(8,128)(2,1)S(1)}, bf16[512,512]{1,0:T(8,128)(2,1)S(1)}, bf16[256,256]{1,0:T(8,128)(2,1)S(1)}, bf16[256,256]{1,0:T(8,128)(2,1)S(1)}) custom-call(bf16[4,320,256]{2,1,0:T(8,128)(2,1)S(1)} %get-tuple-element.50.gp_ref, bf16[4,320,256]{2,1,0:T(8,128)(2,1)S(1)} %get-tuple-element.51.act_ref, ...), custom_call_target="tpu_custom_call" | custom-call | flops 6000000000 | tf_op jit(solution)/shard_map/pallas_call | solution.py:495
  41.0 3.0 %all-to-all-done.1.r_ref = f32[16,48,128]{2,1,0:T(8,128)S(1)} async-done(((f32[16,48,128]{2,1,0:T(8,128)}), f32[16,48,128]{2,1,0:T(8,128)S(1)}, u32[]{:S(2)}, u32[]{:S(2)}) %all-to-all-start.1) | async-done | bytes 393248 | tf_op jit(solution)/shard_map/all_to_all | solution.py:576
  44.1 0.6 collective-permute-start.2
  44.7 4.9 %collective-permute-done.2.b_ref = f32[48,128]{1,0:T(8,128)S(1)} collective-permute-done((f32[48,128]{1,0:T(8,128)S(1)}, f32[48,128]{1,0:T(8,128)S(1)}, u32[]{:S(2)}, u32[]{:S(2)}) %collective-permute-start.2) | collective-permute-done | bytes 24608 | tf_op jit(solution)/shard_map/ppermute | solution.py:602
  49.5 16.4 %all_to_all.20.r_ref = f32[8,48,128]{2,1,0:T(8,128)S(1)} all-to-all(f32[8,48,128]{2,1,0:T(8,128)S(1)} %shard_map.92), channel_id=1, replica_groups={{0,16,8,24,4,20,12,28},{1,17,9,25,5,21,13,29},{2,18,10,26,6,22,14,30},{..., dimensions={0} | all-to-all | bytes 393216 | tf_op jit(solution)/shard_map/all_to_all | solution.py:604
  66.0 0.1 collective-permute-start.3
  66.1 1.2 %collective-permute-done.3.other_ref = f32[48,128]{1,0:T(8,128)S(1)} collective-permute-done((f32[48,128]{1,0:T(8,128)S(1)}, f32[48,128]{1,0:T(8,128)S(1)}, u32[]{:S(2)}, u32[]{:S(2)}) %collective-permute-start.3) | collective-permute-done | bytes 24608 | tf_op jit(solution)/shard_map/ppermute | solution.py:608
  67.3 12.4 %all_to_all.21.r_ref = bf16[8,240,128]{2,1,0:T(8,128)(2,1)S(1)} all-to-all(bf16[8,240,128]{2,1,0:T(8,128)(2,1)S(1)} %get-tuple-element.53), channel_id=1, replica_groups=mesh['sx'=8,'sy'=32] {'sx'}, dimensions={0} | all-to-all | bytes 983040 | tf_op jit(solution)/shard_map/all_to_all | solution.py:618
  79.7 1.4 %shard_map.95 = (bf16[256,128]{1,0:T(8,128)(2,1)}, f32[27,8,32]{2,1,0:T(8,128)}, f32[27,32,32]{2,1,0:T(8,128)}, bf16[512,256]{1,0:T(8,128)(2,1)}) custom-call(bf16[8,240,128]{2,1,0:T(8,128)(2,1)S(1)} %all_to_all.21.r_ref, f32[56,128]{1,0:T(8,128)S(1)} %get-tuple-element.54.g_ref, bf16[512,512]{1,0:T(8,128)(2,1)S(1)} %get-tuple-element.55.fcol_ref, ...), custom_call_target="tpu_custom_call" | custom-call | flops 1000000000 | tf_op jit(solution)/shard_map/pallas_call | solution.py:495
  (5 shorter events, 0.1 us)
Async XLA Ops:
  0.6 7.6 %copy-start.6 = (bf16[32]{0:T(256)(128)(2,1)S(1)}, bf16[32]{0:T(256)(128)(2,1)}, u32[]{:S(2)}) copy-start(bf16[32]{0:T(256)(128)(2,1)} %param.7) | copy-start | bytes 196
  0.6 7.8 %copy-start = (bf16[32,32,3,3,3]{1,0,4,3,2:T(8,128)(2,1)S(1)}, bf16[32,32,3,3,3]{1,0,4,3,2:T(8,128)(2,1)}, u32[]{:S(2)}) copy-start(bf16[32,32,3,3,3]{1,0,4,3,2:T(8,128)(2,1)} %param.6) | copy-start | bytes 165892
  0.7 7.8 %copy-start.1 = (bf16[64,32,3,3,3]{0,1,4,3,2:T(8,128)(2,1)S(1)}, bf16[64,32,3,3,3]{0,1,4,3,2:T(8,128)(2,1)}, u32[]{:S(2)}) copy-start(bf16[64,32,3,3,3]{0,1,4,3,2:T(8,128)(2,1)} %param.8) | copy-start | bytes 331780
  3.2 14.5 %all-to-all-start = ((bf16[8,256,128]{2,1,0:T(8,128)(2,1)}), bf16[8,256,128]{2,1,0:T(8,128)(2,1)S(1)}, u32[]{:S(2)}, u32[]{:S(2)}) async-start(bf16[8,256,128]{2,1,0:T(8,128)(2,1)} %shard_map.84), calls=%async_computation | async-start | bytes 1048576 | tf_op jit(solution)/shard_map/all_to_all | solution.py:533
  9.4 12.5 %copy-start.2 = (bf16[512,512]{1,0:T(8,128)(2,1)}, bf16[512,512]{1,0:T(8,128)(2,1)S(1)}, u32[]{:S(2)}) copy-start(bf16[512,512]{1,0:T(8,128)(2,1)S(1)} %get-tuple-element.33.cls_ref) | copy-start | bytes 1572868
  9.4 12.5 %copy-start.4 = (bf16[1024,256]{1,0:T(8,128)(2,1)}, bf16[1024,256]{1,0:T(8,128)(2,1)S(1)}, u32[]{:S(2)}) copy-start(bf16[1024,256]{1,0:T(8,128)(2,1)S(1)} %get-tuple-element.34.og_cols_ref) | copy-start | bytes 1572868
  17.8 9.1 %collective-permute-start = (bf16[8,64,128]{2,1,0:T(8,128)(2,1)S(1)}, bf16[8,64,128]{2,1,0:T(8,128)(2,1)S(1)}, u32[]{:S(2)}, u32[]{:S(2)}) collective-permute-start(bf16[8,64,128]{2,1,0:T(8,128)(2,1)S(1)} %get-tuple-element.43), channel_id=1, source_target_pairs={{0,0},{1,2},{2,1},{3,4},{4,3},{5,6},{6,5},{7,8},{8,7},{9,10},{10,9... | collective-permute-start | bytes 393224 | tf_op jit(solution)/shard_map/ppermute | solution.py:550
  19.7 7.1 %collective-permute-start.1 = (bf16[8,64,128]{2,1,0:T(8,128)(2,1)S(1)}, bf16[8,64,128]{2,1,0:T(8,128)(2,1)S(1)}, u32[]{:S(2)}, u32[]{:S(2)}) collective-permute-start(bf16[8,64,128]{2,1,0:T(8,128)(2,1)S(1)} %get-tuple-element.44), channel_id=1, source_target_pairs={{0,1},{1,0},{2,3},{3,2},{4,5},{5,4},{6,7},{7,6},{8,9},{9,8},{10,11... | collective-permute-start | bytes 393224 | tf_op jit(solution)/shard_map/ppermute | solution.py:553
  24.6 2.3 %copy-start.3 = (bf16[512,512]{1,0:T(8,128)(2,1)S(1)}, bf16[512,512]{1,0:T(8,128)(2,1)}, u32[]{:S(2)}) copy-start(bf16[512,512]{1,0:T(8,128)(2,1)} %copy-done.2) | copy-start | bytes 1572868
  24.6 2.3 %copy-start.5 = (bf16[1024,256]{1,0:T(8,128)(2,1)S(1)}, bf16[1024,256]{1,0:T(8,128)(2,1)}, u32[]{:S(2)}) copy-start(bf16[1024,256]{1,0:T(8,128)(2,1)} %copy-done.4) | copy-start | bytes 1572868
  31.3 12.8 %all-to-all-start.1 = ((f32[16,48,128]{2,1,0:T(8,128)}), f32[16,48,128]{2,1,0:T(8,128)S(1)}, u32[]{:S(2)}, u32[]{:S(2)}) async-start(f32[16,48,128]{2,1,0:T(8,128)} %get-tuple-element.49), calls=%async_computation.1 | async-start | bytes 786432 | tf_op jit(solution)/shard_map/all_to_all | solution.py:576
  44.1 5.4 %collective-permute-start.2 = (f32[48,128]{1,0:T(8,128)S(1)}, f32[48,128]{1,0:T(8,128)S(1)}, u32[]{:S(2)}, u32[]{:S(2)}) collective-permute-start(f32[48,128]{1,0:T(8,128)S(1)} %shard_map.91.a_ref), channel_id=1, source_target_pairs={{0,2},{1,3},{2,0},{3,1},{4,6},{5,7},{6,4},{7,5},{8,10},{9,11},{10,... | collective-permute-start | bytes 73736 | tf_op jit(solution)/shard_map/ppermute | solution.py:602
  66.0 1.3 %collective-permute-start.3 = (f32[48,128]{1,0:T(8,128)S(1)}, f32[48,128]{1,0:T(8,128)S(1)}, u32[]{:S(2)}, u32[]{:S(2)}) collective-permute-start(f32[48,128]{1,0:T(8,128)S(1)} %shard_map.93.mine_ref), channel_id=1, source_target_pairs={{0,1},{1,0},{2,3},{3,2},{4,5},{5,4},{6,7},{7,6},{8,9},{9,8},{10,11... | collective-permute-start | bytes 73736 | tf_op jit(solution)/shard_map/ppermute | solution.py:608

commit v4 on v3

--- a/solution.py
+++ b/solution.py
@@ -68,6 +68,11 @@
     base = (cls[0] * 2 + cls[1]) * 4
     for n, form in enumerate(variants(x, cls)):
         ref[base + n] = form
+
+
+def width_block(n):
+    flip = lax.rem(lax.axis_index("sy") // 2, 2)
+    return n + (1 - 2 * (n % 2)) * flip
 
 
 def pack_kernel(vol_hbm, og_hbm, out_hbm, vol_ref, og_ref, out_ref, sems):
@@ -108,18 +113,16 @@
             [planes[n][:, block * 128 : (block + 1) * 128] for n, block, _ in chosen[j]], axis=1
         )
         out_ref[j] = move(cat, jnp.concatenate([m for _, _, m in chosen[j]], axis=0))
-        copies += (pltpu.make_async_copy(out_ref.at[j], out_hbm.at[j], sems.at[2 + j]),)
+        copies += (pltpu.make_async_copy(out_ref.at[j], out_hbm.at[width_block(j)], sems.at[2 + j]),)
         copies[-1].start()
     for copy in copies[2:]:
         copy.wait()
 
 
 def split_kernel(r_ref, cross_ref, pair_ref):
-    even = lax.rem(lax.axis_index("sy"), 2) == 0
     for s in range(NX):
-        top, bottom = r_ref[s, 0:64, :], r_ref[s, 192:256, :]
-        cross_ref[s] = jnp.where(even, top, bottom)
-        pair_ref[s] = jnp.where(even, bottom, top)
+        cross_ref[s] = r_ref[s, 192:256, :]
+        pair_ref[s] = r_ref[s, 0:64, :]
 
 
 def by_class(parts, cls_cols):
@@ -225,12 +228,16 @@
                 t2t_ref[t, at, :] = jnp.concatenate([none, strip] if n > 1 else [strip, none], axis=1)
 
 
-def build_back(k1_ref, k2_ref, t1t_ref, t2_ref):
+def build_back(k1_ref, t1t_ref):
     for t, (a, c) in enumerate(TAPS):
         back = jnp.concatenate([x.T for x in reversed(kernel_blocks(k1_ref, a, c))], axis=1)
-        strided = jnp.concatenate([x.T for x in kernel_blocks(k2_ref, a, c)], axis=1)
         for h in range(8):
             t1t_ref[t, h * 32 : (h + 1) * 32, :] = place(back, 32 * h, 320).astype(BF16)
+
+
+def build_strided(k2_ref, t2_ref):
+    for t, (a, c) in enumerate(TAPS):
+        strided = jnp.concatenate([x.T for x in kernel_blocks(k2_ref, a, c)], axis=1)
         for g in range(4):
             t2_ref[t, g * 64 : (g + 1) * 64, :] = place(strided, 64 * g, 320).astype(BF16)
 
@@ -292,14 +299,13 @@
     grads_ref, gp_ref, act_ref,
     rim_ref, ogs_ref, own_ref,
 ):
-    j = lax.axis_index("sx")
+    j = width_block(lax.axis_index("sx"))
     t = lax.axis_index("sy")
     low = t > 0
     high = t < NY - 1
-    even = lax.rem(t, 2) == 0
     none = jnp.zeros((64, 128), BF16)
-    ups = [jnp.where(even, cross_ref[s], pair_ref[s]) for s in range(NX)]
-    downs = [jnp.where(even, pair_ref[s], cross_ref[s]) for s in range(NX)]
+    ups = [cross_ref[s] for s in range(NX)]
+    downs = [pair_ref[s] for s in range(NX)]
     ups = [jnp.where(low, x, none) for x in ups]
     downs = [jnp.where(high, x, none) for x in downs]
     rims = [jnp.concatenate([x, y], axis=0) for x, y in zip(ups, downs)]
@@ -382,10 +388,25 @@
     return x
 
 
+def strided_kernel(act_ref, k2_ref, out_ref, t2_ref):
+    build_strided(k2_ref, t2_ref)
+    col = iota((1, 128), 1)
+    strided_cols = from_row(256, (col >> 4) * 32 + 1 + (col & 15))
+    out = None
+    for tap, (a, c) in enumerate(TAPS):
+        part = dot(t2_ref[tap], act_variant(act_ref, a, c))
+        out = part if out is None else out + part
+    out = dot(out.astype(BF16), strided_cols)
+    for s in range(NX):
+        out_ref[s] = jnp.concatenate(
+            [out[g * 64 + 8 * s : g * 64 + 8 * s + 8] for g in range(4)], axis=0
+        ).astype(BF16)
+
+
 def second_kernel(
-    gp_ref, act_ref, k1_ref, k2_ref,
+    gp_ref, k1_ref, strided_ref,
     out_ref, fcol_ref, rows_ref, og_rows_ref,
-    gs_ref, t1t_ref, t2_ref,
+    gs_ref, t1t_ref,
 ):
     col = iota((1, 512), 1)
     half = (col >> 6) & 1
@@ -399,22 +420,11 @@
         + ((col >> 8) * 2 + (col & 1)) * 16
         + ((col & 31) >> 1),
     )
-    col = col[:, 0:128]
-    strided_cols = from_row(256, (col >> 4) * 32 + 1 + (col & 15))
     row = iota((256, 256), 0)
     col = iota((256, 256), 1)
     rows_ref[...] = pick(col == (row & 7) * 32 + (row >> 3))
     og_rows_ref[...] = pick(col == (row & ~31) + (row & 3) * 8 + ((row >> 2) & 7))
-    build_back(k1_ref, k2_ref, t1t_ref, t2_ref)
-    out = None
-    for tap, (a, c) in enumerate(TAPS):
-        part = dot(t2_ref[tap], act_variant(act_ref, a, c))
-        out = part if out is None else out + part
-    out = dot(out.astype(BF16), strided_cols)
-    for s in range(NX):
-        out_ref[s, 128:160, :] = jnp.concatenate(
-            [out[g * 64 + 8 * s : g * 64 + 8 * s + 8] for g in range(4)], axis=0
-        ).astype(BF16)
+    build_back(k1_ref, t1t_ref)
     for n, cls in enumerate(CLASSES):
         store_variants(gs_ref, gp_ref[n], cls)
     grads = [tap_sum(t1t_ref, gs_ref, conv_taps(pd, pw, -1)).astype(BF16) for pd, pw in CLASSES]
@@ -426,6 +436,15 @@
         got = move(cat, gather_cols)
         for e in range(4):
             out_ref[4 * q + e, 0:128, :] = got[:, e * 128 : (e + 1) * 128]
+    for s in range(NX):
+        out_ref[s, 128:160, :] = strided_ref[s]
+
+
+def first_sum_kernel(r_ref, out_ref):
+    total = r_ref[0]
+    for s in range(1, r_ref.shape[0]):
+        total = total + r_ref[s]
+    out_ref[...] = total
 
 
 def sum_kernel(r_ref, after_ref, out_ref):
@@ -435,7 +454,7 @@
     out_ref[...] = total
 
 
-def pair_kernel(a_ref, b_ref, out_ref):
+def pair_kernel(a_ref, b_ref, after_ref, out_ref):
     total = a_ref[...] + b_ref[...]
     for n in range(out_ref.shape[0]):
         out_ref[n] = total
@@ -461,7 +480,7 @@
 ):
     halves = []
     for q in range(2):
-        cat = jnp.concatenate([r_ref[4 * q + s, 0:128, :] for s in range(4)], axis=1)
+        cat = jnp.concatenate([r_ref[width_block(4 * q + s), 0:128, :] for s in range(4)], axis=1)
         halves.append(move(cat, fcol_ref[...]))
     for pd in range(2):
         blocks = []
@@ -469,7 +488,7 @@
             at = slice((pd * 2 + half) * 128, (pd * 2 + half + 1) * 128)
             blocks.append(jnp.concatenate([halves[0][:, at], halves[1][:, at]], axis=1))
         vol_ref[pd * 256 : (pd + 1) * 256, :] = move(rows_ref[...], jnp.concatenate(blocks, axis=0))
-    parts = [r_ref[s, 128:160, :].astype(F32) for s in range(NX)]
+    parts = [r_ref[width_block(s), 128:160, :].astype(F32) for s in range(NX)]
     group = iota((32, 128), 1) >> 4
     blocks = []
     for e in range(8):
@@ -546,11 +565,11 @@
     cross, pair = call(split_kernel, (shape(NX, 64, 128), shape(NX, 64, 128)), (got,))
     k1, k2, cross = lax.optimization_barrier((k1, k2, cross))
     t1h, t2th = call(rim_kernel, (shape(128, 9 * 128), shape(9, 128, 128)), (k1, k2))
-    ends = (0, NY - 1)
-    cross = lax.ppermute(
-        cross, "sy", [(i, i if i in ends else ((i - 1) ^ 1) + 1) for i in range(NY)]
-    )
-    pair = lax.ppermute(pair, "sy", [(i, i ^ 1) for i in range(NY)])
+    up = [
+        (s * NY + t, (s ^ (t % 2)) * NY + (t + 1) % NY) for s in range(NX) for t in range(NY)
+    ]
+    cross = lax.ppermute(cross, ("sx", "sy"), up)
+    pair = lax.ppermute(pair, ("sx", "sy"), [(b, a) for a, b in up])
     og, xs, pre, grad_act = call(
         inner_kernel,
         (shape(256, 256), shape(16, 256, 256), shape(4, 320, 256, dtype=F32), shape(4, 320, 256, dtype=F32)),
@@ -582,27 +601,38 @@
             [s * NY + 2 * q + r for s in range(NX) for r in range(2)] for q in range(NY // 2)
         ],
     )
+    both = [pl.BlockSpec(memory_space=pltpu.VMEM), pl.BlockSpec(memory_space=pl.ANY)]
+    keep = call(first_sum_kernel, shape(48, 128, dtype=F32), (grads,))
+    keep, act = lax.optimization_barrier((keep, act))
+    other = lax.ppermute(keep, "sy", [(i, i ^ 2) for i in range(NY)])
+    strided = call(
+        strided_kernel,
+        shape(NX, 32, 128),
+        (act, k2),
+        scratch=(pltpu.VMEM((9, 256, 320), BF16),),
+        us=2,
+    )
+    keep = call(
+        pair_kernel,
+        shape(8, 48, 128, dtype=F32),
+        (keep, other, strided),
+        specs=[pl.BlockSpec(memory_space=pltpu.VMEM)] + both,
+    )
+    keep, gp = lax.optimization_barrier((keep, gp))
     buffer, plane_cols, rows_back, og_rows_back = call(
         second_kernel,
         (shape(NX, 240, 128), shape(512, 512), shape(256, 256), shape(256, 256)),
-        (gp, act, k1, k2),
-        scratch=(
-            pltpu.VMEM((16, 320, 256), BF16),
-            pltpu.VMEM((9, 256, 320), BF16),
-            pltpu.VMEM((9, 256, 320), BF16),
-        ),
-        us=6,
+        (gp, k1, strided),
+        scratch=(pltpu.VMEM((16, 320, 256), BF16), pltpu.VMEM((9, 256, 320), BF16)),
+        us=5,
         vmem=20,
     )
-    both = [pl.BlockSpec(memory_space=pltpu.VMEM), pl.BlockSpec(memory_space=pl.ANY)]
-    keep = call(sum_kernel, shape(48, 128, dtype=F32), (grads, buffer), specs=both)
-    keep = call(
-        pair_kernel,
-        shape(8, 48, 128, dtype=F32),
-        (keep, lax.ppermute(keep, "sy", [(i, i ^ 2) for i in range(NY)])),
-    )
     keep = lax.all_to_all(
-        keep, "sy", 0, 0, axis_index_groups=[[4 * z + r for z in (0, 4, 2, 6, 1, 5, 3, 7)] for r in range(4)]
+        keep,
+        "sy",
+        0,
+        0,
+        axis_index_groups=[[4 * z + r for z in (0, 4, 2, 6, 1, 5, 3, 7)] for r in range(4)],
     )
     keep = call(sum_kernel, shape(48, 128, dtype=F32), (keep, buffer), specs=both)
     other = lax.ppermute(keep, "sy", [(i, i ^ 1) for i in range(NY)])

time: 82.8 us -> 80.2 us (0.969); the launches traced: 81.1 us -> 79.8 us
  waiting for transfers between devices: 19.4 us -> 15.2 us
  starting transfers between devices: 13.5 us -> 17.1 us
    ppermute x3, waiting for transfers between devices: 6.88 us -> 1.89 us  [the longest x1 1.88 us: per_device(): other = lax.ppermute(keep, 'sy', [(i, i ^ 2) for i in range(NY)])]
    all_to_all x1, starting transfers between devices: 3.73 us -> 8.33 us  [per_device(): lax.all_to_all(keep, 'sy', 0, 0, axis_index_groups=[[4 * z + r for z in (...]
    ppermute x3, starting transfers between devices: 4.66 us -> 3.66 us  [the longest x1 1.84 us: per_device(): other = lax.ppermute(keep, 'sy', [(i, i ^ 2) for i in range(NY)])]
    pallas_call x12 -> x13, Pallas kernels: 18.4 us -> 18.1 us  [call(): pl.pallas_call(body, out_shape=outs, grid=grid, in_specs=specs or [pl.Blo...]
  transfers between devices with their start and end apart: 6 -> 6, of which waited for: 5 -> 4; matrix products, arithmetic and copies ran while one was open for 0% -> 0% of each run, Pallas kernels for 12% -> 12%
where the time goes in v4:
time: 80.2 us; the launch traced here: 79.8 us
  blocking collectives  28.4 us (35%)
  Pallas kernels  18.1 us (23%)
  starting transfers between devices  17.1 us (21%)
  waiting for transfers between devices  15.2 us (19%)
    pallas_call x13, Pallas kernels, call(): pl.pallas_call(body, out_shape=outs, grid=grid, in_specs=specs or [pl.Blo...  18.1 us
    all_to_all x1, blocking collectives, per_device(): lax.all_to_all(grads, ('sx', 'sy'), 0, 0, axis_index_groups=[[s * NY + 2...  16 us
    all_to_all x1, blocking collectives, per_device(): got = lax.all_to_all(buffer, 'sx', 0, 0)  12.4 us
    all_to_all x1, starting transfers between devices, per_device(): lax.all_to_all(keep, 'sy', 0, 0, axis_index_groups=[[4 * z + r for z in (...  8.33 us
    all_to_all x1, waiting for transfers between devices, per_device(): got = lax.all_to_all(chunks, 'sx', 0, 0)  8.3 us
    all_to_all x1, starting transfers between devices, per_device(): got = lax.all_to_all(chunks, 'sx', 0, 0)  5.03 us
    all_to_all x1, waiting for transfers between devices, per_device(): lax.all_to_all(keep, 'sy', 0, 0, axis_index_groups=[[4 * z + r for z in (...  3.85 us
    ppermute x1, waiting for transfers between devices, per_device(): other = lax.ppermute(keep, 'sy', [(i, i ^ 2) for i in range(NY)])  1.88 us
  transfers between devices with their start and end apart: 6, of which 4 were waited for; matrix products, arithmetic and copies ran while one was open for 0% of the time, Pallas kernels for 12%

profile of v4, /device:TPU:16, one launch (start us, length us, event | category | flops | bytes accessed | tf_op | source)
XLA Modules:
  0.0 79.8 jit_solution(1700328486301129979)
XLA Ops:
  0.6 0.0 copy-start.2
  0.6 0.0 copy-start
  0.7 0.0 copy-start.1
  0.7 2.6 %shard_map.84 = bf16[8,256,128]{2,1,0:T(8,128)(2,1)} custom-call(bf16[512,256]{1,0:T(8,128)(2,1)} %bitcast.22, bf16[256,128]{1,0:T(8,128)(2,1)} %bitcast.23), custom_call_target="tpu_custom_call" | custom-call | flops 1000000000 | tf_op jit(solution)/shard_map/pallas_call | solution.py:514
  3.2 5.0 %all-to-all-start = ((bf16[8,256,128]{2,1,0:T(8,128)(2,1)}), bf16[8,256,128]{2,1,0:T(8,128)(2,1)S(1)}, u32[]{:S(2)}, u32[]{:S(2)}) async-start(bf16[8,256,128]{2,1,0:T(8,128)(2,1)} %shard_map.84), calls=%async_computation | async-start | bytes 1048576 | tf_op jit(solution)/shard_map/all_to_all | solution.py:552
  8.3 0.0 copy-done.2
  8.3 0.2 broadcast_in_dim_tile.4.bias_ref
  8.4 0.0 copy-done
  8.4 0.0 copy-done.1
  8.5 1.0 %shard_map.85 = (bf16[9,4,32,256]{3,2,1,0:T(8,128)(2,1)S(1)}, bf16[9,2,32,256]{3,2,1,0:T(8,128)(2,1)S(1)}, bf16[9,2,32,128]{3,2,1,0:T(8,128)(2,1)S(1)}, bf16[512...) custom-call(bf16[27,32,32]{2,1,0:T(8,128)(2,1)S(1)} %bitcast.19, bf16[27,32,64]{2,1,0:T(8,128)(2,1)S(1)} %bitcast.16), custom_call_target="tpu_custom_call" | custom-call | flops 3000000000 | tf_op jit(solution)/shard_map/pallas_call | solution.py:514
  9.4 8.3 %all-to-all-done.r_ref = bf16[8,256,128]{2,1,0:T(8,128)(2,1)S(1)} async-done(((bf16[8,256,128]{2,1,0:T(8,128)(2,1)}), bf16[8,256,128]{2,1,0:T(8,128)(2,1)S(1)}, u32[]{:S(2)}, u32[]{:S(2)}) %all-to-all-start) | async-done | bytes 524320 | tf_op jit(solution)/shard_map/all_to_all | solution.py:552
  17.7 0.1 collective-permute-start
  17.8 1.7 %collective-permute-start.1 = (bf16[8,64,128]{2,1,0:T(8,128)(2,1)S(1)}, bf16[8,64,128]{2,1,0:T(8,128)(2,1)S(1)}, u32[]{:S(2)}, u32[]{:S(2)}) collective-permute-start(bf16[8,64,128]{2,1,0:T(8,128)(2,1)S(1)} %get-tuple-element.48), channel_id=1, source_target_pairs={{1,0},{34,1},{3,2},{36,3},{5,4},{38,5},{7,6},{40,7},{9,8},{42,9},{... | collective-permute-start | bytes 393224 | tf_op jit(solution)/shard_map/ppermute | solution.py:572
  19.6 2.7 %shard_map.86 = (bf16[256,256]{1,0:T(8,128)(2,1)S(1)}, bf16[16,256,256]{2,1,0:T(8,128)(2,1)S(1)}, f32[4,320,256]{2,1,0:T(8,128)S(1)}, f32[4,320,256]{2,1,0:T(8,128)S(1)}) custom-call(bf16[8,256,128]{2,1,0:T(8,128)(2,1)S(1)} %all-to-all-done.r_ref, bf16[512,512]{1,0:T(8,128)(2,1)S(1)} %get-tuple-element.37.cls_ref, ...), custom_call_target="tpu_custom_call" | custom-call | flops 5000000000 | tf_op jit(solution)/shard_map/pallas_call | solution.py:514
  22.3 0.2 shard_map.88
  22.5 0.0 collective-permute-done.cross_ref
  22.5 0.0 collective-permute-done.1.pair_ref
  22.5 3.7 %shard_map.89 = (f32[16,48,128]{2,1,0:T(8,128)S(1)}, bf16[4,320,256]{2,1,0:T(8,128)(2,1)S(1)}, bf16[4,320,256]{2,1,0:T(8,128)(2,1)S(1)}) custom-call(bf16[16,256,256]{2,1,0:T(8,128)(2,1)S(1)} %get-tuple-element.42.xs_ref, f32[4,320,256]{2,1,0:T(8,128)S(1)} %get-tuple-element.43.pre_ref, f32[4,320,256]{2,1,0:T(8,128)S(1)} %get-tuple-element.44.ga_ref, ...), custom_call_target="tpu_custom_call" | custom-call | flops 5000000000 | tf_op jit(solution)/shard_map/pallas_call | solution.py:514
  26.2 16.0 %all_to_all.20.r_ref = f32[16,48,128]{2,1,0:T(8,128)S(1)} all-to-all(f32[16,48,128]{2,1,0:T(8,128)S(1)} %get-tuple-element.53), channel_id=1, replica_groups={{0,1,32,33,64,65,96,97,128,129,160,161,192,193,224,225},{2,3,34,35,66,6..., dimensions={0} | all-to-all | bytes 786432 | tf_op jit(solution)/shard_map/all_to_all | solution.py:595
  42.2 1.8 %collective-permute-start.2 = (f32[48,128]{1,0:T(8,128)S(1)}, f32[48,128]{1,0:T(8,128)S(1)}, u32[]{:S(2)}, u32[]{:S(2)}) collective-permute-start(f32[48,128]{1,0:T(8,128)S(1)} %shard_map.90.a_ref), channel_id=1, source_target_pairs={{0,2},{1,3},{2,0},{3,1},{4,6},{5,7},{6,4},{7,5},{8,10},{9,11},{10,... | collective-permute-start | bytes 73736 | tf_op jit(solution)/shard_map/ppermute | solution.py:607
  44.1 1.7 %shard_map.91.after_ref.strided_ref = bf16[8,32,128]{2,1,0:T(8,128)(2,1)S(1)} custom-call(bf16[4,320,256]{2,1,0:T(8,128)(2,1)S(1)} %get-tuple-element.56.act_ref, bf16[27,32,64]{2,1,0:T(8,128)(2,1)S(1)} %bitcast.18), custom_call_target="tpu_custom_call" | custom-call | flops 2000000000 | tf_op jit(solution)/shard_map/pallas_call | solution.py:514
  45.7 1.9 %collective-permute-done.2.b_ref = f32[48,128]{1,0:T(8,128)S(1)} collective-permute-done((f32[48,128]{1,0:T(8,128)S(1)}, f32[48,128]{1,0:T(8,128)S(1)}, u32[]{:S(2)}, u32[]{:S(2)}) %collective-permute-start.2) | collective-permute-done | bytes 24608 | tf_op jit(solution)/shard_map/ppermute | solution.py:607
  47.6 0.7 shard_map.92
  48.3 8.3 %all-to-all-start.2 = ((f32[8,48,128]{2,1,0:T(8,128)}), f32[8,48,128]{2,1,0:T(8,128)S(1)}, u32[]{:S(2)}, u32[]{:S(2)}) async-start(f32[8,48,128]{2,1,0:T(8,128)} %shard_map.92), calls=%async_computation.2 | async-start | bytes 393216 | tf_op jit(solution)/shard_map/all_to_all | solution.py:630
  56.6 4.2 %shard_map.93 = (bf16[8,240,128]{2,1,0:T(8,128)(2,1)S(1)}, bf16[512,512]{1,0:T(8,128)(2,1)S(1)}, bf16[256,256]{1,0:T(8,128)(2,1)S(1)}, bf16[256,256]{1,0:T(8,128)(2,1)S(1)}) custom-call(bf16[4,320,256]{2,1,0:T(8,128)(2,1)S(1)} %get-tuple-element.59.gp_ref, bf16[27,32,32]{2,1,0:T(8,128)(2,1)S(1)} %bitcast.21, ...), custom_call_target="tpu_custom_call" | custom-call | flops 5000000000 | tf_op jit(solution)/shard_map/pallas_call | solution.py:514
  60.8 3.9 %all-to-all-done.2.r_ref = f32[8,48,128]{2,1,0:T(8,128)S(1)} async-done(((f32[8,48,128]{2,1,0:T(8,128)}), f32[8,48,128]{2,1,0:T(8,128)S(1)}, u32[]{:S(2)}, u32[]{:S(2)}) %all-to-all-start.2) | async-done | bytes 196640 | tf_op jit(solution)/shard_map/all_to_all | solution.py:630
  64.7 0.1 collective-permute-start.3
  64.8 1.2 %collective-permute-done.3.other_ref = f32[48,128]{1,0:T(8,128)S(1)} collective-permute-done((f32[48,128]{1,0:T(8,128)S(1)}, f32[48,128]{1,0:T(8,128)S(1)}, u32[]{:S(2)}, u32[]{:S(2)}) %collective-permute-start.3) | collective-permute-done | bytes 24608 | tf_op jit(solution)/shard_map/ppermute | solution.py:638
  66.0 12.4 %all_to_all.21.r_ref = bf16[8,240,128]{2,1,0:T(8,128)(2,1)S(1)} all-to-all(bf16[8,240,128]{2,1,0:T(8,128)(2,1)S(1)} %get-tuple-element.61), channel_id=1, replica_groups=mesh['sx'=8,'sy'=32] {'sx'}, dimensions={0} | all-to-all | bytes 983040 | tf_op jit(solution)/shard_map/all_to_all | solution.py:648
  78.5 1.4 %shard_map.96 = (bf16[256,128]{1,0:T(8,128)(2,1)}, f32[27,8,32]{2,1,0:T(8,128)}, f32[27,32,32]{2,1,0:T(8,128)}, bf16[512,256]{1,0:T(8,128)(2,1)}) custom-call(bf16[8,240,128]{2,1,0:T(8,128)(2,1)S(1)} %all_to_all.21.r_ref, f32[56,128]{1,0:T(8,128)S(1)} %get-tuple-element.62.g_ref, bf16[512,512]{1,0:T(8,128)(2,1)S(1)} %get-tuple-element.63.fcol_ref, ...), custom_call_target="tpu_custom_call" | custom-call | flops 1000000000 | tf_op jit(solution)/shard_map/pallas_call | solution.py:514
  (5 shorter events, 0.1 us)
Async XLA Ops:
  0.6 7.6 %copy-start.2 = (bf16[32]{0:T(256)(128)(2,1)S(1)}, bf16[32]{0:T(256)(128)(2,1)}, u32[]{:S(2)}) copy-start(bf16[32]{0:T(256)(128)(2,1)} %param.7) | copy-start | bytes 196
  0.6 7.8 %copy-start = (bf16[64,32,3,3,3]{0,1,4,3,2:T(8,128)(2,1)S(1)}, bf16[64,32,3,3,3]{0,1,4,3,2:T(8,128)(2,1)}, u32[]{:S(2)}) copy-start(bf16[64,32,3,3,3]{0,1,4,3,2:T(8,128)(2,1)} %param.8) | copy-start | bytes 331780
  0.7 7.8 %copy-start.1 = (bf16[32,32,3,3,3]{1,0,4,3,2:T(8,128)(2,1)S(1)}, bf16[32,32,3,3,3]{1,0,4,3,2:T(8,128)(2,1)}, u32[]{:S(2)}) copy-start(bf16[32,32,3,3,3]{1,0,4,3,2:T(8,128)(2,1)} %param.6) | copy-start | bytes 165892
  3.2 14.5 %all-to-all-start = ((bf16[8,256,128]{2,1,0:T(8,128)(2,1)}), bf16[8,256,128]{2,1,0:T(8,128)(2,1)S(1)}, u32[]{:S(2)}, u32[]{:S(2)}) async-start(bf16[8,256,128]{2,1,0:T(8,128)(2,1)} %shard_map.84), calls=%async_computation | async-start | bytes 1048576 | tf_op jit(solution)/shard_map/all_to_all | solution.py:552
  17.7 4.7 %collective-permute-start = (bf16[8,64,128]{2,1,0:T(8,128)(2,1)S(1)}, bf16[8,64,128]{2,1,0:T(8,128)(2,1)S(1)}, u32[]{:S(2)}, u32[]{:S(2)}) collective-permute-start(bf16[8,64,128]{2,1,0:T(8,128)(2,1)S(1)} %get-tuple-element.47), channel_id=1, source_target_pairs={{0,1},{1,34},{2,3},{3,36},{4,5},{5,38},{6,7},{7,40},{8,9},{9,42},{... | collective-permute-start | bytes 393224 | tf_op jit(solution)/shard_map/ppermute | solution.py:571
  17.8 4.6 %collective-permute-start.1 = (bf16[8,64,128]{2,1,0:T(8,128)(2,1)S(1)}, bf16[8,64,128]{2,1,0:T(8,128)(2,1)S(1)}, u32[]{:S(2)}, u32[]{:S(2)}) collective-permute-start(bf16[8,64,128]{2,1,0:T(8,128)(2,1)S(1)} %get-tuple-element.48), channel_id=1, source_target_pairs={{1,0},{34,1},{3,2},{36,3},{5,4},{38,5},{7,6},{40,7},{9,8},{42,9},{... | collective-permute-start | bytes 393224 | tf_op jit(solution)/shard_map/ppermute | solution.py:572
  42.2 5.4 %collective-permute-start.2 = (f32[48,128]{1,0:T(8,128)S(1)}, f32[48,128]{1,0:T(8,128)S(1)}, u32[]{:S(2)}, u32[]{:S(2)}) collective-permute-start(f32[48,128]{1,0:T(8,128)S(1)} %shard_map.90.a_ref), channel_id=1, source_target_pairs={{0,2},{1,3},{2,0},{3,1},{4,6},{5,7},{6,4},{7,5},{8,10},{9,11},{10,... | collective-permute-start | bytes 73736 | tf_op jit(solution)/shard_map/ppermute | solution.py:607
  48.3 16.4 %all-to-all-start.2 = ((f32[8,48,128]{2,1,0:T(8,128)}), f32[8,48,128]{2,1,0:T(8,128)S(1)}, u32[]{:S(2)}, u32[]{:S(2)}) async-start(f32[8,48,128]{2,1,0:T(8,128)} %shard_map.92), calls=%async_computation.2 | async-start | bytes 393216 | tf_op jit(solution)/shard_map/all_to_all | solution.py:630
  64.7 1.3 %collective-permute-start.3 = (f32[48,128]{1,0:T(8,128)S(1)}, f32[48,128]{1,0:T(8,128)S(1)}, u32[]{:S(2)}, u32[]{:S(2)}) collective-permute-start(f32[48,128]{1,0:T(8,128)S(1)} %shard_map.94.mine_ref), channel_id=1, source_target_pairs={{0,1},{1,0},{2,3},{3,2},{4,5},{5,4},{6,7},{7,6},{8,9},{9,8},{10,11... | collective-permute-start | bytes 73736 | tf_op jit(solution)/shard_map/ppermute | solution.py:638

commit v5 on v4

--- a/solution.py
+++ b/solution.py
@@ -297,7 +297,7 @@
     xs_ref, pre_ref, ga_ref, og_ref, cross_ref, pair_ref, cls_ref, og_cols_ref, bias_ref, t1h_ref,
     t2th_ref,
     grads_ref, gp_ref, act_ref,
-    rim_ref, ogs_ref, own_ref,
+    rim_ref, ogs_ref, own_ref, og_own_ref,
 ):
     j = width_block(lax.axis_index("sx"))
     t = lax.axis_index("sy")
@@ -342,10 +342,12 @@
         own_ref[n] = jnp.where(mine, grad[32:288], 0.0).astype(BF16)
 
     lane = lax.rem(lax.broadcasted_iota(jnp.int32, (256, 256), 1), 32)
-    og_own = jnp.where((lane >= 1) & (lane <= 16), og_ref[...].astype(F32), 0.0).astype(BF16)
+    store_cotangents(og_own_ref, jnp.where((lane >= 1) & (lane <= 16), og_ref[...].astype(F32), 0.0).astype(BF16))
     twos, ones = [], []
     for tap, (a, c) in enumerate(TAPS):
-        twos.append(strip_sum(dot_nt(act_variant(act_ref, a, c), og_own), 4, 64))
+        pd, sd = step(0, a - 1)
+        pw, sw = step(0, c - 1)
+        twos.append(strip_sum(dot_nt(act_ref[pd * 2 + pw], og_own_ref[sd * 2 + sw]), 4, 64))
         g = None
         for n, (pd, pw) in enumerate(CLASSES):
             at = variant(pd, pw, a - 1, c - 1)
@@ -589,6 +591,7 @@
             pltpu.VMEM((4, 9 * 128, 256), BF16),
             pltpu.VMEM((4, 128, 256), BF16),
             pltpu.VMEM((4, 256, 256), BF16),
+            pltpu.VMEM((4, 256, 256), BF16),
         ),
         us=5,
     )
@@ -632,7 +635,7 @@
         "sy",
         0,
         0,
-        axis_index_groups=[[4 * z + r for z in (0, 4, 2, 6, 1, 5, 3, 7)] for r in range(4)],
+        axis_index_groups=[[4 * z + r for z in (4, 0, 5, 1, 6, 2, 7, 3)] for r in range(4)],
     )
     keep = call(sum_kernel, shape(48, 128, dtype=F32), (keep, buffer), specs=both)
     other = lax.ppermute(keep, "sy", [(i, i ^ 1) for i in range(NY)])

time: 80.2 us -> 79 us (0.985)
  waiting for transfers between devices: 15.2 us -> 11.4 us
  starting transfers between devices: 17.1 us -> 19.8 us
    all_to_all x1, waiting for transfers between devices: 3.85 us -> 0.01 us  [per_device(): lax.all_to_all(keep, 'sy', 0, 0, axis_index_groups=[[4 * z + r for z in (...]
    all_to_all x1, starting transfers between devices: 8.33 us -> 11 us  [per_device(): lax.all_to_all(keep, 'sy', 0, 0, axis_index_groups=[[4 * z + r for z in (...]
  transfers between devices with their start and end apart: 6 -> 6, of which waited for: 4 -> 3; matrix products, arithmetic and copies ran while one was open for 0% -> 0% of each run, Pallas kernels for 12% -> 12%
where the time goes in v5:
time: 79 us; the launch traced here: 78.6 us
  blocking collectives  28.4 us (36%)
  starting transfers between devices  19.8 us (25%)
  Pallas kernels  18.1 us (23%)
  waiting for transfers between devices  11.4 us (14%)
  between operations  0.79 us (1%)
    pallas_call x13, Pallas kernels, call(): pl.pallas_call(body, out_shape=outs, grid=grid, in_specs=specs or [pl.Blo...  18.1 us
    all_to_all x1, blocking collectives, per_device(): lax.all_to_all(grads, ('sx', 'sy'), 0, 0, axis_index_groups=[[s * NY + 2...  16 us
    all_to_all x1, blocking collectives, per_device(): got = lax.all_to_all(buffer, 'sx', 0, 0)  12.4 us
    all_to_all x1, starting transfers between devices, per_device(): lax.all_to_all(keep, 'sy', 0, 0, axis_index_groups=[[4 * z + r for z in (...  11 us
    all_to_all x1, waiting for transfers between devices, per_device(): got = lax.all_to_all(chunks, 'sx', 0, 0)  8.3 us
    all_to_all x1, starting transfers between devices, per_device(): got = lax.all_to_all(chunks, 'sx', 0, 0)  5.03 us
    ppermute x1, waiting for transfers between devices, per_device(): other = lax.ppermute(keep, 'sy', [(i, i ^ 2) for i in range(NY)])  1.88 us
    ppermute x1, starting transfers between devices, per_device(): other = lax.ppermute(keep, 'sy', [(i, i ^ 2) for i in range(NY)])  1.85 us
  transfers between devices with their start and end apart: 6, of which 3 were waited for; matrix products, arithmetic and copies ran while one was open for 0% of the time, Pallas kernels for 12%

profile of v5, /device:TPU:16, one launch (start us, length us, event | category | flops | bytes accessed | tf_op | source)
XLA Modules:
  0.0 78.6 jit_solution(12314357937919092357)
XLA Ops:
  0.6 0.0 copy-start.2
  0.6 0.0 copy-start
  0.7 0.0 copy-start.1
  0.7 2.6 %shard_map.84 = bf16[8,256,128]{2,1,0:T(8,128)(2,1)} custom-call(bf16[512,256]{1,0:T(8,128)(2,1)} %bitcast.22, bf16[256,128]{1,0:T(8,128)(2,1)} %bitcast.23), custom_call_target="tpu_custom_call" | custom-call | flops 1000000000 | tf_op jit(solution)/shard_map/pallas_call | solution.py:516
  3.2 5.0 %all-to-all-start = ((bf16[8,256,128]{2,1,0:T(8,128)(2,1)}), bf16[8,256,128]{2,1,0:T(8,128)(2,1)S(1)}, u32[]{:S(2)}, u32[]{:S(2)}) async-start(bf16[8,256,128]{2,1,0:T(8,128)(2,1)} %shard_map.84), calls=%async_computation | async-start | bytes 1048576 | tf_op jit(solution)/shard_map/all_to_all | solution.py:554
  8.3 0.0 copy-done.2
  8.3 0.2 broadcast_in_dim_tile.4.bias_ref
  8.4 0.0 copy-done
  8.4 0.0 copy-done.1
  8.5 1.0 %shard_map.85 = (bf16[9,4,32,256]{3,2,1,0:T(8,128)(2,1)S(1)}, bf16[9,2,32,256]{3,2,1,0:T(8,128)(2,1)S(1)}, bf16[9,2,32,128]{3,2,1,0:T(8,128)(2,1)S(1)}, bf16[512...) custom-call(bf16[27,32,32]{2,1,0:T(8,128)(2,1)S(1)} %bitcast.19, bf16[27,32,64]{2,1,0:T(8,128)(2,1)S(1)} %bitcast.16), custom_call_target="tpu_custom_call" | custom-call | flops 3000000000 | tf_op jit(solution)/shard_map/pallas_call | solution.py:516
  9.4 8.3 %all-to-all-done.r_ref = bf16[8,256,128]{2,1,0:T(8,128)(2,1)S(1)} async-done(((bf16[8,256,128]{2,1,0:T(8,128)(2,1)}), bf16[8,256,128]{2,1,0:T(8,128)(2,1)S(1)}, u32[]{:S(2)}, u32[]{:S(2)}) %all-to-all-start) | async-done | bytes 524320 | tf_op jit(solution)/shard_map/all_to_all | solution.py:554
  17.7 0.1 collective-permute-start
  17.8 1.7 %collective-permute-start.1 = (bf16[8,64,128]{2,1,0:T(8,128)(2,1)S(1)}, bf16[8,64,128]{2,1,0:T(8,128)(2,1)S(1)}, u32[]{:S(2)}, u32[]{:S(2)}) collective-permute-start(bf16[8,64,128]{2,1,0:T(8,128)(2,1)S(1)} %get-tuple-element.48), channel_id=1, source_target_pairs={{1,0},{34,1},{3,2},{36,3},{5,4},{38,5},{7,6},{40,7},{9,8},{42,9},{... | collective-permute-start | bytes 393224 | tf_op jit(solution)/shard_map/ppermute | solution.py:574
  19.6 2.7 %shard_map.86 = (bf16[256,256]{1,0:T(8,128)(2,1)S(1)}, bf16[16,256,256]{2,1,0:T(8,128)(2,1)S(1)}, f32[4,320,256]{2,1,0:T(8,128)S(1)}, f32[4,320,256]{2,1,0:T(8,128)S(1)}) custom-call(bf16[8,256,128]{2,1,0:T(8,128)(2,1)S(1)} %all-to-all-done.r_ref, bf16[512,512]{1,0:T(8,128)(2,1)S(1)} %get-tuple-element.37.cls_ref, ...), custom_call_target="tpu_custom_call" | custom-call | flops 5000000000 | tf_op jit(solution)/shard_map/pallas_call | solution.py:516
  22.3 0.2 shard_map.88
  22.5 0.0 collective-permute-done.cross_ref
  22.5 0.0 collective-permute-done.1.pair_ref
  22.5 3.6 %shard_map.89 = (f32[16,48,128]{2,1,0:T(8,128)S(1)}, bf16[4,320,256]{2,1,0:T(8,128)(2,1)S(1)}, bf16[4,320,256]{2,1,0:T(8,128)(2,1)S(1)}) custom-call(bf16[16,256,256]{2,1,0:T(8,128)(2,1)S(1)} %get-tuple-element.42.xs_ref, f32[4,320,256]{2,1,0:T(8,128)S(1)} %get-tuple-element.43.pre_ref, f32[4,320,256]{2,1,0:T(8,128)S(1)} %get-tuple-element.44.ga_ref, ...), custom_call_target="tpu_custom_call" | custom-call | flops 5000000000 | tf_op jit(solution)/shard_map/pallas_call | solution.py:516
  26.1 16.0 %all_to_all.20.r_ref = f32[16,48,128]{2,1,0:T(8,128)S(1)} all-to-all(f32[16,48,128]{2,1,0:T(8,128)S(1)} %get-tuple-element.53), channel_id=1, replica_groups={{0,1,32,33,64,65,96,97,128,129,160,161,192,193,224,225},{2,3,34,35,66,6..., dimensions={0} | all-to-all | bytes 786432 | tf_op jit(solution)/shard_map/all_to_all | solution.py:598
  42.1 1.8 %collective-permute-start.2 = (f32[48,128]{1,0:T(8,128)S(1)}, f32[48,128]{1,0:T(8,128)S(1)}, u32[]{:S(2)}, u32[]{:S(2)}) collective-permute-start(f32[48,128]{1,0:T(8,128)S(1)} %shard_map.90.a_ref), channel_id=1, source_target_pairs={{0,2},{1,3},{2,0},{3,1},{4,6},{5,7},{6,4},{7,5},{8,10},{9,11},{10,... | collective-permute-start | bytes 73736 | tf_op jit(solution)/shard_map/ppermute | solution.py:610
  44.0 1.7 %shard_map.91.after_ref.strided_ref = bf16[8,32,128]{2,1,0:T(8,128)(2,1)S(1)} custom-call(bf16[4,320,256]{2,1,0:T(8,128)(2,1)S(1)} %get-tuple-element.56.act_ref, bf16[27,32,64]{2,1,0:T(8,128)(2,1)S(1)} %bitcast.18), custom_call_target="tpu_custom_call" | custom-call | flops 2000000000 | tf_op jit(solution)/shard_map/pallas_call | solution.py:516
  45.7 1.9 %collective-permute-done.2.b_ref = f32[48,128]{1,0:T(8,128)S(1)} collective-permute-done((f32[48,128]{1,0:T(8,128)S(1)}, f32[48,128]{1,0:T(8,128)S(1)}, u32[]{:S(2)}, u32[]{:S(2)}) %collective-permute-start.2) | collective-permute-done | bytes 24608 | tf_op jit(solution)/shard_map/ppermute | solution.py:610
  47.5 0.7 shard_map.92
  48.2 11.0 %all-to-all-start.2 = ((f32[8,48,128]{2,1,0:T(8,128)}), f32[8,48,128]{2,1,0:T(8,128)S(1)}, u32[]{:S(2)}, u32[]{:S(2)}) async-start(f32[8,48,128]{2,1,0:T(8,128)} %shard_map.92), calls=%async_computation.2 | async-start | bytes 393216 | tf_op jit(solution)/shard_map/all_to_all | solution.py:633
  59.2 4.2 %shard_map.93 = (bf16[8,240,128]{2,1,0:T(8,128)(2,1)S(1)}, bf16[512,512]{1,0:T(8,128)(2,1)S(1)}, bf16[256,256]{1,0:T(8,128)(2,1)S(1)}, bf16[256,256]{1,0:T(8,128)(2,1)S(1)}) custom-call(bf16[4,320,256]{2,1,0:T(8,128)(2,1)S(1)} %get-tuple-element.59.gp_ref, bf16[27,32,32]{2,1,0:T(8,128)(2,1)S(1)} %bitcast.21, ...), custom_call_target="tpu_custom_call" | custom-call | flops 5000000000 | tf_op jit(solution)/shard_map/pallas_call | solution.py:516
  63.4 0.0 all-to-all-done.2.r_ref
  63.5 0.1 collective-permute-start.3
  63.6 1.2 %collective-permute-done.3.other_ref = f32[48,128]{1,0:T(8,128)S(1)} collective-permute-done((f32[48,128]{1,0:T(8,128)S(1)}, f32[48,128]{1,0:T(8,128)S(1)}, u32[]{:S(2)}, u32[]{:S(2)}) %collective-permute-start.3) | collective-permute-done | bytes 24608 | tf_op jit(solution)/shard_map/ppermute | solution.py:641
  64.8 12.4 %all_to_all.21.r_ref = bf16[8,240,128]{2,1,0:T(8,128)(2,1)S(1)} all-to-all(bf16[8,240,128]{2,1,0:T(8,128)(2,1)S(1)} %get-tuple-element.61), channel_id=1, replica_groups=mesh['sx'=8,'sy'=32] {'sx'}, dimensions={0} | all-to-all | bytes 983040 | tf_op jit(solution)/shard_map/all_to_all | solution.py:651
  77.2 1.4 %shard_map.96 = (bf16[256,128]{1,0:T(8,128)(2,1)}, f32[27,8,32]{2,1,0:T(8,128)}, f32[27,32,32]{2,1,0:T(8,128)}, bf16[512,256]{1,0:T(8,128)(2,1)}) custom-call(bf16[8,240,128]{2,1,0:T(8,128)(2,1)S(1)} %all_to_all.21.r_ref, f32[56,128]{1,0:T(8,128)S(1)} %get-tuple-element.62.g_ref, bf16[512,512]{1,0:T(8,128)(2,1)S(1)} %get-tuple-element.63.fcol_ref, ...), custom_call_target="tpu_custom_call" | custom-call | flops 1000000000 | tf_op jit(solution)/shard_map/pallas_call | solution.py:516
  (5 shorter events, 0.1 us)
Async XLA Ops:
  0.6 7.6 %copy-start.2 = (bf16[32]{0:T(256)(128)(2,1)S(1)}, bf16[32]{0:T(256)(128)(2,1)}, u32[]{:S(2)}) copy-start(bf16[32]{0:T(256)(128)(2,1)} %param.7) | copy-start | bytes 196
  0.6 7.8 %copy-start = (bf16[64,32,3,3,3]{0,1,4,3,2:T(8,128)(2,1)S(1)}, bf16[64,32,3,3,3]{0,1,4,3,2:T(8,128)(2,1)}, u32[]{:S(2)}) copy-start(bf16[64,32,3,3,3]{0,1,4,3,2:T(8,128)(2,1)} %param.8) | copy-start | bytes 331780
  0.7 7.8 %copy-start.1 = (bf16[32,32,3,3,3]{1,0,4,3,2:T(8,128)(2,1)S(1)}, bf16[32,32,3,3,3]{1,0,4,3,2:T(8,128)(2,1)}, u32[]{:S(2)}) copy-start(bf16[32,32,3,3,3]{1,0,4,3,2:T(8,128)(2,1)} %param.6) | copy-start | bytes 165892
  3.2 14.5 %all-to-all-start = ((bf16[8,256,128]{2,1,0:T(8,128)(2,1)}), bf16[8,256,128]{2,1,0:T(8,128)(2,1)S(1)}, u32[]{:S(2)}, u32[]{:S(2)}) async-start(bf16[8,256,128]{2,1,0:T(8,128)(2,1)} %shard_map.84), calls=%async_computation | async-start | bytes 1048576 | tf_op jit(solution)/shard_map/all_to_all | solution.py:554
  17.7 4.7 %collective-permute-start = (bf16[8,64,128]{2,1,0:T(8,128)(2,1)S(1)}, bf16[8,64,128]{2,1,0:T(8,128)(2,1)S(1)}, u32[]{:S(2)}, u32[]{:S(2)}) collective-permute-start(bf16[8,64,128]{2,1,0:T(8,128)(2,1)S(1)} %get-tuple-element.47), channel_id=1, source_target_pairs={{0,1},{1,34},{2,3},{3,36},{4,5},{5,38},{6,7},{7,40},{8,9},{9,42},{... | collective-permute-start | bytes 393224 | tf_op jit(solution)/shard_map/ppermute | solution.py:573
  17.8 4.6 %collective-permute-start.1 = (bf16[8,64,128]{2,1,0:T(8,128)(2,1)S(1)}, bf16[8,64,128]{2,1,0:T(8,128)(2,1)S(1)}, u32[]{:S(2)}, u32[]{:S(2)}) collective-permute-start(bf16[8,64,128]{2,1,0:T(8,128)(2,1)S(1)} %get-tuple-element.48), channel_id=1, source_target_pairs={{1,0},{34,1},{3,2},{36,3},{5,4},{38,5},{7,6},{40,7},{9,8},{42,9},{... | collective-permute-start | bytes 393224 | tf_op jit(solution)/shard_map/ppermute | solution.py:574
  42.1 5.4 %collective-permute-start.2 = (f32[48,128]{1,0:T(8,128)S(1)}, f32[48,128]{1,0:T(8,128)S(1)}, u32[]{:S(2)}, u32[]{:S(2)}) collective-permute-start(f32[48,128]{1,0:T(8,128)S(1)} %shard_map.90.a_ref), channel_id=1, source_target_pairs={{0,2},{1,3},{2,0},{3,1},{4,6},{5,7},{6,4},{7,5},{8,10},{9,11},{10,... | collective-permute-start | bytes 73736 | tf_op jit(solution)/shard_map/ppermute | solution.py:610
  48.2 15.2 %all-to-all-start.2 = ((f32[8,48,128]{2,1,0:T(8,128)}), f32[8,48,128]{2,1,0:T(8,128)S(1)}, u32[]{:S(2)}, u32[]{:S(2)}) async-start(f32[8,48,128]{2,1,0:T(8,128)} %shard_map.92), calls=%async_computation.2 | async-start | bytes 393216 | tf_op jit(solution)/shard_map/all_to_all | solution.py:633
  63.5 1.3 %collective-permute-start.3 = (f32[48,128]{1,0:T(8,128)S(1)}, f32[48,128]{1,0:T(8,128)S(1)}, u32[]{:S(2)}, u32[]{:S(2)}) collective-permute-start(f32[48,128]{1,0:T(8,128)S(1)} %shard_map.94.mine_ref), channel_id=1, source_target_pairs={{0,1},{1,0},{2,3},{3,2},{4,5},{5,4},{6,7},{7,6},{8,9},{9,8},{10,11... | collective-permute-start | bytes 73736 | tf_op jit(solution)/shard_map/ppermute | solution.py:641

commit v6 on v5

--- a/solution.py
+++ b/solution.py
@@ -15,6 +15,8 @@
 K = 64
 W = 256
 CLASSES = ((0, 0), (0, 1), (1, 0), (1, 1))
+ORDER = (4, 5, 0, 1, 6, 7, 2, 3)
+PLACE = tuple(ORDER.index(s) for s in range(NX))
 TAPS = tuple((a, c) for a in range(3) for c in range(3))
 
 
@@ -437,9 +439,9 @@
         )
         got = move(cat, gather_cols)
         for e in range(4):
-            out_ref[4 * q + e, 0:128, :] = got[:, e * 128 : (e + 1) * 128]
+            out_ref[PLACE[4 * q + e], 0:128, :] = got[:, e * 128 : (e + 1) * 128]
     for s in range(NX):
-        out_ref[s, 128:160, :] = strided_ref[s]
+        out_ref[PLACE[s], 128:160, :] = strided_ref[s]
 
 
 def first_sum_kernel(r_ref, out_ref):
@@ -482,7 +484,7 @@
 ):
     halves = []
     for q in range(2):
-        cat = jnp.concatenate([r_ref[width_block(4 * q + s), 0:128, :] for s in range(4)], axis=1)
+        cat = jnp.concatenate([r_ref[width_block(PLACE[4 * q + s]), 0:128, :] for s in range(4)], axis=1)
         halves.append(move(cat, fcol_ref[...]))
     for pd in range(2):
         blocks = []
@@ -490,7 +492,7 @@
             at = slice((pd * 2 + half) * 128, (pd * 2 + half + 1) * 128)
             blocks.append(jnp.concatenate([halves[0][:, at], halves[1][:, at]], axis=1))
         vol_ref[pd * 256 : (pd + 1) * 256, :] = move(rows_ref[...], jnp.concatenate(blocks, axis=0))
-    parts = [r_ref[width_block(s), 128:160, :].astype(F32) for s in range(NX)]
+    parts = [r_ref[width_block(PLACE[s]), 128:160, :].astype(F32) for s in range(NX)]
     group = iota((32, 128), 1) >> 4
     blocks = []
     for e in range(8):
@@ -500,7 +502,7 @@
             block = turned if block is None else jnp.where(group == j, turned, block)
         blocks.append(block)
     strided_ref[...] = move(og_rows_ref[...], jnp.concatenate(blocks, axis=0).astype(BF16))
-    sums = [r_ref[s, 160:200, :].astype(F32) + r_ref[s, 200:240, :].astype(F32) for s in range(NX)]
+    sums = [r_ref[s, 160:200, :].astype(F32) + r_ref[s, 200:240, :].astype(F32) for s in PLACE]
     two = g_ref[...] * out_scale
     for n in range(7):
         one = jnp.concatenate([x[4 * n : 4 * n + 4] for x in sums], axis=0) * in_scale
@@ -648,7 +650,7 @@
         grid=(1,),
         aliases={2: 0},
     )
-    got = lax.all_to_all(buffer, "sx", 0, 0)
+    got = lax.all_to_all(buffer, "sx", 0, 0, axis_index_groups=[list(ORDER)])
     strided, two, one, vol = call(
         functools.partial(last_kernel, out_scale=out_scale, in_scale=in_scale),
         (shape(256, 128), shape(27, 8, C, dtype=F32), shape(27, C, C, dtype=F32), shape(512, 256)),

time: 79 us -> 78.5 us (level)
  no operation moved by 1% of the time
where the time goes in v6:
time: 78.5 us; the launch traced here: 78.2 us
  blocking collectives  28 us (36%)
  starting transfers between devices  19.8 us (25%)
  Pallas kernels  18.1 us (23%)
  waiting for transfers between devices  11.4 us (15%)
  between operations  0.79 us (1%)
    pallas_call x13, Pallas kernels, call(): pl.pallas_call(body, out_shape=outs, grid=grid, in_specs=specs or [pl.Blo...  18.1 us
    all_to_all x1, blocking collectives, per_device(): lax.all_to_all(grads, ('sx', 'sy'), 0, 0, axis_index_groups=[[s * NY + 2...  16 us
    all_to_all x1, blocking collectives, per_device(): got = lax.all_to_all(buffer, 'sx', 0, 0, axis_index_groups=[list(ORDER)])  12 us
    all_to_all x1, starting transfers between devices, per_device(): lax.all_to_all(keep, 'sy', 0, 0, axis_index_groups=[[4 * z + r for z in (...  11 us
    all_to_all x1, waiting for transfers between devices, per_device(): got = lax.all_to_all(chunks, 'sx', 0, 0)  8.3 us
    all_to_all x1, starting transfers between devices, per_device(): got = lax.all_to_all(chunks, 'sx', 0, 0)  5.03 us
    ppermute x1, waiting for transfers between devices, per_device(): other = lax.ppermute(keep, 'sy', [(i, i ^ 2) for i in range(NY)])  1.88 us
    ppermute x1, starting transfers between devices, per_device(): other = lax.ppermute(keep, 'sy', [(i, i ^ 2) for i in range(NY)])  1.85 us
  transfers between devices with their start and end apart: 6, of which 3 were waited for; matrix products, arithmetic and copies ran while one was open for 0% of the time, Pallas kernels for 12%

profile of v6, /device:TPU:16, one launch (start us, length us, event | category | flops | bytes accessed | tf_op | source)
XLA Modules:
  0.0 78.2 jit_solution(975824629275260819)
XLA Ops:
  0.6 0.0 copy-start.2
  0.6 0.0 copy-start
  0.7 0.0 copy-start.1
  0.7 2.6 %shard_map.84 = bf16[8,256,128]{2,1,0:T(8,128)(2,1)} custom-call(bf16[512,256]{1,0:T(8,128)(2,1)} %bitcast.22, bf16[256,128]{1,0:T(8,128)(2,1)} %bitcast.23), custom_call_target="tpu_custom_call" | custom-call | flops 1000000000 | tf_op jit(solution)/shard_map/pallas_call | solution.py:518
  3.2 5.0 %all-to-all-start = ((bf16[8,256,128]{2,1,0:T(8,128)(2,1)}), bf16[8,256,128]{2,1,0:T(8,128)(2,1)S(1)}, u32[]{:S(2)}, u32[]{:S(2)}) async-start(bf16[8,256,128]{2,1,0:T(8,128)(2,1)} %shard_map.84), calls=%async_computation | async-start | bytes 1048576 | tf_op jit(solution)/shard_map/all_to_all | solution.py:556
  8.3 0.0 copy-done.2
  8.3 0.2 broadcast_in_dim_tile.4.bias_ref
  8.4 0.0 copy-done
  8.4 0.0 copy-done.1
  8.5 1.0 %shard_map.85 = (bf16[9,4,32,256]{3,2,1,0:T(8,128)(2,1)S(1)}, bf16[9,2,32,256]{3,2,1,0:T(8,128)(2,1)S(1)}, bf16[9,2,32,128]{3,2,1,0:T(8,128)(2,1)S(1)}, bf16[512...) custom-call(bf16[27,32,32]{2,1,0:T(8,128)(2,1)S(1)} %bitcast.19, bf16[27,32,64]{2,1,0:T(8,128)(2,1)S(1)} %bitcast.16), custom_call_target="tpu_custom_call" | custom-call | flops 3000000000 | tf_op jit(solution)/shard_map/pallas_call | solution.py:518
  9.4 8.3 %all-to-all-done.r_ref = bf16[8,256,128]{2,1,0:T(8,128)(2,1)S(1)} async-done(((bf16[8,256,128]{2,1,0:T(8,128)(2,1)}), bf16[8,256,128]{2,1,0:T(8,128)(2,1)S(1)}, u32[]{:S(2)}, u32[]{:S(2)}) %all-to-all-start) | async-done | bytes 524320 | tf_op jit(solution)/shard_map/all_to_all | solution.py:556
  17.7 0.1 collective-permute-start
  17.8 1.7 %collective-permute-start.1 = (bf16[8,64,128]{2,1,0:T(8,128)(2,1)S(1)}, bf16[8,64,128]{2,1,0:T(8,128)(2,1)S(1)}, u32[]{:S(2)}, u32[]{:S(2)}) collective-permute-start(bf16[8,64,128]{2,1,0:T(8,128)(2,1)S(1)} %get-tuple-element.48), channel_id=1, source_target_pairs={{1,0},{34,1},{3,2},{36,3},{5,4},{38,5},{7,6},{40,7},{9,8},{42,9},{... | collective-permute-start | bytes 393224 | tf_op jit(solution)/shard_map/ppermute | solution.py:576
  19.6 2.7 %shard_map.86 = (bf16[256,256]{1,0:T(8,128)(2,1)S(1)}, bf16[16,256,256]{2,1,0:T(8,128)(2,1)S(1)}, f32[4,320,256]{2,1,0:T(8,128)S(1)}, f32[4,320,256]{2,1,0:T(8,128)S(1)}) custom-call(bf16[8,256,128]{2,1,0:T(8,128)(2,1)S(1)} %all-to-all-done.r_ref, bf16[512,512]{1,0:T(8,128)(2,1)S(1)} %get-tuple-element.37.cls_ref, ...), custom_call_target="tpu_custom_call" | custom-call | flops 5000000000 | tf_op jit(solution)/shard_map/pallas_call | solution.py:518
  22.3 0.2 shard_map.88
  22.5 0.0 collective-permute-done.cross_ref
  22.5 0.0 collective-permute-done.1.pair_ref
  22.5 3.6 %shard_map.89 = (f32[16,48,128]{2,1,0:T(8,128)S(1)}, bf16[4,320,256]{2,1,0:T(8,128)(2,1)S(1)}, bf16[4,320,256]{2,1,0:T(8,128)(2,1)S(1)}) custom-call(bf16[16,256,256]{2,1,0:T(8,128)(2,1)S(1)} %get-tuple-element.42.xs_ref, f32[4,320,256]{2,1,0:T(8,128)S(1)} %get-tuple-element.43.pre_ref, f32[4,320,256]{2,1,0:T(8,128)S(1)} %get-tuple-element.44.ga_ref, ...), custom_call_target="tpu_custom_call" | custom-call | flops 5000000000 | tf_op jit(solution)/shard_map/pallas_call | solution.py:518
  26.1 16.0 %all_to_all.20.r_ref = f32[16,48,128]{2,1,0:T(8,128)S(1)} all-to-all(f32[16,48,128]{2,1,0:T(8,128)S(1)} %get-tuple-element.53), channel_id=1, replica_groups={{0,1,32,33,64,65,96,97,128,129,160,161,192,193,224,225},{2,3,34,35,66,6..., dimensions={0} | all-to-all | bytes 786432 | tf_op jit(solution)/shard_map/all_to_all | solution.py:600
  42.1 1.8 %collective-permute-start.2 = (f32[48,128]{1,0:T(8,128)S(1)}, f32[48,128]{1,0:T(8,128)S(1)}, u32[]{:S(2)}, u32[]{:S(2)}) collective-permute-start(f32[48,128]{1,0:T(8,128)S(1)} %shard_map.90.a_ref), channel_id=1, source_target_pairs={{0,2},{1,3},{2,0},{3,1},{4,6},{5,7},{6,4},{7,5},{8,10},{9,11},{10,... | collective-permute-start | bytes 73736 | tf_op jit(solution)/shard_map/ppermute | solution.py:612
  44.0 1.7 %shard_map.91.after_ref.strided_ref = bf16[8,32,128]{2,1,0:T(8,128)(2,1)S(1)} custom-call(bf16[4,320,256]{2,1,0:T(8,128)(2,1)S(1)} %get-tuple-element.56.act_ref, bf16[27,32,64]{2,1,0:T(8,128)(2,1)S(1)} %bitcast.18), custom_call_target="tpu_custom_call" | custom-call | flops 2000000000 | tf_op jit(solution)/shard_map/pallas_call | solution.py:518
  45.7 1.9 %collective-permute-done.2.b_ref = f32[48,128]{1,0:T(8,128)S(1)} collective-permute-done((f32[48,128]{1,0:T(8,128)S(1)}, f32[48,128]{1,0:T(8,128)S(1)}, u32[]{:S(2)}, u32[]{:S(2)}) %collective-permute-start.2) | collective-permute-done | bytes 24608 | tf_op jit(solution)/shard_map/ppermute | solution.py:612
  47.5 0.7 shard_map.92
  48.2 11.0 %all-to-all-start.2 = ((f32[8,48,128]{2,1,0:T(8,128)}), f32[8,48,128]{2,1,0:T(8,128)S(1)}, u32[]{:S(2)}, u32[]{:S(2)}) async-start(f32[8,48,128]{2,1,0:T(8,128)} %shard_map.92), calls=%async_computation.2 | async-start | bytes 393216 | tf_op jit(solution)/shard_map/all_to_all | solution.py:635
  59.2 4.2 %shard_map.93 = (bf16[8,240,128]{2,1,0:T(8,128)(2,1)S(1)}, bf16[512,512]{1,0:T(8,128)(2,1)S(1)}, bf16[256,256]{1,0:T(8,128)(2,1)S(1)}, bf16[256,256]{1,0:T(8,128)(2,1)S(1)}) custom-call(bf16[4,320,256]{2,1,0:T(8,128)(2,1)S(1)} %get-tuple-element.59.gp_ref, bf16[27,32,32]{2,1,0:T(8,128)(2,1)S(1)} %bitcast.21, ...), custom_call_target="tpu_custom_call" | custom-call | flops 5000000000 | tf_op jit(solution)/shard_map/pallas_call | solution.py:518
  63.4 0.0 all-to-all-done.2.r_ref
  63.5 0.1 collective-permute-start.3
  63.6 1.2 %collective-permute-done.3.other_ref = f32[48,128]{1,0:T(8,128)S(1)} collective-permute-done((f32[48,128]{1,0:T(8,128)S(1)}, f32[48,128]{1,0:T(8,128)S(1)}, u32[]{:S(2)}, u32[]{:S(2)}) %collective-permute-start.3) | collective-permute-done | bytes 24608 | tf_op jit(solution)/shard_map/ppermute | solution.py:643
  64.8 12.0 %all_to_all.21.r_ref = bf16[8,240,128]{2,1,0:T(8,128)(2,1)S(1)} all-to-all(bf16[8,240,128]{2,1,0:T(8,128)(2,1)S(1)} %get-tuple-element.61), channel_id=1, replica_groups={{128,160,0,32,192,224,64,96},{129,161,1,33,193,225,65,97},{130,162,2,34..., dimensions={0} | all-to-all | bytes 983040 | tf_op jit(solution)/shard_map/all_to_all | solution.py:653
  76.8 1.4 %shard_map.96 = (bf16[256,128]{1,0:T(8,128)(2,1)}, f32[27,8,32]{2,1,0:T(8,128)}, f32[27,32,32]{2,1,0:T(8,128)}, bf16[512,256]{1,0:T(8,128)(2,1)}) custom-call(bf16[8,240,128]{2,1,0:T(8,128)(2,1)S(1)} %all_to_all.21.r_ref, f32[56,128]{1,0:T(8,128)S(1)} %get-tuple-element.62.g_ref, bf16[512,512]{1,0:T(8,128)(2,1)S(1)} %get-tuple-element.63.fcol_ref, ...), custom_call_target="tpu_custom_call" | custom-call | flops 1000000000 | tf_op jit(solution)/shard_map/pallas_call | solution.py:518
  (5 shorter events, 0.1 us)
Async XLA Ops:
  0.6 7.6 %copy-start.2 = (bf16[32]{0:T(256)(128)(2,1)S(1)}, bf16[32]{0:T(256)(128)(2,1)}, u32[]{:S(2)}) copy-start(bf16[32]{0:T(256)(128)(2,1)} %param.7) | copy-start | bytes 196
  0.6 7.8 %copy-start = (bf16[64,32,3,3,3]{0,1,4,3,2:T(8,128)(2,1)S(1)}, bf16[64,32,3,3,3]{0,1,4,3,2:T(8,128)(2,1)}, u32[]{:S(2)}) copy-start(bf16[64,32,3,3,3]{0,1,4,3,2:T(8,128)(2,1)} %param.8) | copy-start | bytes 331780
  0.7 7.8 %copy-start.1 = (bf16[32,32,3,3,3]{1,0,4,3,2:T(8,128)(2,1)S(1)}, bf16[32,32,3,3,3]{1,0,4,3,2:T(8,128)(2,1)}, u32[]{:S(2)}) copy-start(bf16[32,32,3,3,3]{1,0,4,3,2:T(8,128)(2,1)} %param.6) | copy-start | bytes 165892
  3.2 14.5 %all-to-all-start = ((bf16[8,256,128]{2,1,0:T(8,128)(2,1)}), bf16[8,256,128]{2,1,0:T(8,128)(2,1)S(1)}, u32[]{:S(2)}, u32[]{:S(2)}) async-start(bf16[8,256,128]{2,1,0:T(8,128)(2,1)} %shard_map.84), calls=%async_computation | async-start | bytes 1048576 | tf_op jit(solution)/shard_map/all_to_all | solution.py:556
  17.7 4.7 %collective-permute-start = (bf16[8,64,128]{2,1,0:T(8,128)(2,1)S(1)}, bf16[8,64,128]{2,1,0:T(8,128)(2,1)S(1)}, u32[]{:S(2)}, u32[]{:S(2)}) collective-permute-start(bf16[8,64,128]{2,1,0:T(8,128)(2,1)S(1)} %get-tuple-element.47), channel_id=1, source_target_pairs={{0,1},{1,34},{2,3},{3,36},{4,5},{5,38},{6,7},{7,40},{8,9},{9,42},{... | collective-permute-start | bytes 393224 | tf_op jit(solution)/shard_map/ppermute | solution.py:575
  17.8 4.6 %collective-permute-start.1 = (bf16[8,64,128]{2,1,0:T(8,128)(2,1)S(1)}, bf16[8,64,128]{2,1,0:T(8,128)(2,1)S(1)}, u32[]{:S(2)}, u32[]{:S(2)}) collective-permute-start(bf16[8,64,128]{2,1,0:T(8,128)(2,1)S(1)} %get-tuple-element.48), channel_id=1, source_target_pairs={{1,0},{34,1},{3,2},{36,3},{5,4},{38,5},{7,6},{40,7},{9,8},{42,9},{... | collective-permute-start | bytes 393224 | tf_op jit(solution)/shard_map/ppermute | solution.py:576
  42.1 5.4 %collective-permute-start.2 = (f32[48,128]{1,0:T(8,128)S(1)}, f32[48,128]{1,0:T(8,128)S(1)}, u32[]{:S(2)}, u32[]{:S(2)}) collective-permute-start(f32[48,128]{1,0:T(8,128)S(1)} %shard_map.90.a_ref), channel_id=1, source_target_pairs={{0,2},{1,3},{2,0},{3,1},{4,6},{5,7},{6,4},{7,5},{8,10},{9,11},{10,... | collective-permute-start | bytes 73736 | tf_op jit(solution)/shard_map/ppermute | solution.py:612
  48.2 15.2 %all-to-all-start.2 = ((f32[8,48,128]{2,1,0:T(8,128)}), f32[8,48,128]{2,1,0:T(8,128)S(1)}, u32[]{:S(2)}, u32[]{:S(2)}) async-start(f32[8,48,128]{2,1,0:T(8,128)} %shard_map.92), calls=%async_computation.2 | async-start | bytes 393216 | tf_op jit(solution)/shard_map/all_to_all | solution.py:635
  63.5 1.3 %collective-permute-start.3 = (f32[48,128]{1,0:T(8,128)S(1)}, f32[48,128]{1,0:T(8,128)S(1)}, u32[]{:S(2)}, u32[]{:S(2)}) collective-permute-start(f32[48,128]{1,0:T(8,128)S(1)} %shard_map.94.mine_ref), channel_id=1, source_target_pairs={{0,1},{1,0},{2,3},{3,2},{4,5},{5,4},{6,7},{7,6},{8,9},{9,8},{10,11... | collective-permute-start | bytes 73736 | tf_op jit(solution)/shard_map/ppermute | solution.py:643

commit v7 on v6

--- a/solution.py
+++ b/solution.py
@@ -502,7 +502,8 @@
             block = turned if block is None else jnp.where(group == j, turned, block)
         blocks.append(block)
     strided_ref[...] = move(og_rows_ref[...], jnp.concatenate(blocks, axis=0).astype(BF16))
-    sums = [r_ref[s, 160:200, :].astype(F32) + r_ref[s, 200:240, :].astype(F32) for s in PLACE]
+    sums = [r_ref[s, 160:240, :].astype(F32) for s in PLACE]
+    sums = [x[0:40] + x[40:80] for x in sums]
     two = g_ref[...] * out_scale
     for n in range(7):
         one = jnp.concatenate([x[4 * n : 4 * n + 4] for x in sums], axis=0) * in_scale

time: 78.5 us -> 78.5 us (level)
  no operation moved by 1% of the time
where the time goes in v7:
time: 78.5 us; the launch traced here: 78.2 us
  blocking collectives  28 us (36%)
  starting transfers between devices  19.8 us (25%)
  Pallas kernels  18.1 us (23%)
  waiting for transfers between devices  11.4 us (15%)
  between operations  0.79 us (1%)
    pallas_call x13, Pallas kernels, call(): pl.pallas_call(body, out_shape=outs, grid=grid, in_specs=specs or [pl.Blo...  18.1 us
    all_to_all x1, blocking collectives, per_device(): lax.all_to_all(grads, ('sx', 'sy'), 0, 0, axis_index_groups=[[s * NY + 2...  16 us
    all_to_all x1, blocking collectives, per_device(): got = lax.all_to_all(buffer, 'sx', 0, 0, axis_index_groups=[list(ORDER)])  12 us
    all_to_all x1, starting transfers between devices, per_device(): lax.all_to_all(keep, 'sy', 0, 0, axis_index_groups=[[4 * z + r for z in (...  11 us
    all_to_all x1, waiting for transfers between devices, per_device(): got = lax.all_to_all(chunks, 'sx', 0, 0)  8.3 us
    all_to_all x1, starting transfers between devices, per_device(): got = lax.all_to_all(chunks, 'sx', 0, 0)  5.03 us
    ppermute x1, waiting for transfers between devices, per_device(): other = lax.ppermute(keep, 'sy', [(i, i ^ 2) for i in range(NY)])  1.88 us
    ppermute x1, starting transfers between devices, per_device(): other = lax.ppermute(keep, 'sy', [(i, i ^ 2) for i in range(NY)])  1.85 us
  transfers between devices with their start and end apart: 6, of which 3 were waited for; matrix products, arithmetic and copies ran while one was open for 0% of the time, Pallas kernels for 12%

profile of v7, /device:TPU:16, one launch (start us, length us, event | category | flops | bytes accessed | tf_op | source)
XLA Modules:
  0.0 78.2 jit_solution(975824629275260819)
XLA Ops:
  0.6 0.0 copy-start.2
  0.6 0.0 copy-start
  0.7 0.0 copy-start.1
  0.7 2.6 %shard_map.84 = bf16[8,256,128]{2,1,0:T(8,128)(2,1)} custom-call(bf16[512,256]{1,0:T(8,128)(2,1)} %bitcast.22, bf16[256,128]{1,0:T(8,128)(2,1)} %bitcast.23), custom_call_target="tpu_custom_call" | custom-call | flops 1000000000 | tf_op jit(solution)/shard_map/pallas_call | solution.py:519
  3.2 5.0 %all-to-all-start = ((bf16[8,256,128]{2,1,0:T(8,128)(2,1)}), bf16[8,256,128]{2,1,0:T(8,128)(2,1)S(1)}, u32[]{:S(2)}, u32[]{:S(2)}) async-start(bf16[8,256,128]{2,1,0:T(8,128)(2,1)} %shard_map.84), calls=%async_computation | async-start | bytes 1048576 | tf_op jit(solution)/shard_map/all_to_all | solution.py:557
  8.3 0.0 copy-done.2
  8.3 0.2 broadcast_in_dim_tile.4.bias_ref
  8.4 0.0 copy-done
  8.4 0.0 copy-done.1
  8.5 1.0 %shard_map.85 = (bf16[9,4,32,256]{3,2,1,0:T(8,128)(2,1)S(1)}, bf16[9,2,32,256]{3,2,1,0:T(8,128)(2,1)S(1)}, bf16[9,2,32,128]{3,2,1,0:T(8,128)(2,1)S(1)}, bf16[512...) custom-call(bf16[27,32,32]{2,1,0:T(8,128)(2,1)S(1)} %bitcast.19, bf16[27,32,64]{2,1,0:T(8,128)(2,1)S(1)} %bitcast.16), custom_call_target="tpu_custom_call" | custom-call | flops 3000000000 | tf_op jit(solution)/shard_map/pallas_call | solution.py:519
  9.4 8.3 %all-to-all-done.r_ref = bf16[8,256,128]{2,1,0:T(8,128)(2,1)S(1)} async-done(((bf16[8,256,128]{2,1,0:T(8,128)(2,1)}), bf16[8,256,128]{2,1,0:T(8,128)(2,1)S(1)}, u32[]{:S(2)}, u32[]{:S(2)}) %all-to-all-start) | async-done | bytes 524320 | tf_op jit(solution)/shard_map/all_to_all | solution.py:557
  17.7 0.1 collective-permute-start
  17.8 1.7 %collective-permute-start.1 = (bf16[8,64,128]{2,1,0:T(8,128)(2,1)S(1)}, bf16[8,64,128]{2,1,0:T(8,128)(2,1)S(1)}, u32[]{:S(2)}, u32[]{:S(2)}) collective-permute-start(bf16[8,64,128]{2,1,0:T(8,128)(2,1)S(1)} %get-tuple-element.48), channel_id=1, source_target_pairs={{1,0},{34,1},{3,2},{36,3},{5,4},{38,5},{7,6},{40,7},{9,8},{42,9},{... | collective-permute-start | bytes 393224 | tf_op jit(solution)/shard_map/ppermute | solution.py:577
  19.6 2.7 %shard_map.86 = (bf16[256,256]{1,0:T(8,128)(2,1)S(1)}, bf16[16,256,256]{2,1,0:T(8,128)(2,1)S(1)}, f32[4,320,256]{2,1,0:T(8,128)S(1)}, f32[4,320,256]{2,1,0:T(8,128)S(1)}) custom-call(bf16[8,256,128]{2,1,0:T(8,128)(2,1)S(1)} %all-to-all-done.r_ref, bf16[512,512]{1,0:T(8,128)(2,1)S(1)} %get-tuple-element.37.cls_ref, ...), custom_call_target="tpu_custom_call" | custom-call | flops 5000000000 | tf_op jit(solution)/shard_map/pallas_call | solution.py:519
  22.3 0.2 shard_map.88
  22.5 0.0 collective-permute-done.cross_ref
  22.5 0.0 collective-permute-done.1.pair_ref
  22.5 3.6 %shard_map.89 = (f32[16,48,128]{2,1,0:T(8,128)S(1)}, bf16[4,320,256]{2,1,0:T(8,128)(2,1)S(1)}, bf16[4,320,256]{2,1,0:T(8,128)(2,1)S(1)}) custom-call(bf16[16,256,256]{2,1,0:T(8,128)(2,1)S(1)} %get-tuple-element.42.xs_ref, f32[4,320,256]{2,1,0:T(8,128)S(1)} %get-tuple-element.43.pre_ref, f32[4,320,256]{2,1,0:T(8,128)S(1)} %get-tuple-element.44.ga_ref, ...), custom_call_target="tpu_custom_call" | custom-call | flops 5000000000 | tf_op jit(solution)/shard_map/pallas_call | solution.py:519
  26.1 16.0 %all_to_all.20.r_ref = f32[16,48,128]{2,1,0:T(8,128)S(1)} all-to-all(f32[16,48,128]{2,1,0:T(8,128)S(1)} %get-tuple-element.53), channel_id=1, replica_groups={{0,1,32,33,64,65,96,97,128,129,160,161,192,193,224,225},{2,3,34,35,66,6..., dimensions={0} | all-to-all | bytes 786432 | tf_op jit(solution)/shard_map/all_to_all | solution.py:601
  42.1 1.8 %collective-permute-start.2 = (f32[48,128]{1,0:T(8,128)S(1)}, f32[48,128]{1,0:T(8,128)S(1)}, u32[]{:S(2)}, u32[]{:S(2)}) collective-permute-start(f32[48,128]{1,0:T(8,128)S(1)} %shard_map.90.a_ref), channel_id=1, source_target_pairs={{0,2},{1,3},{2,0},{3,1},{4,6},{5,7},{6,4},{7,5},{8,10},{9,11},{10,... | collective-permute-start | bytes 73736 | tf_op jit(solution)/shard_map/ppermute | solution.py:613
  44.0 1.7 %shard_map.91.after_ref.strided_ref = bf16[8,32,128]{2,1,0:T(8,128)(2,1)S(1)} custom-call(bf16[4,320,256]{2,1,0:T(8,128)(2,1)S(1)} %get-tuple-element.56.act_ref, bf16[27,32,64]{2,1,0:T(8,128)(2,1)S(1)} %bitcast.18), custom_call_target="tpu_custom_call" | custom-call | flops 2000000000 | tf_op jit(solution)/shard_map/pallas_call | solution.py:519
  45.7 1.9 %collective-permute-done.2.b_ref = f32[48,128]{1,0:T(8,128)S(1)} collective-permute-done((f32[48,128]{1,0:T(8,128)S(1)}, f32[48,128]{1,0:T(8,128)S(1)}, u32[]{:S(2)}, u32[]{:S(2)}) %collective-permute-start.2) | collective-permute-done | bytes 24608 | tf_op jit(solution)/shard_map/ppermute | solution.py:613
  47.5 0.7 shard_map.92
  48.2 11.0 %all-to-all-start.2 = ((f32[8,48,128]{2,1,0:T(8,128)}), f32[8,48,128]{2,1,0:T(8,128)S(1)}, u32[]{:S(2)}, u32[]{:S(2)}) async-start(f32[8,48,128]{2,1,0:T(8,128)} %shard_map.92), calls=%async_computation.2 | async-start | bytes 393216 | tf_op jit(solution)/shard_map/all_to_all | solution.py:636
  59.2 4.2 %shard_map.93 = (bf16[8,240,128]{2,1,0:T(8,128)(2,1)S(1)}, bf16[512,512]{1,0:T(8,128)(2,1)S(1)}, bf16[256,256]{1,0:T(8,128)(2,1)S(1)}, bf16[256,256]{1,0:T(8,128)(2,1)S(1)}) custom-call(bf16[4,320,256]{2,1,0:T(8,128)(2,1)S(1)} %get-tuple-element.59.gp_ref, bf16[27,32,32]{2,1,0:T(8,128)(2,1)S(1)} %bitcast.21, ...), custom_call_target="tpu_custom_call" | custom-call | flops 5000000000 | tf_op jit(solution)/shard_map/pallas_call | solution.py:519
  63.4 0.0 all-to-all-done.2.r_ref
  63.5 0.1 collective-permute-start.3
  63.6 1.2 %collective-permute-done.3.other_ref = f32[48,128]{1,0:T(8,128)S(1)} collective-permute-done((f32[48,128]{1,0:T(8,128)S(1)}, f32[48,128]{1,0:T(8,128)S(1)}, u32[]{:S(2)}, u32[]{:S(2)}) %collective-permute-start.3) | collective-permute-done | bytes 24608 | tf_op jit(solution)/shard_map/ppermute | solution.py:644
  64.8 12.0 %all_to_all.21.r_ref = bf16[8,240,128]{2,1,0:T(8,128)(2,1)S(1)} all-to-all(bf16[8,240,128]{2,1,0:T(8,128)(2,1)S(1)} %get-tuple-element.61), channel_id=1, replica_groups={{128,160,0,32,192,224,64,96},{129,161,1,33,193,225,65,97},{130,162,2,34..., dimensions={0} | all-to-all | bytes 983040 | tf_op jit(solution)/shard_map/all_to_all | solution.py:654
  76.8 1.4 %shard_map.96 = (bf16[256,128]{1,0:T(8,128)(2,1)}, f32[27,8,32]{2,1,0:T(8,128)}, f32[27,32,32]{2,1,0:T(8,128)}, bf16[512,256]{1,0:T(8,128)(2,1)}) custom-call(bf16[8,240,128]{2,1,0:T(8,128)(2,1)S(1)} %all_to_all.21.r_ref, f32[56,128]{1,0:T(8,128)S(1)} %get-tuple-element.62.g_ref, bf16[512,512]{1,0:T(8,128)(2,1)S(1)} %get-tuple-element.63.fcol_ref, ...), custom_call_target="tpu_custom_call" | custom-call | flops 1000000000 | tf_op jit(solution)/shard_map/pallas_call | solution.py:519
  (5 shorter events, 0.1 us)
Async XLA Ops:
  0.6 7.6 %copy-start.2 = (bf16[32]{0:T(256)(128)(2,1)S(1)}, bf16[32]{0:T(256)(128)(2,1)}, u32[]{:S(2)}) copy-start(bf16[32]{0:T(256)(128)(2,1)} %param.7) | copy-start | bytes 196
  0.6 7.8 %copy-start = (bf16[64,32,3,3,3]{0,1,4,3,2:T(8,128)(2,1)S(1)}, bf16[64,32,3,3,3]{0,1,4,3,2:T(8,128)(2,1)}, u32[]{:S(2)}) copy-start(bf16[64,32,3,3,3]{0,1,4,3,2:T(8,128)(2,1)} %param.8) | copy-start | bytes 331780
  0.7 7.8 %copy-start.1 = (bf16[32,32,3,3,3]{1,0,4,3,2:T(8,128)(2,1)S(1)}, bf16[32,32,3,3,3]{1,0,4,3,2:T(8,128)(2,1)}, u32[]{:S(2)}) copy-start(bf16[32,32,3,3,3]{1,0,4,3,2:T(8,128)(2,1)} %param.6) | copy-start | bytes 165892
  3.2 14.5 %all-to-all-start = ((bf16[8,256,128]{2,1,0:T(8,128)(2,1)}), bf16[8,256,128]{2,1,0:T(8,128)(2,1)S(1)}, u32[]{:S(2)}, u32[]{:S(2)}) async-start(bf16[8,256,128]{2,1,0:T(8,128)(2,1)} %shard_map.84), calls=%async_computation | async-start | bytes 1048576 | tf_op jit(solution)/shard_map/all_to_all | solution.py:557
  17.7 4.7 %collective-permute-start = (bf16[8,64,128]{2,1,0:T(8,128)(2,1)S(1)}, bf16[8,64,128]{2,1,0:T(8,128)(2,1)S(1)}, u32[]{:S(2)}, u32[]{:S(2)}) collective-permute-start(bf16[8,64,128]{2,1,0:T(8,128)(2,1)S(1)} %get-tuple-element.47), channel_id=1, source_target_pairs={{0,1},{1,34},{2,3},{3,36},{4,5},{5,38},{6,7},{7,40},{8,9},{9,42},{... | collective-permute-start | bytes 393224 | tf_op jit(solution)/shard_map/ppermute | solution.py:576
  17.8 4.6 %collective-permute-start.1 = (bf16[8,64,128]{2,1,0:T(8,128)(2,1)S(1)}, bf16[8,64,128]{2,1,0:T(8,128)(2,1)S(1)}, u32[]{:S(2)}, u32[]{:S(2)}) collective-permute-start(bf16[8,64,128]{2,1,0:T(8,128)(2,1)S(1)} %get-tuple-element.48), channel_id=1, source_target_pairs={{1,0},{34,1},{3,2},{36,3},{5,4},{38,5},{7,6},{40,7},{9,8},{42,9},{... | collective-permute-start | bytes 393224 | tf_op jit(solution)/shard_map/ppermute | solution.py:577
  42.1 5.4 %collective-permute-start.2 = (f32[48,128]{1,0:T(8,128)S(1)}, f32[48,128]{1,0:T(8,128)S(1)}, u32[]{:S(2)}, u32[]{:S(2)}) collective-permute-start(f32[48,128]{1,0:T(8,128)S(1)} %shard_map.90.a_ref), channel_id=1, source_target_pairs={{0,2},{1,3},{2,0},{3,1},{4,6},{5,7},{6,4},{7,5},{8,10},{9,11},{10,... | collective-permute-start | bytes 73736 | tf_op jit(solution)/shard_map/ppermute | solution.py:613
  48.2 15.2 %all-to-all-start.2 = ((f32[8,48,128]{2,1,0:T(8,128)}), f32[8,48,128]{2,1,0:T(8,128)S(1)}, u32[]{:S(2)}, u32[]{:S(2)}) async-start(f32[8,48,128]{2,1,0:T(8,128)} %shard_map.92), calls=%async_computation.2 | async-start | bytes 393216 | tf_op jit(solution)/shard_map/all_to_all | solution.py:636
  63.5 1.3 %collective-permute-start.3 = (f32[48,128]{1,0:T(8,128)S(1)}, f32[48,128]{1,0:T(8,128)S(1)}, u32[]{:S(2)}, u32[]{:S(2)}) collective-permute-start(f32[48,128]{1,0:T(8,128)S(1)} %shard_map.94.mine_ref), channel_id=1, source_target_pairs={{0,1},{1,0},{2,3},{3,2},{4,5},{5,4},{6,7},{7,6},{8,9},{9,8},{10,11... | collective-permute-start | bytes 73736 | tf_op jit(solution)/shard_map/ppermute | solution.py:644
